TPU v7x, 32 devices: a whole 2x2x4 slice. The times are simulated.
32 devices in a mesh: strip: 8 (over z, y), bucket: 4 (over x, core).
Axes of the slice: x: 2, y: 2, z: 4, core: 2. Of those that a mesh axis runs over, the one named last changes fastest.
Arguments:
- block_input: float32 [32, 56, 56, 384], P('bucket', 'strip'), may hold values from -6 to 6
- cotangent: float32 [32, 56, 56, 384], P('bucket', 'strip'), may hold values from -6 to 6
- window_cols: int32 [4], P('bucket'), may hold values from 1 to 8, as said below
- keep_mask: int32 [32, 2], P('bucket'), may hold values 0 or 1
- owner_list: int32 [13879], replicated, may hold values from 0 to 31, as said below
- master: float32 [20832, 128], P(('strip', 'bucket')), as said below
- first_moment: float32 [20832, 128], P(('strip', 'bucket')), as said below
- second_moment: float32 [20832, 128], P(('strip', 'bucket')), as said below
Outputs:
- block_output: float32 [32, 56, 56, 384], P('bucket', 'strip')
- grad_input: float32 [32, 56, 56, 384], P('bucket', 'strip')
- new_first: float32 [20832, 128], P(('strip', 'bucket'))
- new_second: float32 [20832, 128], P(('strip', 'bucket'))
- new_master: float32 [20832, 128], P(('strip', 'bucket'))
Inputs may be any that keep to these rules, and one draw needn't show every extreme that they name: `window_cols`: some bucket is 8 windows wide. `owner_list`: the owner of each packed row, as an index in strip-then-bucket order. No device owns more than 651 rows and some device owns exactly 651. `master`: slot d * 651 + t holds the packed row of device d's t-th owned row in increasing row order; unused slots hold zeros. `first_moment`: same slot layout as master; unused slots are zero. `second_moment`: same slot layout as master; positive in used slots, zero in unused ones.
All inputs are finite; a program needn't handle non-finite values. No bound on the sum of `keep_mask` on one device may be relied on, other than what follows from the above.
Results may differ from a plain program's by a relative error of at most 0.011.
Values may be sent and summed in bfloat16 or wider, within the bound.
A program may use at most 256 MiB of HBM per device.

v0:
```python
import math

import jax
import jax.numpy as jnp
from jax import lax
from jax.sharding import PartitionSpec as P

C = 384
HEADS = 12
HD = 32
FF = 1536
WIN = 7
SHIFT = 3
STEP = 10
SMALL_ROWS = 39
TABLE_ROWS = 16


PRECISE = lax.Precision.HIGHEST
NORM_EPS = 1e-05
KEEP_PROB = 0.8
MASK_FILL = -100.0
BETA_ONE = 0.5
BETA_TWO = 0.5
ADAM_EPS = 1e-08
DECAY = 0.05


def from_behind(value, axis, by):
    peers = lax.axis_size(axis)
    return lax.ppermute(value, axis, [(i, (i + by) % peers) for i in range(peers)])


def row_edges():
    first = 3 * C * C // 128
    second = first + C * C // 128
    third = second + C * FF // 128
    fourth = third + FF * C // 128
    fifth = fourth + SMALL_ROWS
    return [first, second, third, fourth, fifth]


def row_kind(row_ids):
    kind = jnp.zeros(row_ids.shape, jnp.int32)
    for boundary in row_edges():
        kind = kind + (row_ids >= boundary).astype(jnp.int32)
    return jnp.where(row_ids < 0, 6, kind)


def row_rates(row_ids):
    kind = row_kind(row_ids)
    rates = [
        2.0 / math.sqrt(C),
        2.0 / math.sqrt(C // 8),
        2.0 / math.sqrt(C),
        2.0 / math.sqrt(FF),
        1.0,
        1.0,
        0.0,
    ]
    decays = [DECAY, DECAY, DECAY, DECAY, 0.0, 0.0, 0.0]
    rate_rows = jnp.zeros(row_ids.shape, jnp.float32)
    decay_rows = jnp.zeros(row_ids.shape, jnp.float32)
    for index, amount in enumerate(rates):
        rate_rows = rate_rows + jnp.where(kind == index, amount, 0.0).astype(jnp.float32)
        decay_rows = decay_rows + jnp.where(kind == index, decays[index], 0.0).astype(jnp.float32)
    return (rate_rows, decay_rows)


def slot_rows(owner_list, device_count, capacity):
    hits = (owner_list[:, None] == jnp.arange(device_count, dtype=jnp.int32)[None, :]).astype(
        jnp.int32
    )
    rank = jnp.sum(jnp.cumsum(hits, axis=0) * hits, axis=1) - 1
    return owner_list * capacity + rank


def slot_owner_rows(slots, slot_total):
    return (
        jnp.full((slot_total,), -1, jnp.int32)
        .at[slots]
        .set(jnp.arange(slots.shape[0], dtype=jnp.int32))
    )


def unpack(packed):
    flat = packed.reshape(-1)
    lengths = [C * 3 * C, C * C, C * FF, FF * C, 3 * C, C, FF, C, C, C, C, C]
    pieces = []
    start = 0
    for length in lengths:
        pieces.append(flat[start : start + length])
        start = start + length
    table_start = row_edges()[4] * 128
    table = flat[table_start : table_start + (2 * WIN - 1) ** 2 * HEADS].reshape(
        (2 * WIN - 1) ** 2, HEADS
    )
    matrices = (
        pieces[0].reshape(C, 3 * C),
        pieces[1].reshape(C, C),
        pieces[2].reshape(C, FF),
        pieces[3].reshape(FF, C),
    )
    return (matrices, pieces[4:12], table)


def pack(matrices, smalls, table):
    parts = [piece.reshape(-1) for piece in matrices] + [piece for piece in smalls]
    small_pad = SMALL_ROWS * 128 - (9 * C + FF)
    table_pad = TABLE_ROWS * 128 - (2 * WIN - 1) ** 2 * HEADS
    parts = parts + [
        jnp.zeros((small_pad,), jnp.float32),
        table.reshape(-1),
        jnp.zeros((table_pad,), jnp.float32),
    ]
    return jnp.concatenate(parts).reshape(-1, 128)


def column_map(image_width, offset, columns):
    column_ids = jnp.arange(columns, dtype=jnp.int32)
    return jnp.where(column_ids < image_width, (column_ids + offset) % image_width, column_ids)


def relative_onehot():
    position = jnp.arange(WIN * WIN, dtype=jnp.int32)
    row_pos = position // WIN
    col_pos = position % WIN
    index = (
        (row_pos[:, None] - row_pos[None, :] + WIN - 1) * (2 * WIN - 1)
        + col_pos[:, None]
        - col_pos[None, :]
        + WIN
        - 1
    ).reshape(-1)
    return (index[:, None] == jnp.arange((2 * WIN - 1) ** 2, dtype=jnp.int32)[None, :]).astype(
        jnp.float32
    )


def shift_labels(global_rows, image_width, height, columns):
    row_part = (global_rows >= height - WIN).astype(jnp.int32) + (
        global_rows >= height - SHIFT
    ).astype(jnp.int32)
    column_ids = jnp.arange(columns, dtype=jnp.int32)
    col_part = (
        (column_ids >= image_width - WIN).astype(jnp.int32)
        + (column_ids >= image_width - SHIFT).astype(jnp.int32)
        + (column_ids >= image_width).astype(jnp.int32)
    )
    return row_part[:, None] * 4 + col_part[None, :]


def layer_norm(values, gain, offset):
    center = values - jnp.mean(values, axis=-1, keepdims=True)
    spread = jnp.mean(center * center, axis=-1, keepdims=True)
    return center * lax.rsqrt(spread + NORM_EPS) * gain + offset


def gelu_exact(values):
    return jax.nn.gelu(values, approximate=False)


def window_source(samples, row_count, columns, col_map):
    wide = columns // WIN
    win_row = jnp.arange(row_count // WIN, dtype=jnp.int32).reshape(-1, 1, 1, 1)
    win_col = jnp.arange(wide, dtype=jnp.int32).reshape(1, -1, 1, 1)
    inner_row = jnp.arange(WIN, dtype=jnp.int32).reshape(1, 1, -1, 1)
    inner_col = jnp.arange(WIN, dtype=jnp.int32).reshape(1, 1, 1, -1)
    source_row = win_row * WIN + inner_row + SHIFT
    source_col = col_map[win_col * WIN + inner_col]
    sample = jnp.arange(samples, dtype=jnp.int32).reshape(-1, 1, 1, 1, 1)
    local = sample * (row_count * columns) + source_row * columns + source_col
    outside = (
        samples * row_count * columns
        + sample * (SHIFT * columns)
        + (source_row - row_count) * columns
        + source_col
    )
    return jnp.where(source_row < row_count, local, outside).reshape(-1)


def window_cell(row_ids, col_ids, columns):
    wide = columns // WIN
    return (
        (row_ids // WIN * wide + col_ids // WIN) * (WIN * WIN) + row_ids % WIN * WIN + col_ids % WIN
    )


def home_source(samples, row_count, columns, col_map):
    row_ids = jnp.arange(row_count, dtype=jnp.int32).reshape(-1, 1)
    source_col = col_map.reshape(1, -1)
    earlier = row_ids - SHIFT
    inside = window_cell(jnp.maximum(earlier, 0), source_col, columns)
    sample = jnp.arange(samples, dtype=jnp.int32).reshape(-1, 1, 1)
    local = sample * (row_count * columns) + inside
    outside = (
        samples * row_count * columns + sample * (SHIFT * columns) + row_ids * columns + source_col
    )
    return jnp.where(earlier >= 0, local, outside).reshape(-1)


def tail_source(samples, row_count, columns):
    row_ids = row_count - SHIFT + jnp.arange(SHIFT, dtype=jnp.int32).reshape(-1, 1)
    col_ids = jnp.arange(columns, dtype=jnp.int32).reshape(1, -1)
    sample = jnp.arange(samples, dtype=jnp.int32).reshape(-1, 1, 1)
    return (sample * (row_count * columns) + window_cell(row_ids, col_ids, columns)).reshape(-1)


def adamw(weights, first, second, grads, row_ids):
    rate_rows, decay_rows = row_rates(row_ids)
    first = BETA_ONE * first + (1.0 - BETA_ONE) * grads
    second = BETA_TWO * second + (1.0 - BETA_TWO) * grads * grads
    first_hat = first / (1.0 - BETA_ONE**STEP)
    second_hat = second / (1.0 - BETA_TWO**STEP)
    weights = weights - rate_rows[:, None] * (
        first_hat / (jnp.sqrt(second_hat) + ADAM_EPS) + decay_rows[:, None] * weights
    )
    return (first, second, weights)


def shards(
    block_input, cotangent, window_cols, keep_mask, owner_list, master, first_moment, second_moment
):
    strips = lax.axis_size("strip")
    device_count = strips * lax.axis_size("bucket")
    capacity = master.shape[0]
    slots = slot_rows(owner_list, device_count, capacity)
    sources = slot_owner_rows(slots, device_count * capacity)
    gathered = lax.all_gather(master, ("strip", "bucket"), axis=0, tiled=True)
    matrices, smalls, table = unpack(gathered[slots])
    triple_weight, proj_weight, up_weight, down_weight = matrices
    triple_bias, proj_bias, up_bias, down_bias, gain_one, shift_one, gain_two, shift_two = smalls
    triple_low = triple_weight.astype(jnp.bfloat16)
    proj_low = proj_weight.astype(jnp.bfloat16)
    up_low = up_weight.astype(jnp.bfloat16)
    down_low = down_weight.astype(jnp.bfloat16)
    samples, row_count, columns, channels = block_input.shape
    image_width = window_cols[0] * WIN
    height = row_count * strips
    keep_scale = keep_mask.astype(jnp.float32) / KEEP_PROB
    keep_one = keep_scale[:, 0].reshape(samples, 1, 1, 1)
    keep_two = keep_scale[:, 1].reshape(samples, 1, 1, 1)
    column_ids = jnp.arange(columns, dtype=jnp.int32)
    valid = (column_ids < image_width).astype(jnp.float32).reshape(1, 1, columns, 1)
    forward_cols = column_map(image_width, SHIFT, columns)
    backward_cols = column_map(image_width, -SHIFT, columns)
    to_windows = window_source(samples, row_count, columns, forward_cols)
    to_home = home_source(samples, row_count, columns, backward_cols)
    tail_rows = tail_source(samples, row_count, columns)
    score_scale = HD ** (-0.5)
    onehot_rel = relative_onehot()
    rel_bias = (
        jnp.dot(onehot_rel, table, precision=PRECISE)
        .reshape(WIN * WIN, WIN * WIN, HEADS)
        .transpose(2, 0, 1)
    )
    global_rows = lax.axis_index("strip") * row_count + jnp.arange(row_count, dtype=jnp.int32)
    labels = shift_labels(global_rows, image_width, height, columns)
    label_windows = (
        labels.reshape(row_count // WIN, WIN, columns // WIN, WIN)
        .transpose(0, 2, 1, 3)
        .reshape(-1, WIN * WIN)
    )
    masking = jnp.where(
        label_windows[:, :, None] != label_windows[:, None, :], MASK_FILL, 0.0
    ).astype(jnp.float32)
    masking = jnp.tile(masking, (samples, 1, 1))
    normed, norm_one_pull = jax.vjp(layer_norm, block_input, gain_one, shift_one)
    normed_low = normed.astype(jnp.bfloat16)
    incoming = from_behind(normed_low[:, :SHIFT], "strip", -1)
    extended = jnp.concatenate(
        [normed_low.reshape(-1, channels), incoming.reshape(-1, channels)], axis=0
    )
    flat_windows = jnp.take(extended, to_windows, axis=0)
    window_count = flat_windows.shape[0] // (WIN * WIN)
    triple = (
        jnp.dot(flat_windows, triple_low, preferred_element_type=jnp.float32) + triple_bias
    ).astype(jnp.bfloat16)
    triple = triple.reshape(window_count, WIN * WIN, 3, HEADS, HD)
    query = triple[:, :, 0]
    keys = triple[:, :, 1]
    values = triple[:, :, 2]

    def scores_of():
        raw = jnp.einsum("wqhd,wkhd->whqk", query, keys, preferred_element_type=jnp.float32)
        return raw * score_scale + rel_bias[None] + masking[:, None]

    scores = scores_of()
    row_peak = jnp.max(scores, axis=-1, keepdims=True)
    exponent = jnp.exp(scores - row_peak)
    row_total = jnp.sum(exponent, axis=-1, keepdims=True)
    attention_low = (exponent / row_total).astype(jnp.bfloat16)
    log_total = row_peak + jnp.log(row_total)
    context = jnp.einsum(
        "whqk,wkhd->wqhd", attention_low, values, preferred_element_type=jnp.float32
    ).astype(jnp.bfloat16)
    context = context.reshape(-1, channels)
    outgoing = jnp.take(context, tail_rows, axis=0).reshape(samples, SHIFT, columns, channels)
    incoming = from_behind(outgoing, "strip", 1)
    extended = jnp.concatenate([context, incoming.reshape(-1, channels)], axis=0)
    flat_context = jnp.take(extended, to_home, axis=0)
    branch = (
        jnp.dot(flat_context, proj_low, preferred_element_type=jnp.float32) + proj_bias
    ).reshape(block_input.shape)
    mixed = block_input + keep_one * branch
    second, norm_two_pull = jax.vjp(layer_norm, mixed, gain_two, shift_two)
    second_low = second.astype(jnp.bfloat16).reshape(-1, channels)
    hidden = jnp.dot(second_low, up_low, preferred_element_type=jnp.float32) + up_bias
    active, gelu_pull = jax.vjp(gelu_exact, hidden)
    active_low = active.astype(jnp.bfloat16)
    branch_two = (
        jnp.dot(active_low, down_low, preferred_element_type=jnp.float32) + down_bias
    ).reshape(block_input.shape)
    output = (mixed + keep_two * branch_two) * valid
    grad_result = cotangent * valid
    grad_two = (keep_two * grad_result).astype(jnp.bfloat16).reshape(-1, channels)
    grad_down = jnp.einsum("tf,tc->fc", active_low, grad_two, preferred_element_type=jnp.float32)
    grad_down_bias = jnp.sum(grad_two, axis=0, dtype=jnp.float32)
    grad_active = jnp.einsum("tc,fc->tf", grad_two, down_low, preferred_element_type=jnp.float32)
    grad_hidden = gelu_pull(grad_active)[0].astype(jnp.bfloat16)
    grad_up = jnp.einsum("tc,tf->cf", second_low, grad_hidden, preferred_element_type=jnp.float32)
    grad_up_bias = jnp.sum(grad_hidden, axis=0, dtype=jnp.float32)
    grad_second = jnp.einsum(
        "tf,cf->tc", grad_hidden, up_low, preferred_element_type=jnp.float32
    ).reshape(block_input.shape)
    grad_mixed_norm, grad_gain_two, grad_shift_two = norm_two_pull(grad_second)
    grad_mixed = grad_result + grad_mixed_norm
    grad_branch = (keep_one * grad_mixed).astype(jnp.bfloat16).reshape(-1, channels)
    grad_proj = jnp.einsum(
        "tc,te->ce", flat_context, grad_branch, preferred_element_type=jnp.float32
    )
    grad_proj_bias = jnp.sum(grad_branch, axis=0, dtype=jnp.float32)
    grad_context = jnp.einsum(
        "te,ce->tc", grad_branch, proj_low, preferred_element_type=jnp.float32
    ).astype(jnp.bfloat16)
    grad_context = grad_context.reshape(block_input.shape)
    incoming = from_behind(grad_context[:, :SHIFT], "strip", -1)
    extended = jnp.concatenate(
        [grad_context.reshape(-1, channels), incoming.reshape(-1, channels)], axis=0
    )
    grad_context_windows = jnp.take(extended, to_windows, axis=0).reshape(
        window_count, WIN * WIN, HEADS, HD
    )
    attention_again = jnp.exp(scores_of() - log_total)
    grad_attention = jnp.einsum(
        "wqhd,wkhd->whqk", grad_context_windows, values, preferred_element_type=jnp.float32
    )
    grad_values = jnp.einsum(
        "whqk,wqhd->wkhd",
        attention_again.astype(jnp.bfloat16),
        grad_context_windows,
        preferred_element_type=jnp.float32,
    )
    inner = jnp.sum(grad_attention * attention_again, axis=-1, keepdims=True)
    grad_scores = (attention_again * (grad_attention - inner)).astype(jnp.bfloat16)
    grad_query = (
        jnp.einsum("whqk,wkhd->wqhd", grad_scores, keys, preferred_element_type=jnp.float32)
        * score_scale
    )
    grad_keys = (
        jnp.einsum("whqk,wqhd->wkhd", grad_scores, query, preferred_element_type=jnp.float32)
        * score_scale
    )
    grad_rel = (
        jnp.sum(grad_scores, axis=0, dtype=jnp.float32)
        .transpose(1, 2, 0)
        .reshape(WIN * WIN * WIN * WIN, HEADS)
    )
    grad_table = jnp.dot(onehot_rel.T, grad_rel, precision=PRECISE)
    grad_triple = (
        jnp.stack([grad_query, grad_keys, grad_values], axis=2)
        .astype(jnp.bfloat16)
        .reshape(-1, 3 * channels)
    )
    grad_triple_weight = jnp.einsum(
        "tc,tf->cf", flat_windows, grad_triple, preferred_element_type=jnp.float32
    )
    grad_triple_bias = jnp.sum(grad_triple, axis=0, dtype=jnp.float32)
    grad_moved = jnp.einsum(
        "tf,cf->tc", grad_triple, triple_low, preferred_element_type=jnp.float32
    ).astype(jnp.bfloat16)
    outgoing = jnp.take(grad_moved, tail_rows, axis=0).reshape(samples, SHIFT, columns, channels)
    incoming = from_behind(outgoing, "strip", 1)
    extended = jnp.concatenate([grad_moved, incoming.reshape(-1, channels)], axis=0)
    grad_normed = jnp.take(extended, to_home, axis=0).reshape(block_input.shape).astype(jnp.float32)
    grad_input_norm, grad_gain_one, grad_shift_one = norm_one_pull(grad_normed)
    grad_input = grad_mixed + grad_input_norm
    packed_grad = pack(
        [grad_triple_weight, grad_proj, grad_up, grad_down],
        [
            grad_triple_bias,
            grad_proj_bias,
            grad_up_bias,
            grad_down_bias,
            grad_gain_one,
            grad_shift_one,
            grad_gain_two,
            grad_shift_two,
        ],
        grad_table,
    )
    my_index = lax.axis_index(("strip", "bucket"))
    my_sources = lax.dynamic_slice_in_dim(sources, my_index * capacity, capacity)
    spread_out = jnp.where((sources >= 0)[:, None], packed_grad[jnp.maximum(sources, 0)], 0.0)
    grads = lax.psum_scatter(spread_out, ("strip", "bucket"), scatter_dimension=0, tiled=True)
    first, second_new, weights = adamw(master, first_moment, second_moment, grads, my_sources)
    return (output, grad_input, first, second_new, weights)


def solution(mesh):
    in_specs = (
        P("bucket", "strip", None, None),
        P("bucket", "strip", None, None),
        P("bucket"),
        P("bucket", None),
        P(),
        P(("strip", "bucket"), None),
        P(("strip", "bucket"), None),
        P(("strip", "bucket"), None),
    )
    out_specs = (
        P("bucket", "strip", None, None),
        P("bucket", "strip", None, None),
        P(("strip", "bucket"), None),
        P(("strip", "bucket"), None),
        P(("strip", "bucket"), None),
    )
    return jax.shard_map(shards, mesh=mesh, in_specs=in_specs, out_specs=out_specs, check_vma=False)
```

profile of v0, /device:TPU:0, one launch (start us, length us, event | category | flops | bytes accessed | tf_op | source)
XLA Modules:
  0.0 1065.1 jit_solution(15057214990035258733)
XLA Ops:
  13.9 18.4 %reduce-window.6 = s32[32,109,128]{2,1,0:T(8,128)S(1)} reduce-window(s32[32,109,128]{2,1,0:T(8,128)} %reshape.959, s32[]{:T(128)} %constant.98.clone.1), window={size=1x1x128 pad=0_0x0_0x127_0}, to_apply=%region_2.3 | reduce-window | flops 56700928 | bytes 3571716 | tf_op jit(solution)/shard_map/reduce-window
  38.1 65.2 %scatter_custom_fusion = s32[20832]{0:T(1024)S(1)} fusion(s32[13879]{0:T(1024)S(1)} %compare_select_fusion.1, s32[13879]{0:T(1024)S(1)} %iota.196, s32[]{:T(128)} %constant.99.clone.1), kind=kCustom, calls=%fused_computation.130 | custom fusion | bytes 83332 | tf_op jit(solution)/shard_map/scatter | solution.py:82
  117.7 30.6 %gather_fusion = f32[13879,128]{1,0:T(8,128)} fusion(f32[20832,128]{1,0:T(8,128)} %reshape.1057, s32[14336]{0:T(1024)S(1)} %pad_clamp_fusion.1), kind=kCustom, calls=%fused_computation.6 | custom fusion | bytes 14267612 | tf_op jit(solution)/shard_map/gather | solution.py:230
  170.7 11.7 %collective-permute-done = bf16[8,3,56,384]{3,2,1,0:T(8,128)(2,1)} collective-permute-done((bf16[8,3,56,384]{3,2,1,0:T(8,128)(2,1)}, bf16[8,3,56,384]{3,2,1,0:T(8,128)(2,1)}, u32[]{:S(2)}, u32[]{:S(2)}) %collective-permute-start) | collective-permute-done | bytes 1032224 | tf_op jit(solution)/shard_map/ppermute | solution.py:31
  184.8 10.0 gather_fusion.3
  203.4 11.4 %copy.59 = bf16[3136,1152]{0,1:T(8,128)(2,1)} copy(bf16[3136,1152]{1,0:T(8,128)(2,1)} %fusion.9) | data formatting | bytes 14450688 | tf_op jit(solution)/shard_map/convert_element_type | solution.py:278
  214.8 56.7 %reshape.936 = bf16[64,49,3,12,32]{1,0,4,3,2:T(8,128)(2,1)} reshape(bf16[3136,1152]{0,1:T(8,128)(2,1)} %copy.59) | data formatting | bytes 14450688 | tf_op jit(solution)/shard_map/reshape | solution.py:279
  271.5 14.4 %fusion.73 = (bf16[64,49,1,12,32]{1,0,4,3,2:T(8,128)(2,1)}, bf16[64,49,1,12,32]{1,0,4,3,2:T(8,128)(2,1)}, bf16[64,49,1,12,32]{1,0,4,3,2:T(8,128)(2,1)}) fusion(bf16[64,49,3,12,32]{1,0,4,3,2:T(8,128)(2,1)} %reshape.936), kind=kLoop, calls=%fused_computation.234 | loop fusion | bytes 14450688 | tf_op jit(solution)/shard_map/slice | solution.py:282
  286.1 22.3 %fusion.75 = (f32[64,12,49]{2,1,0:T(8,128)S(1)}, f32[64,12,49,49]{2,3,1,0:T(8,128)}) fusion(f32[64,49,49]{1,2,0:T(8,128)S(1)} %bitcast.162, f32[12,49,49]{1,2,0:T(8,128)S(1)} %copy-done.11, bf16[64,49,1,12,32]{1,0,4,3,2:T(8,128)(2,1)} %get-tuple-element.33, bf16[64,49,1,12,32]{1,0,4,3,2:T(8,128)(2,1)} %get-tuple-element.32), kind=kOutput, calls=%fused_computation.236 | convolution fusion | flops 125352192 | bytes 13073200 | tf_op jit(solution)/shard_map/wqhd,wkhd->whqk/dot_general | solution.py:285
  308.3 10.0 fusion.1
  318.4 15.3 %convert_bitcast_fusion = bf16[64,49,12,32]{1,3,2,0:T(8,128)(2,1)} fusion(f32[64,12,49,49]{2,3,1,0:T(8,128)} %get-tuple-element.50, f32[64,12,49]{2,1,0:T(8,128)S(1)} %fusion.1, f32[64,12,49]{2,1,0:T(8,128)S(1)} %get-tuple-element.49, bf16[64,49,1,12,32]{1,0,4,3,2:T(8,128)(2,1)} %get-tuple-element.31), kind=kOutput, calls=%fused_computation.51 | convolution fusion | flops 124750080 | bytes 12493824 | tf_op jit(solution)/shard_map/whqk,wkhd->wqhd/dot_general | solution.py:294
  343.0 10.5 reshape.939
  380.2 13.3 %collective-permute-done.1 = bf16[8,3,56,384]{3,2,1,0:T(8,128)(2,1)} collective-permute-done((bf16[8,3,56,384]{3,2,1,0:T(8,128)(2,1)}, bf16[8,3,56,384]{3,2,1,0:T(8,128)(2,1)}, u32[]{:S(2)}, u32[]{:S(2)}) %collective-permute-start.1) | collective-permute-done | bytes 1032224 | tf_op jit(solution)/shard_map/ppermute | solution.py:31
  395.9 10.0 gather_fusion.5
  421.7 48.1 %multiply_convert_fusion.1 = (bf16[3136,1536]{1,0:T(8,128)(2,1)S(1)}, f32[3136,1536]{1,0:T(8,128)}, f32[3136,1536]{1,0:T(8,128)}) fusion(f32[1536]{0:T(1024)S(1)} %slice_bitcast_fusion, bf16[3136,384]{1,0:T(8,128)(2,1)S(1)} %bitcast.164, bf16[384,1536]{1,0:T(8,128)(2,1)S(1)} %copy-done.18), kind=kOutput, calls=%fused_computation.25 | convolution fusion | flops 4017291264 | bytes 51763200 | tf_op jit(solution)/shard_map/dot_general | solution.py:308
  483.9 21.8 %convert_reduce_fusion.2 = (f32[1536]{0:T(1024)}, bf16[3136,1536]{1,0:T(8,128)(2,1)}) fusion(f32[3136,1536]{1,0:T(8,128)} %get-tuple-element.26, bf16[3136,384]{1,0:T(8,128)(2,1)S(1)} %bitcast.167, bf16[1536,384]{1,0:T(8,128)(2,1)} %convert_element_type.192, f32[3136,1536]{1,0:T(8,128)} %get-tuple-element.51, f32[1536]{0:T(1024)S(1)} %slice_bitcast_fusion), kind=kOutput, calls=%fused_computation.23 | convolution fusion | flops 3781261824 | bytes 51769344 | tf_op jit(solution)/shard_map/tc,fc->tf/dot_general | solution.py:319
  553.4 10.2 gather_fusion.6
  570.8 19.1 %reshape.949 = bf16[64,49,12,32]{1,0,3,2:T(8,128)(2,1)} reshape(bf16[3136,384]{0,1:T(8,128)(2,1)S(1)} %copy.69) | data formatting | bytes 4816896 | tf_op jit(solution)/shard_map/reshape | solution.py:341
  589.9 14.8 %fusion.19 = bf16[64,49,1,12,32]{1,4,3,0,2:T(8,128)(2,1)} fusion(f32[64,12,49,49]{2,3,1,0:T(8,128)} %get-tuple-element.50, f32[64,12,49]{2,1,0:T(8,128)S(1)} %copy-done.8, bf16[64,49,12,32]{1,0,3,2:T(8,128)(2,1)} %reshape.949), kind=kOutput, calls=%fused_computation.78 | convolution fusion | flops 121701888 | bytes 12343296 | tf_op jit(solution)/shard_map/whqk,wqhd->wkhd/dot_general | solution.py:348
  604.7 30.0 %multiply_reduce_fusion = (f32[64,12,49]{2,1,0:T(8,128)}, f32[64,12,49,49]{2,3,1,0:T(8,128)}) fusion(f32[64,12,49,49]{2,3,1,0:T(8,128)} %get-tuple-element.50, f32[64,12,49]{2,1,0:T(8,128)} %log_add_fusion, bf16[64,49,1,12,32]{1,0,4,3,2:T(8,128)(2,1)} %get-tuple-element.31, bf16[64,49,12,32]{1,0,3,2:T(8,128)(2,1)} %reshape.949), kind=kOutput, calls=%fused_computation.15 | convolution fusion | flops 123508224 | bytes 19869696 | tf_op jit(solution)/shard_map/wqhd,wkhd->whqk/dot_general | solution.py:345
  634.7 19.7 %convert_reduce_fusion.1 = (f32[12,49,49]{1,2,0:T(8,128)S(1)}, bf16[64,12,49,49]{2,3,1,0:T(8,128)(2,1)}) fusion(f32[64,12,49,49]{2,3,1,0:T(8,128)} %get-tuple-element.54, f32[64,12,49]{2,1,0:T(8,128)} %get-tuple-element.53, f32[64,12,49,49]{2,3,1,0:T(8,128)} %get-tuple-element.50, f32[64,12,49]{2,1,0:T(8,128)} %log_add_fusion), kind=kLoop, calls=%fused_computation.13 | loop fusion | flops 11034996 | bytes 18855984 | tf_op jit(solution)/shard_map/reduce_sum | solution.py:365
  654.4 18.7 %multiply_bitcast_fusion = bf16[64,49,1,12,32]{1,4,3,0,2:T(8,128)(2,1)} fusion(bf16[64,12,49,49]{2,3,1,0:T(8,128)(2,1)} %get-tuple-element.17, bf16[64,49,1,12,32]{1,0,4,3,2:T(8,128)(2,1)S(1)} %bitcast.147), kind=kOutput, calls=%fused_computation.41 | convolution fusion | flops 120422400 | bytes 8504832 | tf_op jit(solution)/shard_map/whqk,wqhd->wkhd/dot_general | solution.py:361
  673.1 22.7 %multiply_bitcast_fusion.1 = bf16[64,49,1,12,32]{1,4,3,0,2:T(8,128)(2,1)} fusion(bf16[64,12,49,49]{2,3,1,0:T(8,128)(2,1)} %get-tuple-element.17, bf16[64,49,1,12,32]{1,0,4,3,2:T(8,128)(2,1)} %get-tuple-element.33), kind=kOutput, calls=%fused_computation.42 | convolution fusion | flops 120422400 | bytes 8504832 | tf_op jit(solution)/shard_map/whqk,wkhd->wqhd/dot_general | solution.py:357
  696.8 13.8 %convert_reduce_fusion = (f32[3,12,32]{2,1,0:T(8,128)S(1)}, bf16[64,49,3,12,32]{1,4,3,0,2:T(8,128)(2,1)S(1)}) fusion(bf16[64,49,1,12,32]{1,4,3,0,2:T(8,128)(2,1)} %fusion.19, bf16[64,49,1,12,32]{1,4,3,0,2:T(8,128)(2,1)} %multiply_bitcast_fusion, bf16[64,49,1,12,32]{1,4,3,0,2:T(8,128)(2,1)} %multiply_bitcast_fusion.1), kind=kLoop, calls=%fused_computation.11 | loop fusion | flops 14449536 | bytes 14455296 | tf_op jit(solution)/shard_map/reduce_sum | solution.py:378
  710.6 13.3 %copy.75 = bf16[64,49,3,12,32]{1,0,4,3,2:T(8,128)(2,1)} copy(bf16[64,49,3,12,32]{1,4,3,0,2:T(8,128)(2,1)S(1)} %get-tuple-element.24) | data formatting | bytes 14450688 | tf_op jit(solution)/shard_map/convert_element_type | solution.py:372
  723.9 28.5 %convert_element_type.201 = bf16[3136,1152]{0,1:T(8,128)(2,1)} reshape(bf16[64,49,3,12,32]{1,0,4,3,2:T(8,128)(2,1)} %copy.75) | data formatting | bytes 14450688 | tf_op jit(solution)/shard_map/convert_element_type | solution.py:372
  778.7 12.6 %collective-permute-done.3 = bf16[8,3,56,384]{3,2,1,0:T(8,128)(2,1)S(1)} collective-permute-done((bf16[8,3,56,384]{3,2,1,0:T(8,128)(2,1)}, bf16[8,3,56,384]{3,2,1,0:T(8,128)(2,1)S(1)}, u32[]{:S(2)}, u32[]{:S(2)}) %collective-permute-start.3) | collective-permute-done | bytes 1032224 | tf_op jit(solution)/shard_map/ppermute | solution.py:31
  794.6 10.0 gather_fusion.8
  818.4 53.6 %concatenate.19 = f32[1776512]{0:T(1024)} concatenate(f32[442368]{0:T(1024)} %reshape.952, f32[147456]{0:T(1024)S(1)} %copy-done.12, f32[589824]{0:T(1024)S(1)} %copy-done.9, f32[589824]{0:T(1024)} %reshape.955, f32[1152]{0:T(1024)S(1)} %reduce_sum.226, f32[384]{0:T(512)S(1)} %copy-done.59, f32[1536]{0:T(1024)S(1)} %copy-done.56, f32[384]{0:T(512)S(1)} %copy-done.57, ...), dimensions={0} | concatenate | bytes 14212096 | tf_op jit(solution)/shard_map/concatenate | solution.py:116
  872.0 42.2 %gather_fusion.2 = f32[20832,128]{1,0:T(8,128)} fusion(f32[13879,128]{1,0:T(8,128)} %bitcast.143, s32[21504]{0:T(1024)S(1)} %copy-done.29), kind=kCustom, calls=%fused_computation.8 | custom fusion | bytes 21415296 | tf_op jit(solution)/shard_map/gather | solution.py:404
  914.2 12.8 %broadcast_select_fusion = f32[20832,128]{1,0:T(8,128)} fusion(f32[20832,128]{1,0:T(8,128)} %gather_fusion.2, pred[20832]{0:T(1024)(128)(4,1)S(1)} %copy-done.39), kind=kLoop, calls=%fused_computation.61 | loop fusion | flops 2666496 | bytes 21352800 | tf_op jit(solution)/shard_map/jit(_where)/select_n | solution.py:404
  927.0 116.6 %fusion = f32[656,128]{1,0:T(8,128)S(1)} fusion(f32[20832,128]{1,0:T(8,128)} %broadcast_select_fusion), kind=kCustom, calls=%all-reduce-scatter | all-reduce-scatter fusion | flops 2686977 | bytes 11001856
  (319 shorter events, 240.0 us)
Async XLA Ops:
  7.2 102.2 %all-gather.3.cloned.1.call-start = ((), (), s32[]{:S(2)}) async-start(), calls=%async_computation | async-start | bytes 11083776 | tf_op jit(solution)/shard_map/all_gather | solution.py:229
  34.3 69.9 %copy-start.68 = (s32[8,2]{0,1:T(2,128)S(1)}, s32[8,2]{0,1:T(2,128)}, u32[]{:S(2)}) copy-start(s32[8,2]{0,1:T(2,128)} %param.15) | copy-start | bytes 196
  103.4 308.1 %copy-start.65 = (f32[56]{0:T(128)}, f32[56]{0:T(128)S(1)}, u32[]{:S(2)}) copy-start(f32[56]{0:T(128)S(1)} %fusion.58) | copy-start | bytes 676
  103.4 254.9 %copy-start.40 = (s32[2048]{0:T(1024)}, s32[2048]{0:T(1024)S(1)}, u32[]{:S(2)}) copy-start(s32[2048]{0:T(1024)S(1)} %pad_clamp_fusion.4) | copy-start | bytes 24580
  104.1 291.7 %copy-start.36 = (s32[4096]{0:T(1024)}, s32[4096]{0:T(1024)S(1)}, u32[]{:S(2)}) copy-start(s32[4096]{0:T(1024)S(1)} %pad_clamp_fusion.2) | copy-start | bytes 49156
  104.2 80.6 %copy-start.38 = (s32[4096]{0:T(1024)}, s32[4096]{0:T(1024)S(1)}, u32[]{:S(2)}) copy-start(s32[4096]{0:T(1024)S(1)} %pad_clamp_fusion.3) | copy-start | bytes 49156
  104.2 307.3 %copy-start.60 = (f32[8]{0:T(128)}, f32[8]{0:T(128)S(1)}, u32[]{:S(2)}) copy-start(f32[8]{0:T(128)S(1)} %get-tuple-element.45) | copy-start | bytes 100
  104.2 307.3 %copy-start.62 = (f32[8]{0:T(128)}, f32[8]{0:T(128)S(1)}, u32[]{:S(2)}) copy-start(f32[8]{0:T(128)S(1)} %get-tuple-element.46) | copy-start | bytes 100
  104.3 259.4 %copy-start.49 = (pred[1344]{0:T(1024)(128)(4,1)}, pred[1344]{0:T(1024)(128)(4,1)S(1)}, u32[]{:S(2)}) copy-start(pred[1344]{0:T(1024)(128)(4,1)S(1)} %compare_and_fusion.2) | copy-start | bytes 4036
  104.3 301.6 %copy-start.44 = (pred[3136]{0:T(1024)(128)(4,1)}, pred[3136]{0:T(1024)(128)(4,1)S(1)}, u32[]{:S(2)}) copy-start(pred[3136]{0:T(1024)(128)(4,1)S(1)} %compare_and_fusion) | copy-start | bytes 9412
  104.3 90.5 %copy-start.53 = (pred[3136]{0:T(1024)(128)(4,1)}, pred[3136]{0:T(1024)(128)(4,1)S(1)}, u32[]{:S(2)}) copy-start(pred[3136]{0:T(1024)(128)(4,1)S(1)} %compare_and_fusion.1) | copy-start | bytes 9412
  104.4 45.4 %copy-start.14 = (f32[8,7,56]{2,1,0:T(8,128)}, f32[8,7,56]{2,1,0:T(8,128)S(1)}, u32[]{:S(2)}) copy-start(f32[8,7,56]{2,1,0:T(8,128)S(1)} %broadcast_multiply_fusion.1) | copy-start | bytes 37636
  107.9 41.8 %copy-start.24 = (f32[8,7,56]{2,1,0:T(8,128)}, f32[8,7,56]{2,1,0:T(8,128)S(1)}, u32[]{:S(2)}) copy-start(f32[8,7,56]{2,1,0:T(8,128)S(1)} %fusion.43) | copy-start | bytes 37636
  149.7 270.2 %copy-start.47 = (f32[384]{0:T(512)}, f32[384]{0:T(512)S(1)}, u32[]{:S(2)}) copy-start(f32[384]{0:T(512)S(1)} %get-tuple-element.36) | copy-start | bytes 4612
  152.7 29.7 %copy-start.5 = (bf16[8,7,56,384]{3,2,1,0:T(8,128)(2,1)}, bf16[8,7,56,384]{3,2,1,0:T(8,128)(2,1)S(1)}, u32[]{:S(2)}) copy-start(bf16[8,7,56,384]{3,2,1,0:T(8,128)(2,1)S(1)} %add_convert_fusion.2) | copy-start | bytes 7225348
  153.8 28.6 %collective-permute-start = (bf16[8,3,56,384]{3,2,1,0:T(8,128)(2,1)}, bf16[8,3,56,384]{3,2,1,0:T(8,128)(2,1)}, u32[]{:S(2)}, u32[]{:S(2)}) collective-permute-start(bf16[8,3,56,384]{3,2,1,0:T(8,128)(2,1)} %slice.128), channel_id=1, source_target_pairs={{0,28},{4,0},{8,4},{12,8},{16,12},{20,16},{24,20},{28,24},{1,29},{... | collective-permute-start | bytes 3096584 | tf_op jit(solution)/shard_map/ppermute | solution.py:31
  366.1 27.4 %collective-permute-start.1 = (bf16[8,3,56,384]{3,2,1,0:T(8,128)(2,1)}, bf16[8,3,56,384]{3,2,1,0:T(8,128)(2,1)}, u32[]{:S(2)}, u32[]{:S(2)}) collective-permute-start(bf16[8,3,56,384]{3,2,1,0:T(8,128)(2,1)} %bitcast.18), channel_id=1, source_target_pairs={{0,4},{4,8},{8,12},{12,16},{16,20},{20,24},{24,28},{28,0},{1,5},{5... | collective-permute-start | bytes 3096584 | tf_op jit(solution)/shard_map/ppermute | solution.py:31
  419.9 50.0 %copy-start.34 = (f32[8,7,56]{2,1,0:T(8,128)}, f32[8,7,56]{2,1,0:T(8,128)S(1)}, u32[]{:S(2)}) copy-start(f32[8,7,56]{2,1,0:T(8,128)S(1)} %multiply_reduce_fusion.5) | copy-start | bytes 37636
  419.9 50.0 %copy-start.26 = (f32[8,7,56]{2,1,0:T(8,128)}, f32[8,7,56]{2,1,0:T(8,128)S(1)}, u32[]{:S(2)}) copy-start(f32[8,7,56]{2,1,0:T(8,128)S(1)} %fusion.44) | copy-start | bytes 37636
  421.0 48.9 %copy-start.6 = (bf16[8,7,56,384]{3,2,1,0:T(8,128)(2,1)}, bf16[8,7,56,384]{3,2,1,0:T(8,128)(2,1)S(1)}, u32[]{:S(2)}) copy-start(bf16[8,7,56,384]{3,2,1,0:T(8,128)(2,1)S(1)} %add_convert_fusion.1) | copy-start | bytes 7225348
  477.0 28.7 %slice-start.4 = ((s8[4816896]{0:T(1024)(128)(4,1)}), s8[4194304]{0:T(1024)(128)(4,1)S(1)}, s32[]{:S(2)}) async-start(s8[4816896]{0:T(1024)(128)(4,1)} %bitcast.148), calls=%async_computation.5 | async-start | bytes 8388608
  477.0 41.7 %slice-start.6 = ((s8[4816896]{0:T(1024)(128)(4,1)}), s8[4194304]{0:T(1024)(128)(4,1)S(1)}, s32[]{:S(2)}) async-start(s8[4816896]{0:T(1024)(128)(4,1)} %bitcast.154), calls=%async_computation.7 | async-start | bytes 8388608
  483.9 21.8 %copy-start.48 = (f32[384]{0:T(512)S(1)}, f32[384]{0:T(512)}, u32[]{:S(2)}) copy-start(f32[384]{0:T(512)} %copy-done.47) | copy-start | bytes 4612
  483.9 34.8 %slice-start.7 = ((s8[4816896]{0:T(1024)(128)(4,1)}), s8[622592]{0:T(1024)(128)(4,1)S(1)}, s32[]{:S(2)}) async-start(s8[4816896]{0:T(1024)(128)(4,1)} %bitcast.154), calls=%async_computation.8 | async-start | bytes 1245184
  527.8 23.2 %collective-permute-start.2 = (bf16[8,3,56,384]{3,2,1,0:T(8,128)(2,1)S(1)}, bf16[8,3,56,384]{3,2,1,0:T(8,128)(2,1)}, u32[]{:S(2)}, u32[]{:S(2)}) collective-permute-start(bf16[8,3,56,384]{3,2,1,0:T(8,128)(2,1)S(1)} %slice.143), channel_id=1, source_target_pairs={{0,28},{4,0},{8,4},{12,8},{16,12},{20,16},{24,20},{28,24},{1,29},{... | collective-permute-start | bytes 3096584 | tf_op jit(solution)/shard_map/ppermute | solution.py:31
  589.9 64.4 %slice-start.2 = ((s8[6291456]{0:T(1024)(128)(4,1)}), s8[2097152]{0:T(1024)(128)(4,1)S(1)}, s32[]{:S(2)}) async-start(s8[6291456]{0:T(1024)(128)(4,1)} %bitcast.146), calls=%async_computation.3 | async-start | bytes 4194304
  604.7 49.7 %slice-start.3 = ((s8[6291456]{0:T(1024)(128)(4,1)}), s8[4194304]{0:T(1024)(128)(4,1)S(1)}, s32[]{:S(2)}) async-start(s8[6291456]{0:T(1024)(128)(4,1)} %bitcast.146), calls=%async_computation.4 | async-start | bytes 8388608
  723.9 28.5 %copy-start.21 = (bf16[384,1152]{1,0:T(8,128)(2,1)S(1)}, bf16[384,1152]{1,0:T(8,128)(2,1)}, u32[]{:S(2)}) copy-start(bf16[384,1152]{1,0:T(8,128)(2,1)} %convert_element_type.176) | copy-start | bytes 2654212
  766.1 25.2 %collective-permute-start.3 = (bf16[8,3,56,384]{3,2,1,0:T(8,128)(2,1)}, bf16[8,3,56,384]{3,2,1,0:T(8,128)(2,1)S(1)}, u32[]{:S(2)}, u32[]{:S(2)}) collective-permute-start(bf16[8,3,56,384]{3,2,1,0:T(8,128)(2,1)} %bitcast.41), channel_id=1, source_target_pairs={{0,4},{4,8},{8,12},{12,16},{16,20},{20,24},{24,28},{28,0},{1,5},{5... | collective-permute-start | bytes 3096584 | tf_op jit(solution)/shard_map/ppermute | solution.py:31
  818.4 53.6 %copy-start.29 = (s32[21504]{0:T(1024)S(1)}, s32[21504]{0:T(1024)}, u32[]{:S(2)}) copy-start(s32[21504]{0:T(1024)} %pad_clamp_fusion) | copy-start | bytes 258052
  872.0 42.2 %copy-start.39 = (pred[20832]{0:T(1024)(128)(4,1)S(1)}, pred[20832]{0:T(1024)(128)(4,1)}, u32[]{:S(2)}) copy-start(pred[20832]{0:T(1024)(128)(4,1)} %broadcast_compare_fusion) | copy-start | bytes 62500
  1043.6 12.0 %collective-permute-start.4 = (f32[155,128]{1,0:T(8,128)S(1)}, f32[155,128]{1,0:T(8,128)S(1)}, u32[]{:S(2)}, u32[]{:S(2)}) collective-permute-start(f32[155,128]{1,0:T(8,128)S(1)} %slice.144), channel_id=1, source_target_pairs={{0,1},{1,2},{2,3},{3,4},{4,5},{5,6},{6,7},{7,8},{8,9},{9,10},{10,1... | collective-permute-start | bytes 238088
  (54 other events, 392.0 us)
Sparse Core Ops, SparseCore 0:
  10.9 90.3 all-gather.2
where the time goes:
time: 1080 us; the launch traced here: 1070 us
  local copies, waits for them, and re-layouts  466 us (43%)
  matrix products  265 us (25%)
  other arithmetic  148 us (14%)
  blocking collectives  117 us (11%)
  waiting for transfers between devices  41 us (4%)
  between operations  16.6 us (2%)
  starting transfers between devices  12.4 us (1%)
    unnamed x1, blocking collectives  117 us
    scatter x1, local copies, waits for them, and re-layouts, slot_owner_rows(): return jnp.full((slot_total,), -1, jnp.int32).at[slots].set(jnp.arange(sl...  65.2 us
    reshape x1, local copies, waits for them, and re-layouts, shards(): triple = triple.reshape(window_count, WIN * WIN, 3, HEADS, HD)  56.7 us
    concatenate x1, local copies, waits for them, and re-layouts, pack(): return jnp.concatenate(parts).reshape(-1, 128)  53.6 us
    dot_general x1, matrix products, shards(): jnp.dot(second_low, up_low, preferred_element_type=jnp.float32) + up_bias  48.1 us
    gather x1, local copies, waits for them, and re-layouts, shards(): packed_grad[jnp.maximum(sources, 0)]  42.2 us
    convert_element_type x2, local copies, waits for them, and re-layouts, shards(): grad_triple = jnp.stack([grad_query, grad_keys, grad_values], axis=2).ast...  41.9 us
    ppermute x4, waiting for transfers between devices, from_behind(): lax.ppermute(value, axis, [(i, (i + by) % peers) for i in range(peers)])  40.3 us
  transfers between devices with their start and end apart: 6, of which 4 were waited for; matrix products, arithmetic and copies ran while one was open for 15% of the time, Pallas kernels for 0%

commit v1 on v0

v1 whole, which is shorter than its diff:
```python
import math

import jax
import jax.numpy as jnp
import numpy as np
from jax import lax
from jax.experimental import pallas as pl
from jax.experimental.pallas import tpu as pltpu
from jax.sharding import PartitionSpec as P

C = 384
HEADS = 12
HD = 32
FF = 1536
WIN = 7
SHIFT = 3
STEP = 10
SMALL_ROWS = 39
TABLE_ROWS = 16


PRECISE = lax.Precision.HIGHEST
NORM_EPS = 1e-05
KEEP_PROB = 0.8
MASK_FILL = -100.0
BETA_ONE = 0.5
BETA_TWO = 0.5
ADAM_EPS = 1e-08
DECAY = 0.05


def from_behind(value, axis, by):
    peers = lax.axis_size(axis)
    return lax.ppermute(value, axis, [(i, (i + by) % peers) for i in range(peers)])


def row_edges():
    first = 3 * C * C // 128
    second = first + C * C // 128
    third = second + C * FF // 128
    fourth = third + FF * C // 128
    fifth = fourth + SMALL_ROWS
    return [first, second, third, fourth, fifth]


def row_kind(row_ids):
    kind = jnp.zeros(row_ids.shape, jnp.int32)
    for boundary in row_edges():
        kind = kind + (row_ids >= boundary).astype(jnp.int32)
    return jnp.where(row_ids < 0, 6, kind)


def row_rates(row_ids):
    kind = row_kind(row_ids)
    rates = [
        2.0 / math.sqrt(C),
        2.0 / math.sqrt(C // 8),
        2.0 / math.sqrt(C),
        2.0 / math.sqrt(FF),
        1.0,
        1.0,
        0.0,
    ]
    decays = [DECAY, DECAY, DECAY, DECAY, 0.0, 0.0, 0.0]
    rate_rows = jnp.zeros(row_ids.shape, jnp.float32)
    decay_rows = jnp.zeros(row_ids.shape, jnp.float32)
    for index, amount in enumerate(rates):
        rate_rows = rate_rows + jnp.where(kind == index, amount, 0.0).astype(jnp.float32)
        decay_rows = decay_rows + jnp.where(kind == index, decays[index], 0.0).astype(jnp.float32)
    return (rate_rows, decay_rows)


def slot_rows(owner_list, device_count, capacity):
    hits = (owner_list[:, None] == jnp.arange(device_count, dtype=jnp.int32)[None, :]).astype(
        jnp.int32
    )
    rank = jnp.sum(jnp.cumsum(hits, axis=0) * hits, axis=1) - 1
    return owner_list * capacity + rank


def slot_owner_rows(slots, slot_total):
    return (
        jnp.full((slot_total,), -1, jnp.int32)
        .at[slots]
        .set(jnp.arange(slots.shape[0], dtype=jnp.int32))
    )


def unpack(packed):
    flat = packed.reshape(-1)
    lengths = [C * 3 * C, C * C, C * FF, FF * C, 3 * C, C, FF, C, C, C, C, C]
    pieces = []
    start = 0
    for length in lengths:
        pieces.append(flat[start : start + length])
        start = start + length
    table_start = row_edges()[4] * 128
    table = flat[table_start : table_start + (2 * WIN - 1) ** 2 * HEADS].reshape(
        (2 * WIN - 1) ** 2, HEADS
    )
    matrices = (
        pieces[0].reshape(C, 3 * C),
        pieces[1].reshape(C, C),
        pieces[2].reshape(C, FF),
        pieces[3].reshape(FF, C),
    )
    return (matrices, pieces[4:12], table)


def pack(matrices, smalls, table):
    parts = [piece.reshape(-1) for piece in matrices] + [piece for piece in smalls]
    small_pad = SMALL_ROWS * 128 - (9 * C + FF)
    table_pad = TABLE_ROWS * 128 - (2 * WIN - 1) ** 2 * HEADS
    parts = parts + [
        jnp.zeros((small_pad,), jnp.float32),
        table.reshape(-1),
        jnp.zeros((table_pad,), jnp.float32),
    ]
    return jnp.concatenate(parts).reshape(-1, 128)


GROUPS = 3
GROUP_HEADS = HEADS // GROUPS
CELLS = WIN * 8
LANES = 64
LOG2E = math.log2(math.e)
F32 = jnp.float32
BF16 = jnp.bfloat16


def relative_pairs():
    key = np.arange(CELLS)
    query = np.arange(LANES)
    key_row, key_col = key // 8, key % 8
    query_row, query_col = query // 8, query % 8
    index = (query_row[None, :] - key_row[:, None] + WIN - 1) * (2 * WIN - 1)
    index = index + query_col[None, :] - key_col[:, None] + WIN - 1
    real = (key_col < WIN)[:, None] & ((query_col < WIN) & (query_row < WIN))[None, :]
    return np.where(real, index, -1).astype(np.int32)


def pair_onehot():
    pairs = jnp.asarray(relative_pairs().reshape(-1))
    return (pairs[:, None] == jnp.arange((2 * WIN - 1) ** 2, dtype=jnp.int32)[None, :]).astype(F32)


def attention_bias(table, last_strip):
    spread = lax.dot_general(
        table, pair_onehot(), (((0,), (1,)), ((), ())), precision=PRECISE, preferred_element_type=F32
    ).reshape(HEADS, CELLS, LANES)
    key, query = np.arange(CELLS), np.arange(LANES)
    key_low, query_low = key // 8 >= WIN - SHIFT, query // 8 >= WIN - SHIFT
    key_side, query_side = key % 8 >= WIN - SHIFT, query % 8 >= WIN - SHIFT
    by_row = key_low[:, None] != query_low[None, :]
    by_col = key_side[:, None] != query_side[None, :]
    by_row = jnp.asarray(by_row) & last_strip
    both = jnp.stack([by_row, by_row | jnp.asarray(by_col)])
    masking = jnp.where(both, MASK_FILL, 0.0).astype(F32)
    total = spread[None] + masking[:, None]
    total = jnp.where(jnp.asarray(key % 8 < WIN)[None, None, :, None], total * LOG2E, -1e30)
    total = total.reshape(2, GROUPS, GROUP_HEADS, CELLS, LANES).transpose(0, 1, 3, 2, 4)
    return total.reshape(2, GROUPS, CELLS, GROUP_HEADS * LANES)


def nn(left, right):
    return lax.dot_general(left, right, (((1,), (0,)), ((), ())), preferred_element_type=F32)


def nt(left, right):
    return lax.dot_general(left, right, (((1,), (1,)), ((), ())), preferred_element_type=F32)


def tn(left, right):
    return lax.dot_general(left, right, (((0,), (0,)), ((), ())), preferred_element_type=F32)


def gelu_pair(u):
    x = jnp.abs(u) * (0.3275911 / math.sqrt(2.0)) + 1.0
    t = pl.reciprocal(x)
    gauss = jnp.exp2(u * u * (-0.5 * LOG2E))
    poly = t * (0.5 * 1.061405429) - 0.5 * 1.453152027
    poly = poly * t + 0.5 * 1.421413741
    poly = poly * t - 0.5 * 0.284496736
    poly = poly * t + 0.5 * 0.254829592
    tail = poly * t * gauss
    normal = jnp.where(u >= 0, 1.0 - tail, tail)
    return u * normal, normal + u * gauss * (1.0 / math.sqrt(2.0 * math.pi))


def row_norm(values):
    center = values - jnp.mean(values, axis=-1, keepdims=True)
    scale = lax.rsqrt(jnp.mean(center * center, axis=-1, keepdims=True) + NORM_EPS)
    return center * scale, scale


def norm_pull(grad, normal, scale):
    first = jnp.mean(grad, axis=-1, keepdims=True)
    second = jnp.mean(grad * normal, axis=-1, keepdims=True)
    return scale * (grad - first - normal * second)


def column_sum(values):
    return jnp.sum(values, axis=0, keepdims=True)


def block_kernel(
    cols_ref, keep_ref, x_ref, xh_ref, dy_ref, dyh_ref, bias_ref,
    wq_ref, wp_ref, wu_ref, wd_ref, bq_ref, bp_ref, bu_ref, bd_ref, g1_ref, b1_ref, g2_ref, b2_ref,
    out_ref, outh_ref, gx_ref, gxh_ref,
    gwq_ref, gwp_ref, gwu_ref, gwdt_ref,
    gbq_ref, gbp_ref, gbu_ref, gbd_ref, gg1_ref, gb1_ref, gg2_ref, gb2_ref, gs_ref,
    line, xw, dyw, n1s, zs, qkv, prob, ctx, x1s, n2s, h2s, gfs, ys, gh2s, gctx, gqkv, resw, htr, gtr,
):
    step = pl.program_id(0)
    width = cols_ref[0] * WIN
    keep_one = keep_ref[step, 0]
    keep_two = keep_ref[step, 1]
    wide = xw.shape[0] // CELLS
    columns = x_ref.shape[2]
    slabs = C // 128
    own = WIN - SHIFT

    @pl.when(step == 0)
    def _():
        line[...] = jnp.zeros_like(line)
        qkv[...] = jnp.zeros_like(qkv)
        gctx[...] = jnp.zeros_like(gctx)
        for ref in (gwq_ref, gwp_ref, gwu_ref, gwdt_ref, gbq_ref, gbp_ref, gbu_ref, gbd_ref,
                    gg1_ref, gb1_ref, gg2_ref, gb2_ref, gs_ref):
            ref[...] = jnp.zeros_like(ref)

    def to_windows(main, halo, target):
        for a in range(WIN):
            row = main[0, SHIFT + a] if a < own else halo[0, a - own].astype(F32)
            for s in range(slabs):
                part = row[:, s * 128 : s * 128 + 128]
                line[s, a, 0:columns, :] = part
                line[s, a, pl.ds(width, 8), :] = part[0:8]
        for w in range(wide):
            for a in range(WIN):
                for s in range(slabs):
                    target[w * CELLS + a * 8 : w * CELLS + a * 8 + 8, s * 128 : s * 128 + 128] = line[
                        s, a, w * WIN + SHIFT : w * WIN + SHIFT + 8, :
                    ]

    def from_windows(source, main, halo):
        for w in range(wide):
            for a in range(WIN):
                for s in range(slabs):
                    line[s, a, w * WIN + SHIFT : w * WIN + SHIFT + 8, :] = source[
                        w * CELLS + a * 8 : w * CELLS + a * 8 + 8, s * 128 : s * 128 + 128
                    ]
        kept = lax.broadcasted_iota(jnp.int32, (columns, 128), 0) < width
        front = lax.broadcasted_iota(jnp.int32, (8, 128), 0) < SHIFT
        for a in range(WIN):
            for s in range(slabs):
                wrapped = line[s, a, pl.ds(width, 8), :]
                line[s, a, 0:8, :] = jnp.where(front, wrapped, line[s, a, 0:8, :])
                row = jnp.where(kept, line[s, a, 0:columns, :], 0.0)
                if a < own:
                    main[0, SHIFT + a, :, s * 128 : s * 128 + 128] = row
                else:
                    halo[0, a - own, :, s * 128 : s * 128 + 128] = row.astype(BF16)

    to_windows(x_ref, xh_ref, xw)
    to_windows(dy_ref, dyh_ref, dyw)

    normal, scale_one = row_norm(xw[...])
    n1s[...] = normal
    z = normal * g1_ref[...] + b1_ref[...]
    zs[...] = z.astype(BF16)
    triple = nn(zs[...], wq_ref[...]) + bq_ref[...]
    for w in range(wide):
        qkv[w, 0:CELLS, :] = triple[w * CELLS : w * CELLS + CELLS].astype(BF16)

    lane_head = lax.broadcasted_iota(jnp.int32, (1, 128), 1) // HD
    head_bits = [(lane_head == h).astype(F32).astype(BF16) for h in range(GROUP_HEADS)]

    def stack_of(part):
        return jnp.concatenate([part * head_bits[h] for h in range(GROUP_HEADS)], axis=0)

    def unstack(part):
        total = None
        for h in range(GROUP_HEADS):
            piece = jnp.where(lane_head == h, part[h * LANES : h * LANES + CELLS], 0.0)
            total = piece if total is None else total + piece
        return total

    score_scale = HD ** (-0.5)

    def attend(w, _):
        variant = (w == cols_ref[0] - 1).astype(jnp.int32)
        rows = pl.ds(pl.multiple_of(w * CELLS, 8), CELLS)
        for g in range(GROUPS):
            q = qkv[w, :, g * 128 : g * 128 + 128]
            k = qkv[w, 0:CELLS, C + g * 128 : C + g * 128 + 128]
            v = qkv[w, 0:CELLS, 2 * C + g * 128 : 2 * C + g * 128 + 128]
            s = nt(k, stack_of(q)) * (score_scale * LOG2E) + bias_ref[variant, g]
            e = jnp.exp2(s - jnp.max(s, axis=0, keepdims=True))
            a = e * (1.0 / jnp.sum(e, axis=0, keepdims=True))
            prob[w, g] = a
            ctx[rows, g * 128 : g * 128 + 128] = unstack(tn(a.astype(BF16), v))
        return 0

    lax.fori_loop(0, wide, attend, 0)

    ctx_low = ctx[...].astype(BF16)
    x1 = xw[...] + keep_one * (nn(ctx_low, wp_ref[...]) + bp_ref[...])
    x1s[...] = x1
    normal, scale_two = row_norm(x1)
    n2s[...] = normal
    h2 = (normal * g2_ref[...] + b2_ref[...]).astype(BF16)
    h2s[...] = h2
    htr[...] = h2.astype(F32).T.astype(BF16)

    token = lax.broadcasted_iota(jnp.int32, (wide * CELLS, 1), 0)
    valid = ((token % 8 < WIN) & (token < cols_ref[0] * CELLS)).astype(F32)
    gy = dyw[...] * valid
    gf = (gy * keep_two).astype(BF16)
    gfs[...] = gf
    gbd_ref[...] += column_sum(gf.astype(F32))
    gtr[...] = gf.astype(F32).T.astype(BF16)
    ys[...] = jnp.zeros_like(ys)
    gh2s[...] = jnp.zeros_like(gh2s)

    chunk = 512

    def feed(j, _):
        part = pl.ds(pl.multiple_of(j * chunk, chunk), chunk)
        u = nn(h2s[...], wu_ref[:, part]) + bu_ref[:, part]
        gm = nt(gfs[...], wd_ref[part, :])
        m, slope = gelu_pair(u)
        m = m.astype(BF16)
        gu = (gm * slope).astype(BF16)
        ys[...] += nn(m, wd_ref[part, :])
        gwdt_ref[:, part] += nn(gtr[...], m)
        gwu_ref[:, part] += nn(htr[...], gu)
        gbu_ref[:, part] += column_sum(gu.astype(F32))
        gh2s[...] += nt(gu, wu_ref[:, part])
        return 0

    lax.fori_loop(0, FF // chunk, feed, 0)

    resw[...] = (x1s[...] + keep_two * (ys[...] + bd_ref[...])) * valid
    from_windows(resw, out_ref, outh_ref)

    gh2 = gh2s[...]
    gg2_ref[...] += column_sum(gh2 * n2s[...])
    gb2_ref[...] += column_sum(gh2)
    gx1 = dyw[...] * valid + norm_pull(gh2 * g2_ref[...], n2s[...], scale_two)
    x1s[...] = gx1
    ga = (keep_one * gx1).astype(BF16)
    gbp_ref[...] += column_sum(ga.astype(F32))
    gwp_ref[...] += nn(ctx[...].T.astype(BF16), ga)
    gc = nt(ga, wp_ref[...])
    for w in range(wide):
        gctx[w, 0:CELLS, :] = gc[w * CELLS : w * CELLS + CELLS].astype(BF16)

    def pull(w, _):
        rows = pl.ds(pl.multiple_of(w * CELLS, 8), CELLS)
        for g in range(GROUPS):
            q = qkv[w, :, g * 128 : g * 128 + 128]
            k = qkv[w, 0:CELLS, C + g * 128 : C + g * 128 + 128]
            v = qkv[w, 0:CELLS, 2 * C + g * 128 : 2 * C + g * 128 + 128]
            gstack = stack_of(gctx[w, :, g * 128 : g * 128 + 128])
            a = prob[w, g]
            grad = nt(v, gstack)
            inner = jnp.sum(grad * a, axis=0, keepdims=True)
            gs = (a * (grad - inner)).astype(BF16)
            gs_ref[g] += gs.astype(F32)
            gqkv[rows, g * 128 : g * 128 + 128] = unstack(tn(gs, k)) * score_scale
            gqkv[rows, C + g * 128 : C + g * 128 + 128] = nn(gs, stack_of(q)) * score_scale
            gqkv[rows, 2 * C + g * 128 : 2 * C + g * 128 + 128] = nn(a.astype(BF16), gstack)
        return 0

    lax.fori_loop(0, wide, pull, 0)

    gtriple = gqkv[...].astype(BF16)
    gbq_ref[...] += column_sum(gtriple.astype(F32))
    gwq_ref[...] += nn(zs[...].astype(F32).T.astype(BF16), gtriple)
    gz = nt(gtriple, wq_ref[...]).astype(BF16).astype(F32)
    gg1_ref[...] += column_sum(gz * n1s[...])
    gb1_ref[...] += column_sum(gz)
    resw[...] = x1s[...] + norm_pull(gz * g1_ref[...], n1s[...], scale_one)
    from_windows(resw, gx_ref, gxh_ref)


def run_block(cols, keep, x, xh, dy, dyh, bias, weights, vectors):
    samples, rows, columns, _ = x.shape
    wide = columns // WIN
    tokens = wide * CELLS

    def per_image(array):
        return pl.BlockSpec((1,) + array.shape[1:], lambda i: (i, 0, 0, 0))

    def whole(shape):
        return pl.BlockSpec(shape, lambda i: (0,) * len(shape))

    smem = pl.BlockSpec(memory_space=pltpu.SMEM)
    full = jax.ShapeDtypeStruct(x.shape, F32)
    part = jax.ShapeDtypeStruct(xh.shape, BF16)
    grads = [(C, 3 * C), (C, C), (C, FF), (C, FF), (1, 3 * C), (1, C), (1, FF), (1, C),
             (1, C), (1, C), (1, C), (1, C), (GROUPS, CELLS, GROUP_HEADS * LANES)]
    return pl.pallas_call(
        block_kernel,
        grid=(samples,),
        in_specs=[smem, smem, per_image(x), per_image(xh), per_image(dy), per_image(dyh), whole(bias.shape)]
        + [whole(w.shape) for w in weights] + [whole(v.shape) for v in vectors],
        out_specs=[per_image(x), per_image(xh), per_image(x), per_image(xh)] + [whole(s) for s in grads],
        out_shape=[full, part, full, part] + [jax.ShapeDtypeStruct(s, F32) for s in grads],
        scratch_shapes=[
            pltpu.VMEM((C // 128, WIN, columns + 8, 128), F32),
            pltpu.VMEM((tokens, C), F32),
            pltpu.VMEM((tokens, C), F32),
            pltpu.VMEM((tokens, C), F32),
            pltpu.VMEM((tokens, C), BF16),
            pltpu.VMEM((wide, LANES, 3 * C), BF16),
            pltpu.VMEM((wide, GROUPS, CELLS, GROUP_HEADS * LANES), F32),
            pltpu.VMEM((tokens, C), F32),
            pltpu.VMEM((tokens, C), F32),
            pltpu.VMEM((tokens, C), F32),
            pltpu.VMEM((tokens, C), BF16),
            pltpu.VMEM((tokens, C), BF16),
            pltpu.VMEM((tokens, C), F32),
            pltpu.VMEM((tokens, C), F32),
            pltpu.VMEM((wide, LANES, C), BF16),
            pltpu.VMEM((tokens, 3 * C), F32),
            pltpu.VMEM((tokens, C), F32),
            pltpu.VMEM((C, tokens), BF16),
            pltpu.VMEM((C, tokens), BF16),
        ],
        compiler_params=pltpu.CompilerParams(vmem_limit_bytes=58 * 1024 * 1024),
        name="block",
    )(cols, keep, x, xh, dy, dyh, bias, *weights, *vectors)


def adamw(weights, first, second, grads, row_ids):
    rate_rows, decay_rows = row_rates(row_ids)
    first = BETA_ONE * first + (1.0 - BETA_ONE) * grads
    second = BETA_TWO * second + (1.0 - BETA_TWO) * grads * grads
    first_hat = first / (1.0 - BETA_ONE**STEP)
    second_hat = second / (1.0 - BETA_TWO**STEP)
    weights = weights - rate_rows[:, None] * (
        first_hat / (jnp.sqrt(second_hat) + ADAM_EPS) + decay_rows[:, None] * weights
    )
    return (first, second, weights)


def shards(
    block_input, cotangent, window_cols, keep_mask, owner_list, master, first_moment, second_moment
):
    strips = lax.axis_size("strip")
    device_count = strips * lax.axis_size("bucket")
    capacity = master.shape[0]
    x_halo = from_behind(block_input[:, :SHIFT].astype(BF16), "strip", -1)
    dy_halo = from_behind(cotangent[:, :SHIFT].astype(BF16), "strip", -1)
    slots = slot_rows(owner_list, device_count, capacity)
    sources = slot_owner_rows(slots, device_count * capacity)
    gathered = lax.all_gather(master, ("strip", "bucket"), axis=0, tiled=True)
    matrices, smalls, table = unpack(gathered[slots])
    weights = [matrix.astype(BF16) for matrix in matrices]
    vectors = [small.reshape(1, -1) for small in smalls]
    bias = attention_bias(table, lax.axis_index("strip") == strips - 1)
    keep = keep_mask.astype(F32) / KEEP_PROB
    results = run_block(
        window_cols, keep, block_input, x_halo, cotangent, dy_halo, bias, weights, vectors
    )
    output, output_halo, grad_input, grad_halo = results[:4]
    gwq, gwp, gwu, gwdt = results[4:8]
    smalls_grad = [small.reshape(-1) for small in results[8:16]]
    pair_sums = results[16].reshape(GROUPS, CELLS, GROUP_HEADS, LANES).transpose(0, 2, 1, 3)
    grad_table = lax.dot_general(
        pair_onehot(), pair_sums.reshape(HEADS, -1), (((0,), (1,)), ((), ())),
        precision=PRECISE, preferred_element_type=F32,
    )
    output = output.at[:, :SHIFT].set(from_behind(output_halo, "strip", 1).astype(F32))
    grad_input = grad_input.at[:, :SHIFT].set(from_behind(grad_halo, "strip", 1).astype(F32))
    packed_grad = pack([gwq, gwp, gwu, gwdt.T], smalls_grad, grad_table)
    my_index = lax.axis_index(("strip", "bucket"))
    my_sources = lax.dynamic_slice_in_dim(sources, my_index * capacity, capacity)
    spread_out = jnp.where((sources >= 0)[:, None], packed_grad[jnp.maximum(sources, 0)], 0.0)
    grads = lax.psum_scatter(spread_out, ("strip", "bucket"), scatter_dimension=0, tiled=True)
    first, second_new, new_weights = adamw(master, first_moment, second_moment, grads, my_sources)
    return (output, grad_input, first, second_new, new_weights)


def solution(mesh):
    in_specs = (
        P("bucket", "strip", None, None),
        P("bucket", "strip", None, None),
        P("bucket"),
        P("bucket", None),
        P(),
        P(("strip", "bucket"), None),
        P(("strip", "bucket"), None),
        P(("strip", "bucket"), None),
    )
    out_specs = (
        P("bucket", "strip", None, None),
        P("bucket", "strip", None, None),
        P(("strip", "bucket"), None),
        P(("strip", "bucket"), None),
        P(("strip", "bucket"), None),
    )
    return jax.shard_map(shards, mesh=mesh, in_specs=in_specs, out_specs=out_specs, check_vma=False)
```

time: 1080 us -> 675 us (0.62)
  matrix products: 265 us -> 4.5 us
  local copies, waits for them, and re-layouts: 466 us -> 247 us
  Pallas kernels: 0 us -> 193 us
  other arithmetic: 148 us -> 51.6 us
  waiting for transfers between devices: 41 us -> 23.7 us
    dot_general x20 -> x2, matrix products: 265 us -> 4.5 us  [the longest x1 3.26 us: attention_bias(): lax.dot_general(table, pair_onehot(), (((0,), (1,)), ((), ())), precision...]
    pallas_call x0 -> x1, Pallas kernels: none -> 193 us  [run_block(): pl.pallas_call(block_kernel, grid=(samples,), in_specs=[smem, smem, per_i...]
    reshape x5 -> x6, local copies, waits for them, and re-layouts: 91.9 us -> 3.02 us  [the longest x3 1.77 us: shards(): vectors = [small.reshape(1, -1) for small in smalls]]
    reduce_sum x12 -> x0, other arithmetic: 76.8 us -> none  [the longest x1 19.7 us: shards(): jnp.sum(grad_scores, axis=0, dtype=jnp.float32).transpose(1, 2, 0)]
    convert_element_type x9 -> x4, local copies, waits for them, and re-layouts: 72.3 us -> 9.05 us  [shards(): weights = [matrix.astype(BF16) for matrix in matrices]]
    gather x7 -> x0, local copies, waits for them, and re-layouts: 51.2 us -> none  [the longest x1 10.2 us: shards(): jnp.take(extended, to_windows, axis=0)]
    ppermute x4, waiting for transfers between devices: 40.3 us -> 0.01 us  [from_behind(): lax.ppermute(value, axis, [(i, (i + by) % peers) for i in range(peers)])]
    all_gather x1, waiting for transfers between devices: 0.01 us -> 22.9 us  [shards(): gathered = lax.all_gather(master, ('strip', 'bucket'), axis=0, tiled=True)]
  transfers between devices with their start and end apart: 6 -> 6, of which waited for: 4 -> 2; matrix products, arithmetic and copies ran while one was open for 15% -> 62% of each run, Pallas kernels for 0% -> 0%
where the time goes in v1:
time: 675 us; the launch traced here: 667 us
  local copies, waits for them, and re-layouts  247 us (37%)
  Pallas kernels  193 us (29%)
  blocking collectives  121 us (18%)
  other arithmetic  51.6 us (8%)
  waiting for transfers between devices  23.7 us (4%)
  between operations  15 us (2%)
  starting transfers between devices  11.4 us (2%)
    pallas_call x1, Pallas kernels, run_block(): pl.pallas_call(block_kernel, grid=(samples,), in_specs=[smem, smem, per_i...  193 us
    unnamed x1, blocking collectives  121 us
    scatter x1, local copies, waits for them, and re-layouts, slot_owner_rows(): return jnp.full((slot_total,), -1, jnp.int32).at[slots].set(jnp.arange(sl...  65.2 us
    concatenate x1, local copies, waits for them, and re-layouts, pack(): return jnp.concatenate(parts).reshape(-1, 128)  60.7 us
    gather x1, local copies, waits for them, and re-layouts, shards(): packed_grad[jnp.maximum(sources, 0)]  42.2 us
    gather x1, local copies, waits for them, and re-layouts, shards(): matrices, smalls, table = unpack(gathered[slots])  30.6 us
    all_gather x1, waiting for transfers between devices, shards(): gathered = lax.all_gather(master, ('strip', 'bucket'), axis=0, tiled=True)  22.9 us
    another operation x5, other arithmetic  22.7 us
  transfers between devices with their start and end apart: 6, of which 2 were waited for; matrix products, arithmetic and copies ran while one was open for 62% of the time, Pallas kernels for 0%

profile of v1, /device:TPU:0, one launch (start us, length us, event | category | flops | bytes accessed | tf_op | source)
XLA Modules:
  0.0 666.9 jit_solution(9556368248333949257)
XLA Ops:
  7.9 2.7 slice.181
  10.6 6.0 collective-permute-start.1
  16.6 2.7 slice.182
  21.9 1.5 reshape.288
  23.4 18.4 %reduce-window.6 = s32[32,109,128]{2,1,0:T(8,128)S(1)} reduce-window(s32[32,109,128]{2,1,0:T(8,128)} %reshape.288, s32[]{:T(128)} %constant.112.clone.1), window={size=1x1x128 pad=0_0x0_0x127_0}, to_apply=%region_0.0 | reduce-window | flops 56700928 | bytes 3571716 | tf_op jit(solution)/shard_map/reduce-window
  44.7 65.2 %scatter_custom_fusion = s32[20832]{0:T(1024)S(1)} fusion(s32[13879]{0:T(1024)S(1)} %compare_select_fusion, s32[13879]{0:T(1024)S(1)} %iota.17, s32[]{:T(128)} %constant.113.clone.1), kind=kCustom, calls=%fused_computation.36 | custom fusion | bytes 83332 | tf_op jit(solution)/shard_map/scatter | solution.py:85
  111.9 22.9 %all-gather.3.cloned.1.call-done = f32[32,651,128]{2,1,0:T(8,128)} async-done(((f32[1,651,128]{2,1,0:T(8,128)}), f32[32,651,128]{2,1,0:T(8,128)}) %all-gather.3.cloned.1.call-update) | async-done | bytes 10666000 | tf_op jit(solution)/shard_map/all_gather | solution.py:459
  134.8 8.2 %reshape.317 = f32[20832,128]{1,0:T(8,128)} reshape(f32[32,651,128]{2,1,0:T(8,128)} %all-gather.3.cloned.1.call-done) | data formatting | bytes 21331968
  143.0 30.6 %gather_fusion = f32[13879,128]{1,0:T(8,128)} fusion(f32[20832,128]{1,0:T(8,128)} %reshape.317, s32[14336]{0:T(1024)S(1)} %pad_clamp_fusion.1), kind=kCustom, calls=%fused_computation | custom fusion | bytes 14267612 | tf_op jit(solution)/shard_map/gather | solution.py:460
  175.0 3.3 convert.20
  179.1 2.0 fusion.17
  181.1 1.3 slice.153
  184.6 1.8 convert_element_type.44.wp_ref
  186.5 3.3 fusion.8
  190.0 3.1 convert_element_type.46.wd_ref
  193.1 1.9 convert_element_type.43.wq_ref
  195.0 2.2 convert_element_type.45.wu_ref
  200.7 192.9 %block.1 = (f32[8,7,56,384]{3,2,1,0:T(8,128)}, bf16[8,3,56,384]{3,2,1,0:T(8,128)(2,1)}, f32[8,7,56,384]{3,2,1,0:T(8,128)}, bf16[8,3,56,384]{3,2,1,0:T(8,128)(2,1...) custom-call(s32[1]{0:T(128)S(6)} %copy.61.cols_ref, ...), custom_call_target="tpu_custom_call" | custom-call | tf_op jit(solution)/shard_map/block/pallas_call | solution.py:404
  400.4 1.2 fusion.4
  402.9 1.5 collective-permute-start.2
  404.4 1.3 collective-permute-start.3
  405.6 2.5 reshape.272
  408.2 1.5 reshape.274
  409.7 2.0 copy.31
  411.8 1.6 reshape.275
  413.3 60.7 %concatenate.11 = f32[1776512]{0:T(1024)} concatenate(f32[442368]{0:T(1024)} %reshape.272, f32[147456]{0:T(1024)S(1)} %reshape.273, f32[589824]{0:T(1024)} %reshape.274, f32[589824]{0:T(1024)} %reshape.275, f32[1152]{0:T(1024)S(1)} %reduce.5, f32[384]{0:T(512)S(1)} %reduce.6, f32[1536]{0:T(1024)S(1)} %reduce.7, f32[384]{0:T(512)S(1)} %reduce.8, f32[384]{0:T(512)S(1)} %reduce.9, ...), dimensions={0} | concatenate | bytes 14212096 | tf_op jit(solution)/shard_map/concatenate | solution.py:119
  474.0 42.2 %gather_fusion.1 = f32[20832,128]{1,0:T(8,128)} fusion(f32[13879,128]{1,0:T(8,128)} %bitcast.77, s32[21504]{0:T(1024)S(1)} %copy-done.7), kind=kCustom, calls=%fused_computation.1 | custom fusion | bytes 21415296 | tf_op jit(solution)/shard_map/gather | solution.py:481
  516.3 12.8 %broadcast_select_fusion = f32[20832,128]{1,0:T(8,128)} fusion(f32[20832,128]{1,0:T(8,128)} %gather_fusion.1, pred[20832]{0:T(1024)(128)(4,1)S(1)} %copy-done.10), kind=kLoop, calls=%fused_computation.3 | loop fusion | flops 2666496 | bytes 21352800 | tf_op jit(solution)/shard_map/jit(_where)/select_n | solution.py:481
  529.1 120.5 %fusion = f32[656,128]{1,0:T(8,128)S(1)} fusion(f32[20832,128]{1,0:T(8,128)} %broadcast_select_fusion), kind=kCustom, calls=%all-reduce-scatter | all-reduce-scatter fusion | flops 2686977 | bytes 11001856
  649.6 2.1 collective-permute-start.4
  654.7 2.7 convert_dynamic-update-slice_fusion.1
  657.4 2.7 convert_dynamic-update-slice_fusion
  (93 shorter events, 26.5 us)
Async XLA Ops:
  7.2 13.4 %copy-start.11 = (pred[56,64]{1,0:T(8,128)(4,1)S(1)}, pred[56,64]{1,0:T(8,128)(4,1)}, u32[]{:S(2)}) copy-start(pred[56,64]{1,0:T(8,128)(4,1)} %constant.144.clone) | copy-start | bytes 10756
  7.2 13.4 %copy-start.12 = (pred[56,64]{1,0:T(8,128)(4,1)S(1)}, pred[56,64]{1,0:T(8,128)(4,1)}, u32[]{:S(2)}) copy-start(pred[56,64]{1,0:T(8,128)(4,1)} %constant.143.clone) | copy-start | bytes 10756
  7.2 13.3 %copy-start.13 = (s32[8,2]{0,1:T(2,128)S(1)}, s32[8,2]{0,1:T(2,128)}, u32[]{:S(2)}) copy-start(s32[8,2]{0,1:T(2,128)} %param.20) | copy-start | bytes 196
  7.2 14.3 %copy-start.5 = (s32[13879]{0:T(1024)S(1)}, s32[13879]{0:T(1024)}, u32[]{:S(2)}) copy-start(s32[13879]{0:T(1024)} %param.21) | copy-start | bytes 166552
  7.2 127.6 %all-gather.3.cloned.1.call-start = ((), (), s32[]{:S(2)}) async-start(), calls=%async_computation | async-start | bytes 11083776 | tf_op jit(solution)/shard_map/all_gather | solution.py:459
  10.6 190.0 %collective-permute-start.1 = (bf16[8,3,56,384]{3,2,1,0:T(8,128)(2,1)}, bf16[8,3,56,384]{3,2,1,0:T(8,128)(2,1)}, u32[]{:S(2)}, u32[]{:S(2)}) collective-permute-start(bf16[8,3,56,384]{3,2,1,0:T(8,128)(2,1)} %slice.181), channel_id=1, source_target_pairs={{0,28},{4,0},{8,4},{12,8},{16,12},{20,16},{24,20},{28,24},{1,29},{... | collective-permute-start | bytes 3096584 | tf_op jit(solution)/shard_map/ppermute | solution.py:34
  19.3 181.3 %collective-permute-start = (bf16[8,3,56,384]{3,2,1,0:T(8,128)(2,1)}, bf16[8,3,56,384]{3,2,1,0:T(8,128)(2,1)}, u32[]{:S(2)}, u32[]{:S(2)}) collective-permute-start(bf16[8,3,56,384]{3,2,1,0:T(8,128)(2,1)} %slice.182), channel_id=1, source_target_pairs={{0,28},{4,0},{8,4},{12,8},{16,12},{20,16},{24,20},{28,24},{1,29},{... | collective-permute-start | bytes 3096584 | tf_op jit(solution)/shard_map/ppermute | solution.py:34
  110.0 33.0 %copy-start.4 = (s32[20832]{0:T(1024)}, s32[20832]{0:T(1024)S(1)}, u32[]{:S(2)}) copy-start(s32[20832]{0:T(1024)S(1)} %scatter_custom_fusion) | copy-start | bytes 249988
  178.3 4.7 copy-start
  183.6 9.5 %slice-start = ((bf16[13879,128]{1,0:T(8,128)(2,1)}), bf16[3456,128]{1,0:T(8,128)(2,1)S(1)}, s32[]{:S(2)}) async-start(bf16[13879,128]{1,0:T(8,128)(2,1)} %copy-done), calls=%async_computation.1 | async-start | bytes 1769472 | tf_op jit(solution)/shard_map/slice | solution.py:95
  183.6 11.4 %copy-start.1 = (bf16[4608,128]{1,0:T(8,128)(2,1)S(1)}, bf16[4608,128]{1,0:T(8,128)(2,1)}, u32[]{:S(2)}) copy-start(bf16[4608,128]{1,0:T(8,128)(2,1)} %get-tuple-element.73) | copy-start | bytes 3538948
  189.7 10.1 %copy-start.6 = (f32[2,56,256]{2,1,0:T(8,128)S(1)}, f32[2,56,256]{2,1,0:T(8,128)}, u32[]{:S(2)}) copy-start(f32[2,56,256]{2,1,0:T(8,128)} %add.107) | copy-start | bytes 344068
  189.7 10.1 %copy-start.14 = (pred[56]{0:T(512)(128)(4,1)S(1)}, pred[56]{0:T(512)(128)(4,1)}, u32[]{:S(2)}) copy-start(pred[56]{0:T(512)(128)(4,1)} %constant.145.clone) | copy-start | bytes 172
  200.6 199.8 %copy-start.15 = (s32[3584]{0:T(1024)S(1)}, s32[3584]{0:T(1024)}, u32[]{:S(2)}) copy-start(s32[3584]{0:T(1024)} %constant.142.clone) | copy-start | bytes 43012
  400.2 8.0 %copy-start.2 = (f32[384,1536]{1,0:T(8,128)S(1)}, f32[384,1536]{1,0:T(8,128)}, u32[]{:S(2)}) copy-start(f32[384,1536]{1,0:T(8,128)} %get-tuple-element.52) | copy-start | bytes 7077892
  402.9 251.8 %collective-permute-start.2 = (bf16[8,3,56,384]{3,2,1,0:T(8,128)(2,1)}, bf16[8,3,56,384]{3,2,1,0:T(8,128)(2,1)}, u32[]{:S(2)}, u32[]{:S(2)}) collective-permute-start(bf16[8,3,56,384]{3,2,1,0:T(8,128)(2,1)} %get-tuple-element.47), channel_id=1, source_target_pairs={{0,4},{4,8},{8,12},{12,16},{16,20},{20,24},{24,28},{28,0},{1,5},{5... | collective-permute-start | bytes 3096584 | tf_op jit(solution)/shard_map/ppermute | solution.py:34
  404.4 253.0 %collective-permute-start.3 = (bf16[8,3,56,384]{3,2,1,0:T(8,128)(2,1)}, bf16[8,3,56,384]{3,2,1,0:T(8,128)(2,1)}, u32[]{:S(2)}, u32[]{:S(2)}) collective-permute-start(bf16[8,3,56,384]{3,2,1,0:T(8,128)(2,1)} %get-tuple-element.49), channel_id=1, source_target_pairs={{0,4},{4,8},{8,12},{12,16},{16,20},{20,24},{24,28},{28,0},{1,5},{5... | collective-permute-start | bytes 3096584 | tf_op jit(solution)/shard_map/ppermute | solution.py:34
  413.3 60.7 %copy-start.7 = (s32[21504]{0:T(1024)S(1)}, s32[21504]{0:T(1024)}, u32[]{:S(2)}) copy-start(s32[21504]{0:T(1024)} %pad_clamp_fusion) | copy-start | bytes 258052
  474.0 42.2 %copy-start.10 = (pred[20832]{0:T(1024)(128)(4,1)S(1)}, pred[20832]{0:T(1024)(128)(4,1)}, u32[]{:S(2)}) copy-start(pred[20832]{0:T(1024)(128)(4,1)} %broadcast_compare_fusion) | copy-start | bytes 62500
  529.0 124.4 %copy-start.3 = (f32[651,128]{1,0:T(8,128)S(1)}, f32[651,128]{1,0:T(8,128)}, u32[]{:S(2)}) copy-start(f32[651,128]{1,0:T(8,128)} %param.22) | copy-start | bytes 999940
  529.0 124.4 %copy-start.8 = (f32[651,128]{1,0:T(8,128)S(1)}, f32[651,128]{1,0:T(8,128)}, u32[]{:S(2)}) copy-start(f32[651,128]{1,0:T(8,128)} %param.24) | copy-start | bytes 999940
  529.1 124.4 %copy-start.9 = (f32[651,128]{1,0:T(8,128)S(1)}, f32[651,128]{1,0:T(8,128)}, u32[]{:S(2)}) copy-start(f32[651,128]{1,0:T(8,128)} %param.23) | copy-start | bytes 999940
  649.6 3.0 collective-permute-start.4
Sparse Core Ops, SparseCore 0:
  10.9 123.8 all-gather.2

commit v2 on v1

--- a/solution.py
+++ b/solution.py
@@ -41,82 +41,6 @@
     fourth = third + FF * C // 128
     fifth = fourth + SMALL_ROWS
     return [first, second, third, fourth, fifth]
-
-
-def row_kind(row_ids):
-    kind = jnp.zeros(row_ids.shape, jnp.int32)
-    for boundary in row_edges():
-        kind = kind + (row_ids >= boundary).astype(jnp.int32)
-    return jnp.where(row_ids < 0, 6, kind)
-
-
-def row_rates(row_ids):
-    kind = row_kind(row_ids)
-    rates = [
-        2.0 / math.sqrt(C),
-        2.0 / math.sqrt(C // 8),
-        2.0 / math.sqrt(C),
-        2.0 / math.sqrt(FF),
-        1.0,
-        1.0,
-        0.0,
-    ]
-    decays = [DECAY, DECAY, DECAY, DECAY, 0.0, 0.0, 0.0]
-    rate_rows = jnp.zeros(row_ids.shape, jnp.float32)
-    decay_rows = jnp.zeros(row_ids.shape, jnp.float32)
-    for index, amount in enumerate(rates):
-        rate_rows = rate_rows + jnp.where(kind == index, amount, 0.0).astype(jnp.float32)
-        decay_rows = decay_rows + jnp.where(kind == index, decays[index], 0.0).astype(jnp.float32)
-    return (rate_rows, decay_rows)
-
-
-def slot_rows(owner_list, device_count, capacity):
-    hits = (owner_list[:, None] == jnp.arange(device_count, dtype=jnp.int32)[None, :]).astype(
-        jnp.int32
-    )
-    rank = jnp.sum(jnp.cumsum(hits, axis=0) * hits, axis=1) - 1
-    return owner_list * capacity + rank
-
-
-def slot_owner_rows(slots, slot_total):
-    return (
-        jnp.full((slot_total,), -1, jnp.int32)
-        .at[slots]
-        .set(jnp.arange(slots.shape[0], dtype=jnp.int32))
-    )
-
-
-def unpack(packed):
-    flat = packed.reshape(-1)
-    lengths = [C * 3 * C, C * C, C * FF, FF * C, 3 * C, C, FF, C, C, C, C, C]
-    pieces = []
-    start = 0
-    for length in lengths:
-        pieces.append(flat[start : start + length])
-        start = start + length
-    table_start = row_edges()[4] * 128
-    table = flat[table_start : table_start + (2 * WIN - 1) ** 2 * HEADS].reshape(
-        (2 * WIN - 1) ** 2, HEADS
-    )
-    matrices = (
-        pieces[0].reshape(C, 3 * C),
-        pieces[1].reshape(C, C),
-        pieces[2].reshape(C, FF),
-        pieces[3].reshape(FF, C),
-    )
-    return (matrices, pieces[4:12], table)
-
-
-def pack(matrices, smalls, table):
-    parts = [piece.reshape(-1) for piece in matrices] + [piece for piece in smalls]
-    small_pad = SMALL_ROWS * 128 - (9 * C + FF)
-    table_pad = TABLE_ROWS * 128 - (2 * WIN - 1) ** 2 * HEADS
-    parts = parts + [
-        jnp.zeros((small_pad,), jnp.float32),
-        table.reshape(-1),
-        jnp.zeros((table_pad,), jnp.float32),
-    ]
-    return jnp.concatenate(parts).reshape(-1, 128)
 
 
 GROUPS = 3
@@ -205,10 +129,11 @@
 
 def block_kernel(
     cols_ref, keep_ref, x_ref, xh_ref, dy_ref, dyh_ref, bias_ref,
+    wire_ref,
+    out_ref, outh_ref, gx_ref, gxh_ref, gwire_ref, gs_ref,
     wq_ref, wp_ref, wu_ref, wd_ref, bq_ref, bp_ref, bu_ref, bd_ref, g1_ref, b1_ref, g2_ref, b2_ref,
-    out_ref, outh_ref, gx_ref, gxh_ref,
     gwq_ref, gwp_ref, gwu_ref, gwdt_ref,
-    gbq_ref, gbp_ref, gbu_ref, gbd_ref, gg1_ref, gb1_ref, gg2_ref, gb2_ref, gs_ref,
+    gbq_ref, gbp_ref, gbu_ref, gbd_ref, gg1_ref, gb1_ref, gg2_ref, gb2_ref,
     line, xw, dyw, n1s, zs, qkv, prob, ctx, x1s, n2s, h2s, gfs, ys, gh2s, gctx, gqkv, resw, htr, gtr,
 ):
     step = pl.program_id(0)
@@ -220,13 +145,28 @@
     slabs = C // 128
     own = WIN - SHIFT
 
+    matrices = (wq_ref, wp_ref, wu_ref, wd_ref)
+    vectors = (bq_ref, bp_ref, bu_ref, bd_ref, g1_ref, b1_ref, g2_ref, b2_ref)
+    vector_grads = (gbq_ref, gbp_ref, gbu_ref, gbd_ref, gg1_ref, gb1_ref, gg2_ref, gb2_ref)
+
     @pl.when(step == 0)
     def _():
+        for ref, (first, slabs, rows) in zip(matrices, slab_plan()):
+            for j in range(slabs):
+                ref[:, j * 128 : j * 128 + 128] = wire_ref[first + j * rows : first + (j + 1) * rows, :]
+        small = jnp.zeros((SMALL_SPAN, 128), F32)
+        for i in range(3):
+            first = SMALL_START + i * SMALL_SPAN
+            small = small + wire_ref[first : first + SMALL_SPAN, :].astype(F32)
+        row = 0
+        for ref in vectors:
+            for j in range(ref.shape[1] // 128):
+                ref[:, j * 128 : j * 128 + 128] = small[row : row + 1]
+                row += 1
         line[...] = jnp.zeros_like(line)
         qkv[...] = jnp.zeros_like(qkv)
         gctx[...] = jnp.zeros_like(gctx)
-        for ref in (gwq_ref, gwp_ref, gwu_ref, gwdt_ref, gbq_ref, gbp_ref, gbu_ref, gbd_ref,
-                    gg1_ref, gb1_ref, gg2_ref, gb2_ref, gs_ref):
+        for ref in (gwq_ref, gwp_ref, gwu_ref, gwdt_ref, gs_ref) + vector_grads:
             ref[...] = jnp.zeros_like(ref)
 
     def to_windows(main, halo, target):
@@ -384,8 +324,21 @@
     resw[...] = x1s[...] + norm_pull(gz * g1_ref[...], n1s[...], scale_one)
     from_windows(resw, gx_ref, gxh_ref)
 
-
-def run_block(cols, keep, x, xh, dy, dyh, bias, weights, vectors):
+    @pl.when(step == pl.num_programs(0) - 1)
+    def _():
+        for grad, (first, slabs, rows) in zip((gwq_ref, gwp_ref, gwu_ref), slab_plan()):
+            for j in range(slabs):
+                gwire_ref[first + j * rows : first + (j + 1) * rows, :] = grad[:, j * 128 : j * 128 + 128].astype(BF16)
+        first, slabs, rows = slab_plan()[3]
+        for j in range(slabs):
+            gwire_ref[first + j * rows : first + (j + 1) * rows, :] = gwdt_ref[j * 128 : j * 128 + 128, :].T.astype(BF16)
+        pieces = [ref[:, j * 128 : j * 128 + 128] for ref in vector_grads for j in range(ref.shape[1] // 128)]
+        spare = gwire_ref.shape[0] - SMALL_START - len(pieces)
+        pieces.append(jnp.zeros((spare, 128), F32))
+        gwire_ref[SMALL_START:, :] = jnp.concatenate(pieces, axis=0).astype(BF16)
+
+
+def run_block(cols, keep, x, xh, dy, dyh, bias, wire):
     samples, rows, columns, _ = x.shape
     wide = columns // WIN
     tokens = wide * CELLS
@@ -399,16 +352,20 @@
     smem = pl.BlockSpec(memory_space=pltpu.SMEM)
     full = jax.ShapeDtypeStruct(x.shape, F32)
     part = jax.ShapeDtypeStruct(xh.shape, BF16)
-    grads = [(C, 3 * C), (C, C), (C, FF), (C, FF), (1, 3 * C), (1, C), (1, FF), (1, C),
-             (1, C), (1, C), (1, C), (1, C), (GROUPS, CELLS, GROUP_HEADS * LANES)]
+    sums = (GROUPS, CELLS, GROUP_HEADS * LANES)
+    vectors = [3 * C, C, FF, C, C, C, C, C]
     return pl.pallas_call(
         block_kernel,
         grid=(samples,),
         in_specs=[smem, smem, per_image(x), per_image(xh), per_image(dy), per_image(dyh), whole(bias.shape)]
-        + [whole(w.shape) for w in weights] + [whole(v.shape) for v in vectors],
-        out_specs=[per_image(x), per_image(xh), per_image(x), per_image(xh)] + [whole(s) for s in grads],
-        out_shape=[full, part, full, part] + [jax.ShapeDtypeStruct(s, F32) for s in grads],
-        scratch_shapes=[
+        + [whole(wire.shape)],
+        out_specs=[per_image(x), per_image(xh), per_image(x), per_image(xh), whole(wire.shape), whole(sums)],
+        out_shape=[full, part, full, part, jax.ShapeDtypeStruct(wire.shape, BF16), jax.ShapeDtypeStruct(sums, F32)],
+        scratch_shapes=[pltpu.VMEM(s, BF16) for s in ((C, 3 * C), (C, C), (C, FF), (FF, C))]
+        + [pltpu.VMEM((1, size), F32) for size in vectors]
+        + [pltpu.VMEM(s, F32) for s in ((C, 3 * C), (C, C), (C, FF), (C, FF))]
+        + [pltpu.VMEM((1, size), F32) for size in vectors]
+        + [
             pltpu.VMEM((C // 128, WIN, columns + 8, 128), F32),
             pltpu.VMEM((tokens, C), F32),
             pltpu.VMEM((tokens, C), F32),
@@ -431,56 +388,350 @@
         ],
         compiler_params=pltpu.CompilerParams(vmem_limit_bytes=58 * 1024 * 1024),
         name="block",
-    )(cols, keep, x, xh, dy, dyh, bias, *weights, *vectors)
-
-
-def adamw(weights, first, second, grads, row_ids):
-    rate_rows, decay_rows = row_rates(row_ids)
-    first = BETA_ONE * first + (1.0 - BETA_ONE) * grads
-    second = BETA_TWO * second + (1.0 - BETA_TWO) * grads * grads
+    )(cols, keep, x, xh, dy, dyh, bias, wire)
+
+
+SMALL_START = 3 * C * C // 128 + C * C // 128 + 2 * C * FF // 128
+SMALL_SPAN = 64
+WIRE_ROWS = SMALL_START + 3 * SMALL_SPAN
+
+
+def slab_plan():
+    return [
+        (0, 3 * C // 128, C),
+        (3 * C * C // 128, C // 128, C),
+        (4 * C * C // 128, FF // 128, C),
+        (4 * C * C // 128 + C * FF // 128, C // 128, FF),
+    ]
+
+
+def wire_rows(device_count):
+    unit = 2 * device_count * 16
+    return -(-WIRE_ROWS // unit) * unit
+
+
+def split_three(values):
+    high = values.astype(BF16)
+    rest = values - high.astype(F32)
+    middle = rest.astype(BF16)
+    return high, middle, (rest - middle.astype(F32)).astype(BF16)
+
+
+def dispatch_kernel(me_ref, owner_ref, master_ref, out_ref, rank_ref, start_ref, padded, packed, start_s, sem):
+    blocks = owner_ref.shape[0]
+    capacity = master_ref.shape[0]
+    mine = (owner_ref[...] == me_ref[0]).astype(F32)
+    low = mine.astype(BF16)
+    row = lax.broadcasted_iota(jnp.int32, (128, 128), 0)
+    col = lax.broadcasted_iota(jnp.int32, (128, 128), 1)
+    within = nn(low, (row <= col).astype(F32).astype(BF16))
+    sums = nn(low, jnp.ones((128, 128), BF16))
+    below = lax.broadcasted_iota(jnp.int32, (blocks, blocks), 1) < lax.broadcasted_iota(jnp.int32, (blocks, blocks), 0)
+    start = nn(below.astype(F32).astype(BF16), sums.astype(BF16))
+    rank_ref[...] = jnp.where(mine > 0, within - 1.0, -1.0)
+    start_ref[...] = start.astype(jnp.int32)
+    copy = pltpu.make_async_copy(start_ref, start_s, sem)
+    copy.start()
+    padded[...] = jnp.zeros_like(padded)
+    padded[0:capacity, :] = master_ref[...]
+    out_ref[...] = jnp.zeros_like(out_ref)
+    copy.wait()
+    slot = row.astype(F32)
+
+    def block(b, _):
+        hot = (slot == rank_ref[pl.ds(b, 1), :]).astype(F32).astype(BF16)
+        rows = padded[pl.ds(start_s[b, 0], 128), :].astype(BF16)
+        packed[pl.ds(pl.multiple_of(b * 128, 128), 128), :] = tn(hot, rows)
+        return 0
+
+    small = SMALL_START // 128
+    lax.fori_loop(0, small, block, 0, unroll=4)
+    hot = (slot == rank_ref[small : small + 1, :]).astype(F32).astype(BF16)
+    for i, piece in enumerate(split_three(padded[pl.ds(start_s[small, 0], 128), :])):
+        first = SMALL_START + i * SMALL_SPAN
+        out_ref[first : first + SMALL_SPAN, :] = tn(hot, piece)[0:SMALL_SPAN].astype(BF16)
+    for first, slabs, rows in slab_plan():
+        for j in range(slabs):
+            out_ref[first + j * rows : first + (j + 1) * rows, :] = packed[
+                pl.ds(first + j, rows, stride=slabs), :
+            ].astype(BF16)
+
+
+def run_dispatch(me, owners, master, wire):
+    blocks = owners.shape[0]
+    vmem = pl.BlockSpec(memory_space=pltpu.VMEM)
+    return pl.pallas_call(
+        dispatch_kernel,
+        in_specs=[pl.BlockSpec(memory_space=pltpu.SMEM), vmem, vmem],
+        out_specs=[vmem] * 3,
+        out_shape=[
+            jax.ShapeDtypeStruct((wire, 128), BF16),
+            jax.ShapeDtypeStruct((blocks, 128), F32),
+            jax.ShapeDtypeStruct((blocks, 128), jnp.int32),
+        ],
+        scratch_shapes=[
+            pltpu.VMEM((-(-(master.shape[0] + 128) // 8) * 8, 128), F32),
+            pltpu.VMEM((SMALL_START, 128), F32),
+            pltpu.SMEM((blocks, 128), jnp.int32),
+            pltpu.SemaphoreType.DMA,
+        ],
+        compiler_params=pltpu.CompilerParams(vmem_limit_bytes=40 * 1024 * 1024),
+        name="dispatch",
+    )(me, owners, master)
+
+
+def collect_kernel(start_ref, rank_ref, grad_ref, master_ref, first_ref, second_ref,
+                   first_out, second_out, master_out, packed, total):
+    capacity = master_ref.shape[0]
+    total[...] = jnp.zeros_like(total)
+    for first, slabs, rows in slab_plan():
+        for j in range(slabs):
+            packed[pl.ds(first + j, rows, stride=slabs), :] = grad_ref[
+                first + j * rows : first + (j + 1) * rows, :
+            ].astype(F32)
+    packed[SMALL_START : SMALL_START + SMALL_SPAN, :] = grad_ref[SMALL_START : SMALL_START + SMALL_SPAN, :].astype(F32)
+    packed[SMALL_START + SMALL_SPAN : SMALL_START + 128, :] = jnp.zeros((128 - SMALL_SPAN, 128), F32)
+    slot = lax.broadcasted_iota(jnp.int32, (128, 128), 0).astype(F32)
+
+    def block(b, _):
+        hot = (slot == rank_ref[pl.ds(b, 1), :]).astype(F32).astype(BF16)
+        part = nn(hot, packed[pl.ds(pl.multiple_of(b * 128, 128), 128), :].astype(BF16))
+        where = pl.ds(start_ref[b, 0], 128)
+        total[where, :] = total[where, :] + part
+        return 0
+
+    lax.fori_loop(0, SMALL_START // 128 + 1, block, 0)
+    slots = lax.broadcasted_iota(jnp.int32, (capacity, 1), 0)
+    edges = [edge // 128 for edge in row_edges()[:4]] + [SMALL_START // 128 + 1]
+    rates = [2.0 / math.sqrt(C), 2.0 / math.sqrt(C // 8), 2.0 / math.sqrt(C), 2.0 / math.sqrt(FF), 1.0, 0.0]
+    rate = jnp.full((capacity, 1), rates[0], F32)
+    for edge, amount in zip(edges, rates[1:]):
+        rate = jnp.where(slots >= start_ref[edge, 0], amount, rate)
+    decay = jnp.where(slots < start_ref[edges[3], 0], DECAY, 0.0)
+    grads = total[0:capacity, :]
+    weights = master_ref[...]
+    first = BETA_ONE * first_ref[...] + (1.0 - BETA_ONE) * grads
+    second = BETA_TWO * second_ref[...] + (1.0 - BETA_TWO) * grads * grads
+    first_out[...] = first
+    second_out[...] = second
     first_hat = first / (1.0 - BETA_ONE**STEP)
     second_hat = second / (1.0 - BETA_TWO**STEP)
-    weights = weights - rate_rows[:, None] * (
-        first_hat / (jnp.sqrt(second_hat) + ADAM_EPS) + decay_rows[:, None] * weights
-    )
-    return (first, second, weights)
+    master_out[...] = weights - rate * (first_hat / (jnp.sqrt(second_hat) + ADAM_EPS) + decay * weights)
+
+
+def run_collect(starts, ranks, grads, master, first, second):
+    vmem = pl.BlockSpec(memory_space=pltpu.VMEM)
+    return pl.pallas_call(
+        collect_kernel,
+        in_specs=[pl.BlockSpec(memory_space=pltpu.SMEM)] + [vmem] * 5,
+        out_specs=[vmem] * 3,
+        out_shape=[jax.ShapeDtypeStruct(master.shape, F32)] * 3,
+        scratch_shapes=[
+            pltpu.VMEM((SMALL_START + 128, 128), F32),
+            pltpu.VMEM((-(-(master.shape[0] + 128) // 8) * 8, 128), F32),
+        ],
+        compiler_params=pltpu.CompilerParams(vmem_limit_bytes=40 * 1024 * 1024),
+        name="collect",
+    )(starts, ranks, grads, master, first, second)
+
+
+def all_reduce_kernel(strips, buckets, in_ref, out_ref, core_in, core_sum, in_one, sum_one, in_two, sum_two,
+                      in_three, send_sems, recv_sems):
+    strip, bucket = lax.axis_index("strip"), lax.axis_index("bucket")
+    sizes = {"z": strips // 2, "y": 2, "x": buckets // 2, "core": 2}
+    mine = {"z": strip // 2, "y": strip % 2, "x": bucket // 2, "core": bucket % 2}
+
+    def device(axis, index):
+        place = dict(mine)
+        place[axis] = index
+        return (place["z"] * 2 + place["y"], place["x"] * 2 + place["core"])
+
+    def peer(axis, offset):
+        return lax.rem(mine[axis] + offset, sizes[axis])
+
+    barrier = pltpu.get_barrier_semaphore()
+    greeted = 0
+    for axis, size in sizes.items():
+        for offset in range(1, size):
+            pl.semaphore_signal(barrier, inc=1, device_id=device(axis, peer(axis, offset)),
+                                device_id_type=pl.DeviceIdType.MESH)
+            greeted += 1
+    pl.semaphore_wait(barrier, greeted)
+
+    used = [0]
+
+    def send(source, target, axis, offset):
+        at = used[0]
+        used[0] += 1
+        copy = pltpu.make_async_remote_copy(
+            src_ref=source, dst_ref=target, send_sem=send_sems.at[at], recv_sem=recv_sems.at[at],
+            device_id=device(axis, peer(axis, offset)), device_id_type=pl.DeviceIdType.MESH,
+        )
+        copy.start()
+        return copy
+
+    rows = in_ref.shape[0]
+    quarter = rows // 4
+    orders = [("x", "y"), ("y", "x")]
+    started = []
+
+    def at(start, length):
+        return pl.ds(pl.multiple_of(start, 16), length)
+
+    flight = []
+    for p in range(2):
+        other = (1 - mine["core"]) * 2 * quarter + p * quarter
+        flight.append(send(in_ref.at[at(other, quarter)], core_in.at[p], "core", 1))
+    stage = []
+    for p in range(2):
+        flight[p].wait()
+        own = mine["core"] * 2 * quarter + p * quarter
+        core_sum[p] = in_ref[at(own, quarter), :] + core_in[p]
+        stage.append(core_sum.at[p])
+
+    def scatter(level, length, axis_of, inboxes, sums):
+        flights = []
+        for p in range(2):
+            axis = axis_of(p)
+            piece = length // sizes[axis]
+            group = []
+            for offset in range(1, sizes[axis]):
+                source = stage[p].at[at(peer(axis, offset) * piece, piece)]
+                group.append(send(source, inboxes.at[p, pl.ds((offset - 1) * piece, piece)], axis, offset))
+            flights.append(group)
+        for p in range(2):
+            axis = axis_of(p)
+            piece = length // sizes[axis]
+            for copy in flights[p]:
+                copy.wait()
+            value = stage[p][at(mine[axis] * piece, piece), :].astype(F32)
+            for offset in range(1, sizes[axis]):
+                value = value + inboxes[p, (offset - 1) * piece : offset * piece, :].astype(F32)
+            if sums is None:
+                base = mine["core"] * 2 * quarter + p * quarter + spans(p)[-1][0]
+                out_ref[at(base, piece), :] = value.astype(BF16)
+            else:
+                sums[p, 0:piece, :] = value.astype(BF16)
+                stage[p] = sums.at[p]
+
+    def spans(p):
+        result = []
+        start, length = 0, quarter
+        for axis in orders[p] + ("z",):
+            length = length // sizes[axis]
+            start = start + mine[axis] * length
+            result.append((start, length))
+        return result
+
+    scatter(1, quarter, lambda p: orders[p][0], in_one, sum_one)
+    lengths = [quarter // sizes[orders[p][0]] for p in range(2)]
+
+    def scatter_two():
+        flights = []
+        for p in range(2):
+            axis = orders[p][1]
+            piece = lengths[p] // sizes[axis]
+            group = []
+            for offset in range(1, sizes[axis]):
+                source = stage[p].at[at(peer(axis, offset) * piece, piece)]
+                group.append(send(source, in_two.at[p, pl.ds((offset - 1) * piece, piece)], axis, offset))
+            flights.append(group)
+        for p in range(2):
+            axis = orders[p][1]
+            piece = lengths[p] // sizes[axis]
+            for copy in flights[p]:
+                copy.wait()
+            value = stage[p][at(mine[axis] * piece, piece), :].astype(F32)
+            for offset in range(1, sizes[axis]):
+                value = value + in_two[p, (offset - 1) * piece : offset * piece, :].astype(F32)
+            sum_two[p, 0:piece, :] = value.astype(BF16)
+            stage[p] = sum_two.at[p]
+
+    scatter_two()
+    eighth = quarter // (sizes["x"] * sizes["y"])
+    scatter(3, eighth, lambda p: "z", in_three, None)
+
+    for level in (2, 1, 0):
+        flights = []
+        for p in range(2):
+            axis = (orders[p] + ("z",))[level]
+            start, length = spans(p)[level]
+            region = out_ref.at[at(mine["core"] * 2 * quarter + p * quarter + start, length)]
+            flights.append([send(region, region, axis, offset) for offset in range(1, sizes[axis])])
+        for group in flights:
+            for copy in group:
+                copy.wait()
+    flights = []
+    for p in range(2):
+        region = out_ref.at[at(mine["core"] * 2 * quarter + p * quarter, quarter)]
+        flights.append(send(region, region, "core", 1))
+    for copy in flights:
+        copy.wait()
+
+
+def all_reduce(values, strips, buckets):
+    rows = values.shape[0]
+    quarter = rows // 4
+    x, y, z = buckets // 2, 2, strips // 2
+    vmem = pl.BlockSpec(memory_space=pltpu.VMEM)
+    copies = 2 * (2 * 1 + 2 * (x - 1 + y - 1 + z - 1))
+    small = min(x, y)
+    return pl.pallas_call(
+        lambda *refs: all_reduce_kernel(strips, buckets, *refs),
+        in_specs=[vmem],
+        out_specs=vmem,
+        out_shape=jax.ShapeDtypeStruct(values.shape, BF16),
+        scratch_shapes=[
+            pltpu.VMEM((2, quarter, 128), BF16),
+            pltpu.VMEM((2, quarter, 128), BF16),
+            pltpu.VMEM((2, quarter, 128), BF16),
+            pltpu.VMEM((2, quarter // small, 128), BF16),
+            pltpu.VMEM((2, quarter // small, 128), BF16),
+            pltpu.VMEM((2, quarter // (x * y), 128), BF16),
+            pltpu.VMEM((2, quarter // (x * y), 128), BF16),
+            pltpu.SemaphoreType.DMA((copies,)),
+            pltpu.SemaphoreType.DMA((copies,)),
+        ],
+        compiler_params=pltpu.CompilerParams(
+            vmem_limit_bytes=40 * 1024 * 1024, collective_id=0, has_side_effects=True
+        ),
+        name="all_reduce",
+    )(values)
 
 
 def shards(
     block_input, cotangent, window_cols, keep_mask, owner_list, master, first_moment, second_moment
 ):
     strips = lax.axis_size("strip")
-    device_count = strips * lax.axis_size("bucket")
-    capacity = master.shape[0]
+    buckets = lax.axis_size("bucket")
+    wire_total = wire_rows(strips * buckets)
     x_halo = from_behind(block_input[:, :SHIFT].astype(BF16), "strip", -1)
     dy_halo = from_behind(cotangent[:, :SHIFT].astype(BF16), "strip", -1)
-    slots = slot_rows(owner_list, device_count, capacity)
-    sources = slot_owner_rows(slots, device_count * capacity)
-    gathered = lax.all_gather(master, ("strip", "bucket"), axis=0, tiled=True)
-    matrices, smalls, table = unpack(gathered[slots])
-    weights = [matrix.astype(BF16) for matrix in matrices]
-    vectors = [small.reshape(1, -1) for small in smalls]
+    my_index = lax.axis_index(("strip", "bucket")).astype(jnp.int32).reshape(1)
+    blocks = -(-(SMALL_START // 128 + 2) // 8) * 8
+    owners = jnp.pad(owner_list, (0, blocks * 128 - owner_list.shape[0]), constant_values=-1).reshape(blocks, 128)
+    sparse, ranks, starts = run_dispatch(my_index, owners, master, wire_total)
+    wire = all_reduce(sparse, strips, buckets)
+    small = [wire[SMALL_START + i * SMALL_SPAN : SMALL_START + (i + 1) * SMALL_SPAN].astype(F32) for i in range(3)]
+    pairs = (2 * WIN - 1) ** 2
+    table = (small[0] + small[1] + small[2])[SMALL_ROWS : SMALL_ROWS + TABLE_ROWS].reshape(-1)
+    table = table[: pairs * HEADS].reshape(pairs, HEADS)
     bias = attention_bias(table, lax.axis_index("strip") == strips - 1)
     keep = keep_mask.astype(F32) / KEEP_PROB
-    results = run_block(
-        window_cols, keep, block_input, x_halo, cotangent, dy_halo, bias, weights, vectors
+    output, output_halo, grad_input, grad_halo, grad_wire, pair_sums = run_block(
+        window_cols, keep, block_input, x_halo, cotangent, dy_halo, bias, wire
     )
-    output, output_halo, grad_input, grad_halo = results[:4]
-    gwq, gwp, gwu, gwdt = results[4:8]
-    smalls_grad = [small.reshape(-1) for small in results[8:16]]
-    pair_sums = results[16].reshape(GROUPS, CELLS, GROUP_HEADS, LANES).transpose(0, 2, 1, 3)
+    pair_sums = pair_sums.reshape(GROUPS, CELLS, GROUP_HEADS, LANES).transpose(0, 2, 1, 3)
     grad_table = lax.dot_general(
         pair_onehot(), pair_sums.reshape(HEADS, -1), (((0,), (1,)), ((), ())),
         precision=PRECISE, preferred_element_type=F32,
-    )
+    ).reshape(-1)
+    grad_table = jnp.pad(grad_table, (0, TABLE_ROWS * 128 - pairs * HEADS)).reshape(TABLE_ROWS, 128)
+    grad_wire = lax.dynamic_update_slice(grad_wire, grad_table.astype(BF16), (SMALL_START + SMALL_ROWS, 0))
     output = output.at[:, :SHIFT].set(from_behind(output_halo, "strip", 1).astype(F32))
     grad_input = grad_input.at[:, :SHIFT].set(from_behind(grad_halo, "strip", 1).astype(F32))
-    packed_grad = pack([gwq, gwp, gwu, gwdt.T], smalls_grad, grad_table)
-    my_index = lax.axis_index(("strip", "bucket"))
-    my_sources = lax.dynamic_slice_in_dim(sources, my_index * capacity, capacity)
-    spread_out = jnp.where((sources >= 0)[:, None], packed_grad[jnp.maximum(sources, 0)], 0.0)
-    grads = lax.psum_scatter(spread_out, ("strip", "bucket"), scatter_dimension=0, tiled=True)
-    first, second_new, new_weights = adamw(master, first_moment, second_moment, grads, my_sources)
+    grads = all_reduce(grad_wire, strips, buckets)
+    first, second_new, new_weights = run_collect(starts, ranks, grads, master, first_moment, second_moment)
     return (output, grad_input, first, second_new, new_weights)
 
 

time: 675 us -> 445 us (0.66)
  local copies, waits for them, and re-layouts: 247 us -> 15.1 us
  Pallas kernels: 193 us -> 408 us
  blocking collectives: 121 us -> 0 us
  other arithmetic: 51.6 us -> 4.34 us
  waiting for transfers between devices: 23.7 us -> 0.01 us
  between operations: 15 us -> 1.52 us
    pallas_call x0 -> x4, Pallas kernels: none -> 214 us  [the longest x2 186 us: all_reduce(): pl.pallas_call(lambda *refs: all_reduce_kernel(strips, buckets, *refs), i...]
    unnamed x1 -> x0, blocking collectives: 121 us -> none
    gather x2 -> x0, local copies, waits for them, and re-layouts: 72.8 us -> none  [the longest x1 42.2 us: shards(): packed_grad[jnp.maximum(sources, 0)]]
    scatter x1 -> x0, local copies, waits for them, and re-layouts: 65.2 us -> none  [slot_owner_rows(): return jnp.full((slot_total,), -1, jnp.int32).at[slots].set(jnp.arange(sl...]
    concatenate x1 -> x0, local copies, waits for them, and re-layouts: 60.7 us -> none  [pack(): return jnp.concatenate(parts).reshape(-1, 128)]
    all_gather x1 -> x0, waiting for transfers between devices: 22.9 us -> none  [shards(): gathered = lax.all_gather(master, ('strip', 'bucket'), axis=0, tiled=True)]
    another operation x5 -> x0, other arithmetic: 22.7 us -> none
    select_n x2 -> x0, other arithmetic: 12.8 us -> none  [the longest x1 12.8 us: shards(): jnp.where((sources >= 0)[:, None], packed_grad[jnp.maximum(sources, 0)],...]
  transfers between devices with their start and end apart: 6 -> 4, of which waited for: 2 -> 0; matrix products, arithmetic and copies ran while one was open for 62% -> 3% of each run, Pallas kernels for 0% -> 48%
where the time goes in v2:
time: 445 us; the launch traced here: 443 us
  Pallas kernels  408 us (92%)
  local copies, waits for them, and re-layouts  15.1 us (3%)
  starting transfers between devices  9.82 us (2%)
    pallas_call x1, Pallas kernels, run_block(): pl.pallas_call(block_kernel, grid=(samples,), in_specs=[smem, smem, per_i...  194 us
    pallas_call x2, Pallas kernels, all_reduce(): pl.pallas_call(lambda *refs: all_reduce_kernel(strips, buckets, *refs), i...  186 us
    pallas_call x1, Pallas kernels, run_collect(): pl.pallas_call(collect_kernel, in_specs=[pl.BlockSpec(memory_space=pltpu....  18.8 us
    ppermute x4, starting transfers between devices, from_behind(): lax.ppermute(value, axis, [(i, (i + by) % peers) for i in range(peers)])  9.82 us
  transfers between devices with their start and end apart: 4, of which 0 were waited for; matrix products, arithmetic and copies ran while one was open for 3% of the time, Pallas kernels for 48%

profile of v2, /device:TPU:0, one launch (start us, length us, event | category | flops | bytes accessed | tf_op | source)
XLA Modules:
  0.0 442.6 jit_solution(502897671778914365)
XLA Ops:
  0.7 2.7 slice.95
  3.4 6.0 %collective-permute-start.1 = (bf16[8,3,56,384]{3,2,1,0:T(8,128)(2,1)}, bf16[8,3,56,384]{3,2,1,0:T(8,128)(2,1)S(1)}, u32[]{:S(2)}, u32[]{:S(2)}) collective-permute-start(bf16[8,3,56,384]{3,2,1,0:T(8,128)(2,1)} %slice.95), channel_id=1, source_target_pairs={{0,28},{4,0},{8,4},{12,8},{16,12},{20,16},{24,20},{28,24},{1,29},{... | collective-permute-start | bytes 3096584 | tf_op jit(solution)/shard_map/ppermute | solution.py:34
  9.4 2.7 slice.96
  12.0 0.5 collective-permute-start
  13.2 0.1 copy.23
  13.3 8.4 %dispatch.1 = (bf16[14336,128]{1,0:T(8,128)(2,1)S(1)}, f32[112,128]{1,0:T(8,128)S(1)}, s32[112,128]{1,0:T(8,128)S(1)}) custom-call(s32[1]{0:T(128)} %bitcast.me_ref, s32[112,128]{1,0:T(8,128)S(1)} %pad_bitcast_fusion.owner_ref, f32[651,128]{1,0:T(8,128)S(1)} %copy-done.2), custom_call_target="tpu_custom_call" | custom-call | tf_op jit(solution)/shard_map/dispatch/pallas_call | solution.py:463
  21.7 0.0 copy-start.8
  21.8 90.6 %all_reduce.2.wire_ref = bf16[14336,128]{1,0:T(8,128)(2,1)S(1)} custom-call(bf16[14336,128]{1,0:T(8,128)(2,1)S(1)} %get-tuple-element.41.refs_0_), custom_call_target="tpu_custom_call" | custom-call | tf_op jit(solution)/shard_map/all_reduce/pallas_call | solution.py:679
  112.4 1.8 copy-done
  114.3 0.2 add.48
  114.5 0.1 reshape.162
  114.6 0.1 copy.24
  114.7 2.6 fusion.6
  117.3 0.2 add.45
  117.5 0.6 convert_multiply_fusion.keep_ref
  118.1 0.8 multiply_select_fusion.bias_ref
  119.0 1.0 copy-done.5
  119.9 1.0 copy-done.6
  120.9 194.3 %block.1 = (f32[8,7,56,384]{3,2,1,0:T(8,128)}, bf16[8,3,56,384]{3,2,1,0:T(8,128)(2,1)}, f32[8,7,56,384]{3,2,1,0:T(8,128)}, bf16[8,3,56,384]{3,2,1,0:T(8,128)(2,1...) custom-call(s32[1]{0:T(128)S(6)} %copy.33.cols_ref, f32[8,2]{1,0:T(8,128)} %convert_multiply_fusion.keep_ref, ...), custom_call_target="tpu_custom_call" | custom-call | tf_op jit(solution)/shard_map/block/pallas_call | solution.py:357
  315.3 0.7 collective-permute-start.2
  316.0 2.6 collective-permute-start.3
  318.6 1.1 reshape.163
  319.7 0.1 reshape.164
  319.9 1.2 fusion.9
  321.1 0.1 copy.26
  321.2 0.1 reshape.165
  321.4 1.6 dynamic_update_slice.3.refs_0_
  323.0 2.0 copy-done.1
  325.0 95.8 %all_reduce.3.grad_ref = bf16[14336,128]{1,0:T(8,128)(2,1)S(1)} custom-call(bf16[14336,128]{1,0:T(8,128)(2,1)S(1)} %copy-done.1), custom_call_target="tpu_custom_call" | custom-call | tf_op jit(solution)/shard_map/all_reduce/pallas_call | solution.py:679
  420.9 18.8 %collect.1 = (f32[651,128]{1,0:T(8,128)}, f32[651,128]{1,0:T(8,128)}, f32[651,128]{1,0:T(8,128)}) custom-call(s32[112,128]{1,0:T(8,128)S(1)} %get-tuple-element.46.start_ref, f32[112,128]{1,0:T(8,128)S(1)} %get-tuple-element.47.rank_ref, bf16[14336,128]{1,0:T(8,128)(2,1)S(1)} %all_reduce.3.grad_ref, f32[651,128]{1,0:T(8,128)S(1)} %copy-done.2, ...), custom_call_target="tpu_custom_call" | custom-call | tf_op jit(solution)/shard_map/collect/pallas_call | solution.py:524
  439.7 1.4 convert_dynamic-update-slice_fusion.1
  441.1 1.4 convert_dynamic-update-slice_fusion
  (36 shorter events, 0.2 us)
Async XLA Ops:
  0.6 12.6 %copy-start.10 = (s32[8,2]{0,1:T(2,128)S(1)}, s32[8,2]{0,1:T(2,128)}, u32[]{:S(2)}) copy-start(s32[8,2]{0,1:T(2,128)} %param.20) | copy-start | bytes 196
  0.6 12.6 %copy-start.7 = (s32[13879]{0:T(1024)S(1)}, s32[13879]{0:T(1024)}, u32[]{:S(2)}) copy-start(s32[13879]{0:T(1024)} %param.21) | copy-start | bytes 166552
  0.7 12.6 %copy-start.2 = (f32[651,128]{1,0:T(8,128)S(1)}, f32[651,128]{1,0:T(8,128)}, u32[]{:S(2)}) copy-start(f32[651,128]{1,0:T(8,128)} %master_ref.3) | copy-start | bytes 999940
  3.4 115.6 %collective-permute-start.1 = (bf16[8,3,56,384]{3,2,1,0:T(8,128)(2,1)}, bf16[8,3,56,384]{3,2,1,0:T(8,128)(2,1)S(1)}, u32[]{:S(2)}, u32[]{:S(2)}) collective-permute-start(bf16[8,3,56,384]{3,2,1,0:T(8,128)(2,1)} %slice.95), channel_id=1, source_target_pairs={{0,28},{4,0},{8,4},{12,8},{16,12},{20,16},{24,20},{28,24},{1,29},{... | collective-permute-start | bytes 3096584 | tf_op jit(solution)/shard_map/ppermute | solution.py:34
  12.0 107.0 %collective-permute-start = (bf16[8,3,56,384]{3,2,1,0:T(8,128)(2,1)}, bf16[8,3,56,384]{3,2,1,0:T(8,128)(2,1)S(1)}, u32[]{:S(2)}, u32[]{:S(2)}) collective-permute-start(bf16[8,3,56,384]{3,2,1,0:T(8,128)(2,1)} %slice.96), channel_id=1, source_target_pairs={{0,28},{4,0},{8,4},{12,8},{16,12},{20,16},{24,20},{28,24},{1,29},{... | collective-permute-start | bytes 3096584 | tf_op jit(solution)/shard_map/ppermute | solution.py:34
  21.7 92.5 %copy-start.8 = (pred[56,64]{1,0:T(8,128)(4,1)S(1)}, pred[56,64]{1,0:T(8,128)(4,1)}, u32[]{:S(2)}) copy-start(pred[56,64]{1,0:T(8,128)(4,1)} %constant.89.clone) | copy-start | bytes 10756
  21.8 92.5 %copy-start.9 = (pred[56,64]{1,0:T(8,128)(4,1)S(1)}, pred[56,64]{1,0:T(8,128)(4,1)}, u32[]{:S(2)}) copy-start(pred[56,64]{1,0:T(8,128)(4,1)} %constant.88.clone) | copy-start | bytes 10756
  21.8 93.0 %copy-start.12 = (s32[56,64]{1,0:T(8,128)S(1)}, s32[56,64]{1,0:T(8,128)}, u32[]{:S(2)}) copy-start(s32[56,64]{1,0:T(8,128)} %constant.101) | copy-start | bytes 43012
  21.8 96.4 %copy-start.11 = (pred[56]{0:T(512)(128)(4,1)S(1)}, pred[56]{0:T(512)(128)(4,1)}, u32[]{:S(2)}) copy-start(pred[56]{0:T(512)(128)(4,1)} %constant.90.clone) | copy-start | bytes 172
  112.4 1.8 copy-start
  119.0 200.9 %copy-start.13 = (s32[3584]{0:T(1024)S(1)}, s32[3584]{0:T(1024)}, u32[]{:S(2)}) copy-start(s32[3584]{0:T(1024)} %constant.87.clone) | copy-start | bytes 43012
  119.0 1.0 copy-start.5
  119.9 1.0 copy-start.6
  315.3 124.4 %collective-permute-start.2 = (bf16[8,3,56,384]{3,2,1,0:T(8,128)(2,1)}, bf16[8,3,56,384]{3,2,1,0:T(8,128)(2,1)S(1)}, u32[]{:S(2)}, u32[]{:S(2)}) collective-permute-start(bf16[8,3,56,384]{3,2,1,0:T(8,128)(2,1)} %get-tuple-element.43), channel_id=1, source_target_pairs={{0,4},{4,8},{8,12},{12,16},{16,20},{20,24},{24,28},{28,0},{1,5},{5... | collective-permute-start | bytes 3096584 | tf_op jit(solution)/shard_map/ppermute | solution.py:34
  316.0 125.1 %collective-permute-start.3 = (bf16[8,3,56,384]{3,2,1,0:T(8,128)(2,1)}, bf16[8,3,56,384]{3,2,1,0:T(8,128)(2,1)S(1)}, u32[]{:S(2)}, u32[]{:S(2)}) collective-permute-start(bf16[8,3,56,384]{3,2,1,0:T(8,128)(2,1)} %get-tuple-element.45), channel_id=1, source_target_pairs={{0,4},{4,8},{8,12},{12,16},{16,20},{20,24},{24,28},{28,0},{1,5},{5... | collective-permute-start | bytes 3096584 | tf_op jit(solution)/shard_map/ppermute | solution.py:34
  323.0 2.0 copy-start.1
  325.0 95.9 %copy-start.3 = (f32[651,128]{1,0:T(8,128)S(1)}, f32[651,128]{1,0:T(8,128)}, u32[]{:S(2)}) copy-start(f32[651,128]{1,0:T(8,128)} %first_ref.1) | copy-start | bytes 999940
  325.0 95.9 %copy-start.4 = (f32[651,128]{1,0:T(8,128)S(1)}, f32[651,128]{1,0:T(8,128)}, u32[]{:S(2)}) copy-start(f32[651,128]{1,0:T(8,128)} %second_ref.1) | copy-start | bytes 999940

commit v3 on v2

--- a/solution.py
+++ b/solution.py
@@ -99,15 +99,8 @@
 
 
 def gelu_pair(u):
-    x = jnp.abs(u) * (0.3275911 / math.sqrt(2.0)) + 1.0
-    t = pl.reciprocal(x)
+    normal = 0.5 + 0.5 * lax.erf(u * math.sqrt(0.5))
     gauss = jnp.exp2(u * u * (-0.5 * LOG2E))
-    poly = t * (0.5 * 1.061405429) - 0.5 * 1.453152027
-    poly = poly * t + 0.5 * 1.421413741
-    poly = poly * t - 0.5 * 0.284496736
-    poly = poly * t + 0.5 * 0.254829592
-    tail = poly * t * gauss
-    normal = jnp.where(u >= 0, 1.0 - tail, tail)
     return u * normal, normal + u * gauss * (1.0 / math.sqrt(2.0 * math.pi))
 
 
@@ -242,7 +235,7 @@
             ctx[rows, g * 128 : g * 128 + 128] = unstack(tn(a.astype(BF16), v))
         return 0
 
-    lax.fori_loop(0, wide, attend, 0)
+    lax.fori_loop(0, wide, attend, 0, unroll=True)
 
     ctx_low = ctx[...].astype(BF16)
     x1 = xw[...] + keep_one * (nn(ctx_low, wp_ref[...]) + bp_ref[...])
@@ -279,7 +272,7 @@
         gh2s[...] += nt(gu, wu_ref[:, part])
         return 0
 
-    lax.fori_loop(0, FF // chunk, feed, 0)
+    lax.fori_loop(0, FF // chunk, feed, 0, unroll=True)
 
     resw[...] = (x1s[...] + keep_two * (ys[...] + bd_ref[...])) * valid
     from_windows(resw, out_ref, outh_ref)
@@ -296,24 +289,31 @@
     for w in range(wide):
         gctx[w, 0:CELLS, :] = gc[w * CELLS : w * CELLS + CELLS].astype(BF16)
 
-    def pull(w, _):
+    def pull_scores(w, _):
         rows = pl.ds(pl.multiple_of(w * CELLS, 8), CELLS)
         for g in range(GROUPS):
-            q = qkv[w, :, g * 128 : g * 128 + 128]
-            k = qkv[w, 0:CELLS, C + g * 128 : C + g * 128 + 128]
             v = qkv[w, 0:CELLS, 2 * C + g * 128 : 2 * C + g * 128 + 128]
             gstack = stack_of(gctx[w, :, g * 128 : g * 128 + 128])
             a = prob[w, g]
             grad = nt(v, gstack)
             inner = jnp.sum(grad * a, axis=0, keepdims=True)
-            gs = (a * (grad - inner)).astype(BF16)
-            gs_ref[g] += gs.astype(F32)
+            prob[w, g] = a * (grad - inner)
+            gqkv[rows, 2 * C + g * 128 : 2 * C + g * 128 + 128] = nn(a.astype(BF16), gstack)
+        return 0
+
+    def pull_pairs(w, _):
+        rows = pl.ds(pl.multiple_of(w * CELLS, 8), CELLS)
+        for g in range(GROUPS):
+            q = qkv[w, :, g * 128 : g * 128 + 128]
+            k = qkv[w, 0:CELLS, C + g * 128 : C + g * 128 + 128]
+            gs = prob[w, g].astype(BF16)
             gqkv[rows, g * 128 : g * 128 + 128] = unstack(tn(gs, k)) * score_scale
             gqkv[rows, C + g * 128 : C + g * 128 + 128] = nn(gs, stack_of(q)) * score_scale
-            gqkv[rows, 2 * C + g * 128 : 2 * C + g * 128 + 128] = nn(a.astype(BF16), gstack)
         return 0
 
-    lax.fori_loop(0, wide, pull, 0)
+    lax.fori_loop(0, wide, pull_scores, 0, unroll=True)
+    lax.fori_loop(0, wide, pull_pairs, 0, unroll=True)
+    gs_ref[...] += jnp.sum(prob[...], axis=0)
 
     gtriple = gqkv[...].astype(BF16)
     gbq_ref[...] += column_sum(gtriple.astype(F32))
@@ -406,7 +406,7 @@
 
 
 def wire_rows(device_count):
-    unit = 2 * device_count * 16
+    unit = 4 * device_count * 16
     return -(-WIRE_ROWS // unit) * unit
 
 
@@ -535,28 +535,39 @@
     )(starts, ranks, grads, master, first, second)
 
 
-def all_reduce_kernel(strips, buckets, in_ref, out_ref, core_in, core_sum, in_one, sum_one, in_two, sum_two,
-                      in_three, send_sems, recv_sems):
+def reduce_parts(strips, buckets, rows, orders):
+    sizes = {"z": strips // 2, "y": 2, "x": buckets // 2}
+    length = rows // 2 // len(orders)
+    parts = []
+    for order in orders:
+        levels, share = [], length
+        for axis in order:
+            share = share // sizes[axis]
+            levels.append((axis, sizes[axis], share))
+        parts.append((length, levels))
+    return parts
+
+
+def all_reduce_kernel(strips, buckets, parts, in_ref, out_ref, *scratch):
     strip, bucket = lax.axis_index("strip"), lax.axis_index("bucket")
     sizes = {"z": strips // 2, "y": 2, "x": buckets // 2, "core": 2}
     mine = {"z": strip // 2, "y": strip % 2, "x": bucket // 2, "core": bucket % 2}
-
-    def device(axis, index):
-        place = dict(mine)
-        place[axis] = index
-        return (place["z"] * 2 + place["y"], place["x"] * 2 + place["core"])
+    send_sems, recv_sems = scratch[-2:]
+    buffers = list(scratch[:-2])
 
     def peer(axis, offset):
         return lax.rem(mine[axis] + offset, sizes[axis])
 
+    def device(axis, offset):
+        place = dict(mine)
+        place[axis] = peer(axis, offset)
+        return (place["z"] * 2 + place["y"], place["x"] * 2 + place["core"])
+
     barrier = pltpu.get_barrier_semaphore()
-    greeted = 0
-    for axis, size in sizes.items():
-        for offset in range(1, size):
-            pl.semaphore_signal(barrier, inc=1, device_id=device(axis, peer(axis, offset)),
-                                device_id_type=pl.DeviceIdType.MESH)
-            greeted += 1
-    pl.semaphore_wait(barrier, greeted)
+    partners = [(axis, offset) for axis, size in sizes.items() for offset in range(1, size)]
+    for axis, offset in partners:
+        pl.semaphore_signal(barrier, inc=1, device_id=device(axis, offset), device_id_type=pl.DeviceIdType.MESH)
+    pl.semaphore_wait(barrier, len(partners))
 
     used = [0]
 
@@ -565,138 +576,88 @@
         used[0] += 1
         copy = pltpu.make_async_remote_copy(
             src_ref=source, dst_ref=target, send_sem=send_sems.at[at], recv_sem=recv_sems.at[at],
-            device_id=device(axis, peer(axis, offset)), device_id_type=pl.DeviceIdType.MESH,
+            device_id=device(axis, offset), device_id_type=pl.DeviceIdType.MESH,
         )
         copy.start()
         return copy
 
-    rows = in_ref.shape[0]
-    quarter = rows // 4
-    orders = [("x", "y"), ("y", "x")]
-    started = []
-
-    def at(start, length):
+    def span(start, length):
         return pl.ds(pl.multiple_of(start, 16), length)
 
-    flight = []
-    for p in range(2):
-        other = (1 - mine["core"]) * 2 * quarter + p * quarter
-        flight.append(send(in_ref.at[at(other, quarter)], core_in.at[p], "core", 1))
-    stage = []
-    for p in range(2):
-        flight[p].wait()
-        own = mine["core"] * 2 * quarter + p * quarter
-        core_sum[p] = in_ref[at(own, quarter), :] + core_in[p]
-        stage.append(core_sum.at[p])
-
-    def scatter(level, length, axis_of, inboxes, sums):
-        flights = []
-        for p in range(2):
-            axis = axis_of(p)
-            piece = length // sizes[axis]
-            group = []
-            for offset in range(1, sizes[axis]):
-                source = stage[p].at[at(peer(axis, offset) * piece, piece)]
-                group.append(send(source, inboxes.at[p, pl.ds((offset - 1) * piece, piece)], axis, offset))
-            flights.append(group)
-        for p in range(2):
-            axis = axis_of(p)
-            piece = length // sizes[axis]
-            for copy in flights[p]:
+    half = in_ref.shape[0] // 2
+
+    def part_steps(p, length, levels):
+        core_in, core_sum = buffers.pop(0), buffers.pop(0)
+        boxes = [(buffers.pop(0), buffers.pop(0)) for _ in levels]
+        own = mine["core"] * half + p * length
+        other = (1 - mine["core"]) * half + p * length
+        copy = send(in_ref.at[span(other, length)], core_in, "core", 1)
+        yield
+        copy.wait()
+        core_sum[...] = in_ref[span(own, length), :] + core_in[...]
+        held, spans = core_sum, [(own, length)]
+        for (axis, size, share), (inbox, total) in zip(levels, boxes):
+            copies = [
+                send(held.at[span(peer(axis, offset) * share, share)],
+                     inbox.at[pl.ds((offset - 1) * share, share)], axis, offset)
+                for offset in range(1, size)
+            ]
+            yield
+            for copy in copies:
                 copy.wait()
-            value = stage[p][at(mine[axis] * piece, piece), :].astype(F32)
-            for offset in range(1, sizes[axis]):
-                value = value + inboxes[p, (offset - 1) * piece : offset * piece, :].astype(F32)
-            if sums is None:
-                base = mine["core"] * 2 * quarter + p * quarter + spans(p)[-1][0]
-                out_ref[at(base, piece), :] = value.astype(BF16)
-            else:
-                sums[p, 0:piece, :] = value.astype(BF16)
-                stage[p] = sums.at[p]
-
-    def spans(p):
-        result = []
-        start, length = 0, quarter
-        for axis in orders[p] + ("z",):
-            length = length // sizes[axis]
-            start = start + mine[axis] * length
-            result.append((start, length))
-        return result
-
-    scatter(1, quarter, lambda p: orders[p][0], in_one, sum_one)
-    lengths = [quarter // sizes[orders[p][0]] for p in range(2)]
-
-    def scatter_two():
-        flights = []
-        for p in range(2):
-            axis = orders[p][1]
-            piece = lengths[p] // sizes[axis]
-            group = []
-            for offset in range(1, sizes[axis]):
-                source = stage[p].at[at(peer(axis, offset) * piece, piece)]
-                group.append(send(source, in_two.at[p, pl.ds((offset - 1) * piece, piece)], axis, offset))
-            flights.append(group)
-        for p in range(2):
-            axis = orders[p][1]
-            piece = lengths[p] // sizes[axis]
-            for copy in flights[p]:
+            value = held[span(mine[axis] * share, share), :].astype(F32)
+            for offset in range(1, size):
+                value = value + inbox[(offset - 1) * share : offset * share, :].astype(F32)
+            spans.append((spans[-1][0] + mine[axis] * share, share))
+            total[...] = value.astype(BF16)
+            held = total
+        start, share = spans[-1]
+        out_ref[span(start, share), :] = held[...]
+        for (axis, size, share), (start, _) in zip(levels[::-1], spans[:0:-1]):
+            region = out_ref.at[span(start, share)]
+            copies = [send(region, region, axis, offset) for offset in range(1, size)]
+            yield
+            for copy in copies:
                 copy.wait()
-            value = stage[p][at(mine[axis] * piece, piece), :].astype(F32)
-            for offset in range(1, sizes[axis]):
-                value = value + in_two[p, (offset - 1) * piece : offset * piece, :].astype(F32)
-            sum_two[p, 0:piece, :] = value.astype(BF16)
-            stage[p] = sum_two.at[p]
-
-    scatter_two()
-    eighth = quarter // (sizes["x"] * sizes["y"])
-    scatter(3, eighth, lambda p: "z", in_three, None)
-
-    for level in (2, 1, 0):
-        flights = []
-        for p in range(2):
-            axis = (orders[p] + ("z",))[level]
-            start, length = spans(p)[level]
-            region = out_ref.at[at(mine["core"] * 2 * quarter + p * quarter + start, length)]
-            flights.append([send(region, region, axis, offset) for offset in range(1, sizes[axis])])
-        for group in flights:
-            for copy in group:
-                copy.wait()
-    flights = []
-    for p in range(2):
-        region = out_ref.at[at(mine["core"] * 2 * quarter + p * quarter, quarter)]
-        flights.append(send(region, region, "core", 1))
-    for copy in flights:
+        region = out_ref.at[span(own, length)]
+        copy = send(region, region, "core", 1)
+        yield
         copy.wait()
 
-
-def all_reduce(values, strips, buckets):
+    running = [part_steps(p, length, levels) for p, (length, levels) in enumerate(parts)]
+    waiting, active = running, []
+    while waiting or active:
+        active, waiting = active + waiting[:2], waiting[2:]
+        for steps in list(active):
+            if next(steps, steps) is steps:
+                active.remove(steps)
+
+
+def all_reduce(values, strips, buckets, orders):
     rows = values.shape[0]
-    quarter = rows // 4
-    x, y, z = buckets // 2, 2, strips // 2
+    parts = reduce_parts(strips, buckets, rows, orders)
     vmem = pl.BlockSpec(memory_space=pltpu.VMEM)
-    copies = 2 * (2 * 1 + 2 * (x - 1 + y - 1 + z - 1))
-    small = min(x, y)
+    shapes, copies = [], 0
+    for length, levels in parts:
+        shapes += [(length, 128), (length, 128)]
+        for _, size, share in levels:
+            shapes += [((size - 1) * share, 128), (share, 128)]
+        copies += 2 + 2 * sum(size - 1 for _, size, _ in levels)
     return pl.pallas_call(
-        lambda *refs: all_reduce_kernel(strips, buckets, *refs),
+        lambda *refs: all_reduce_kernel(strips, buckets, parts, *refs),
         in_specs=[vmem],
         out_specs=vmem,
         out_shape=jax.ShapeDtypeStruct(values.shape, BF16),
-        scratch_shapes=[
-            pltpu.VMEM((2, quarter, 128), BF16),
-            pltpu.VMEM((2, quarter, 128), BF16),
-            pltpu.VMEM((2, quarter, 128), BF16),
-            pltpu.VMEM((2, quarter // small, 128), BF16),
-            pltpu.VMEM((2, quarter // small, 128), BF16),
-            pltpu.VMEM((2, quarter // (x * y), 128), BF16),
-            pltpu.VMEM((2, quarter // (x * y), 128), BF16),
-            pltpu.SemaphoreType.DMA((copies,)),
-            pltpu.SemaphoreType.DMA((copies,)),
-        ],
+        scratch_shapes=[pltpu.VMEM(shape, BF16) for shape in shapes]
+        + [pltpu.SemaphoreType.DMA((copies,)), pltpu.SemaphoreType.DMA((copies,))],
         compiler_params=pltpu.CompilerParams(
             vmem_limit_bytes=40 * 1024 * 1024, collective_id=0, has_side_effects=True
         ),
         name="all_reduce",
     )(values)
+
+
+ORDERS = (("x", "y", "z"), ("y", "x", "z")) * 2
 
 
 def shards(
@@ -711,7 +672,7 @@
     blocks = -(-(SMALL_START // 128 + 2) // 8) * 8
     owners = jnp.pad(owner_list, (0, blocks * 128 - owner_list.shape[0]), constant_values=-1).reshape(blocks, 128)
     sparse, ranks, starts = run_dispatch(my_index, owners, master, wire_total)
-    wire = all_reduce(sparse, strips, buckets)
+    wire = all_reduce(sparse, strips, buckets, ORDERS)
     small = [wire[SMALL_START + i * SMALL_SPAN : SMALL_START + (i + 1) * SMALL_SPAN].astype(F32) for i in range(3)]
     pairs = (2 * WIN - 1) ** 2
     table = (small[0] + small[1] + small[2])[SMALL_ROWS : SMALL_ROWS + TABLE_ROWS].reshape(-1)
@@ -730,7 +691,7 @@
     grad_wire = lax.dynamic_update_slice(grad_wire, grad_table.astype(BF16), (SMALL_START + SMALL_ROWS, 0))
     output = output.at[:, :SHIFT].set(from_behind(output_halo, "strip", 1).astype(F32))
     grad_input = grad_input.at[:, :SHIFT].set(from_behind(grad_halo, "strip", 1).astype(F32))
-    grads = all_reduce(grad_wire, strips, buckets)
+    grads = all_reduce(grad_wire, strips, buckets, ORDERS)
     first, second_new, new_weights = run_collect(starts, ranks, grads, master, first_moment, second_moment)
     return (output, grad_input, first, second_new, new_weights)
 

time: 445 us -> 322 us (0.72)
  Pallas kernels: 408 us -> 288 us
    pallas_call x1, Pallas kernels: 194 us -> 103 us  [run_block(): pl.pallas_call(block_kernel, grid=(samples,), in_specs=[smem, smem, per_i...]
    pallas_call x2, Pallas kernels: 186 us -> 158 us  [all_reduce(): pl.pallas_call(lambda *refs: all_reduce_kernel(strips, buckets, parts, *r...]
  transfers between devices with their start and end apart: 4 -> 4, of which waited for: 0 -> 0; matrix products, arithmetic and copies ran while one was open for 3% -> 4% of each run, Pallas kernels for 48% -> 58%
where the time goes in v3:
time: 322 us; the launch traced here: 321 us
  Pallas kernels  288 us (89%)
  local copies, waits for them, and re-layouts  14.9 us (5%)
  starting transfers between devices  8.94 us (3%)
  other arithmetic  4.34 us (1%)
  matrix products  3.78 us (1%)
    pallas_call x2, Pallas kernels, all_reduce(): pl.pallas_call(lambda *refs: all_reduce_kernel(strips, buckets, parts, *r...  158 us
    pallas_call x1, Pallas kernels, run_block(): pl.pallas_call(block_kernel, grid=(samples,), in_specs=[smem, smem, per_i...  103 us
    pallas_call x1, Pallas kernels, run_collect(): pl.pallas_call(collect_kernel, in_specs=[pl.BlockSpec(memory_space=pltpu....  18.8 us
    ppermute x4, starting transfers between devices, from_behind(): lax.ppermute(value, axis, [(i, (i + by) % peers) for i in range(peers)])  8.94 us
    pallas_call x1, Pallas kernels, run_dispatch(): pl.pallas_call(dispatch_kernel, in_specs=[pl.BlockSpec(memory_space=pltpu...  8.44 us
  transfers between devices with their start and end apart: 4, of which 0 were waited for; matrix products, arithmetic and copies ran while one was open for 4% of the time, Pallas kernels for 58%

profile of v3, /device:TPU:0, one launch (start us, length us, event | category | flops | bytes accessed | tf_op | source)
XLA Modules:
  0.0 321.5 jit_solution(4780812562822671043)
XLA Ops:
  0.7 2.7 slice.95
  3.4 6.0 %collective-permute-start.1 = (bf16[8,3,56,384]{3,2,1,0:T(8,128)(2,1)}, bf16[8,3,56,384]{3,2,1,0:T(8,128)(2,1)S(1)}, u32[]{:S(2)}, u32[]{:S(2)}) collective-permute-start(bf16[8,3,56,384]{3,2,1,0:T(8,128)(2,1)} %slice.95), channel_id=1, source_target_pairs={{0,28},{4,0},{8,4},{12,8},{16,12},{20,16},{24,20},{28,24},{1,29},{... | collective-permute-start | bytes 3096584 | tf_op jit(solution)/shard_map/ppermute | solution.py:34
  9.4 2.7 slice.96
  12.0 0.5 collective-permute-start
  13.2 0.1 copy.23
  13.3 8.4 %dispatch.1 = (bf16[14336,128]{1,0:T(8,128)(2,1)S(1)}, f32[112,128]{1,0:T(8,128)S(1)}, s32[112,128]{1,0:T(8,128)S(1)}) custom-call(s32[1]{0:T(128)} %bitcast.me_ref, s32[112,128]{1,0:T(8,128)S(1)} %pad_bitcast_fusion.owner_ref, f32[651,128]{1,0:T(8,128)S(1)} %copy-done.2), custom_call_target="tpu_custom_call" | custom-call | tf_op jit(solution)/shard_map/dispatch/pallas_call | solution.py:463
  21.7 0.0 copy-start.8
  21.8 75.9 %all_reduce.2.wire_ref = bf16[14336,128]{1,0:T(8,128)(2,1)S(1)} custom-call(bf16[14336,128]{1,0:T(8,128)(2,1)S(1)} %get-tuple-element.41.refs_0_), custom_call_target="tpu_custom_call" | custom-call | tf_op jit(solution)/shard_map/all_reduce/pallas_call | solution.py:646
  97.7 1.8 copy-done
  99.7 0.2 add.48
  99.9 0.1 reshape.162
  100.0 0.1 copy.24
  100.1 2.6 fusion.6
  102.6 0.2 add.45
  102.9 0.6 convert_multiply_fusion.keep_ref
  103.5 0.8 multiply_select_fusion.bias_ref
  104.3 1.0 copy-done.5
  105.3 1.0 copy-done.6
  106.3 102.7 %block.1 = (f32[8,7,56,384]{3,2,1,0:T(8,128)}, bf16[8,3,56,384]{3,2,1,0:T(8,128)(2,1)}, f32[8,7,56,384]{3,2,1,0:T(8,128)}, bf16[8,3,56,384]{3,2,1,0:T(8,128)(2,1...) custom-call(s32[1]{0:T(128)S(6)} %copy.33.cols_ref, f32[8,2]{1,0:T(8,128)} %convert_multiply_fusion.keep_ref, ...), custom_call_target="tpu_custom_call" | custom-call | tf_op jit(solution)/shard_map/block/pallas_call | solution.py:357
  209.0 0.1 collective-permute-start.2
  209.0 2.4 collective-permute-start.3
  211.4 1.1 reshape.163
  212.5 0.1 reshape.164
  212.7 1.2 fusion.9
  213.9 0.1 copy.26
  214.0 0.1 reshape.165
  214.2 1.3 dynamic_update_slice.3.refs_0_
  215.5 2.0 copy-done.1
  217.6 82.2 %all_reduce.3.grad_ref = bf16[14336,128]{1,0:T(8,128)(2,1)S(1)} custom-call(bf16[14336,128]{1,0:T(8,128)(2,1)S(1)} %copy-done.1), custom_call_target="tpu_custom_call" | custom-call | tf_op jit(solution)/shard_map/all_reduce/pallas_call | solution.py:646
  299.7 18.8 %collect.1 = (f32[651,128]{1,0:T(8,128)}, f32[651,128]{1,0:T(8,128)}, f32[651,128]{1,0:T(8,128)}) custom-call(s32[112,128]{1,0:T(8,128)S(1)} %get-tuple-element.46.start_ref, f32[112,128]{1,0:T(8,128)S(1)} %get-tuple-element.47.rank_ref, bf16[14336,128]{1,0:T(8,128)(2,1)S(1)} %all_reduce.3.grad_ref, f32[651,128]{1,0:T(8,128)S(1)} %copy-done.2, ...), custom_call_target="tpu_custom_call" | custom-call | tf_op jit(solution)/shard_map/collect/pallas_call | solution.py:524
  318.6 1.4 convert_dynamic-update-slice_fusion.1
  320.0 1.4 convert_dynamic-update-slice_fusion
  (36 shorter events, 0.2 us)
Async XLA Ops:
  0.6 12.6 %copy-start.10 = (s32[8,2]{0,1:T(2,128)S(1)}, s32[8,2]{0,1:T(2,128)}, u32[]{:S(2)}) copy-start(s32[8,2]{0,1:T(2,128)} %param.20) | copy-start | bytes 196
  0.6 12.6 %copy-start.7 = (s32[13879]{0:T(1024)S(1)}, s32[13879]{0:T(1024)}, u32[]{:S(2)}) copy-start(s32[13879]{0:T(1024)} %param.21) | copy-start | bytes 166552
  0.7 12.6 %copy-start.2 = (f32[651,128]{1,0:T(8,128)S(1)}, f32[651,128]{1,0:T(8,128)}, u32[]{:S(2)}) copy-start(f32[651,128]{1,0:T(8,128)} %master_ref.3) | copy-start | bytes 999940
  3.4 101.0 %collective-permute-start.1 = (bf16[8,3,56,384]{3,2,1,0:T(8,128)(2,1)}, bf16[8,3,56,384]{3,2,1,0:T(8,128)(2,1)S(1)}, u32[]{:S(2)}, u32[]{:S(2)}) collective-permute-start(bf16[8,3,56,384]{3,2,1,0:T(8,128)(2,1)} %slice.95), channel_id=1, source_target_pairs={{0,28},{4,0},{8,4},{12,8},{16,12},{20,16},{24,20},{28,24},{1,29},{... | collective-permute-start | bytes 3096584 | tf_op jit(solution)/shard_map/ppermute | solution.py:34
  12.0 92.3 %collective-permute-start = (bf16[8,3,56,384]{3,2,1,0:T(8,128)(2,1)}, bf16[8,3,56,384]{3,2,1,0:T(8,128)(2,1)S(1)}, u32[]{:S(2)}, u32[]{:S(2)}) collective-permute-start(bf16[8,3,56,384]{3,2,1,0:T(8,128)(2,1)} %slice.96), channel_id=1, source_target_pairs={{0,28},{4,0},{8,4},{12,8},{16,12},{20,16},{24,20},{28,24},{1,29},{... | collective-permute-start | bytes 3096584 | tf_op jit(solution)/shard_map/ppermute | solution.py:34
  21.7 77.8 %copy-start.8 = (pred[56,64]{1,0:T(8,128)(4,1)S(1)}, pred[56,64]{1,0:T(8,128)(4,1)}, u32[]{:S(2)}) copy-start(pred[56,64]{1,0:T(8,128)(4,1)} %constant.89.clone) | copy-start | bytes 10756
  21.8 77.8 %copy-start.9 = (pred[56,64]{1,0:T(8,128)(4,1)S(1)}, pred[56,64]{1,0:T(8,128)(4,1)}, u32[]{:S(2)}) copy-start(pred[56,64]{1,0:T(8,128)(4,1)} %constant.88.clone) | copy-start | bytes 10756
  21.8 78.3 %copy-start.12 = (s32[56,64]{1,0:T(8,128)S(1)}, s32[56,64]{1,0:T(8,128)}, u32[]{:S(2)}) copy-start(s32[56,64]{1,0:T(8,128)} %constant.101) | copy-start | bytes 43012
  21.8 81.7 %copy-start.11 = (pred[56]{0:T(512)(128)(4,1)S(1)}, pred[56]{0:T(512)(128)(4,1)}, u32[]{:S(2)}) copy-start(pred[56]{0:T(512)(128)(4,1)} %constant.90.clone) | copy-start | bytes 172
  97.7 1.8 copy-start
  104.3 108.3 %copy-start.13 = (s32[3584]{0:T(1024)S(1)}, s32[3584]{0:T(1024)}, u32[]{:S(2)}) copy-start(s32[3584]{0:T(1024)} %constant.87.clone) | copy-start | bytes 43012
  104.3 1.0 copy-start.5
  105.3 1.0 copy-start.6
  209.0 109.6 %collective-permute-start.2 = (bf16[8,3,56,384]{3,2,1,0:T(8,128)(2,1)}, bf16[8,3,56,384]{3,2,1,0:T(8,128)(2,1)S(1)}, u32[]{:S(2)}, u32[]{:S(2)}) collective-permute-start(bf16[8,3,56,384]{3,2,1,0:T(8,128)(2,1)} %get-tuple-element.43), channel_id=1, source_target_pairs={{0,4},{4,8},{8,12},{12,16},{16,20},{20,24},{24,28},{28,0},{1,5},{5... | collective-permute-start | bytes 3096584 | tf_op jit(solution)/shard_map/ppermute | solution.py:34
  209.0 111.0 %collective-permute-start.3 = (bf16[8,3,56,384]{3,2,1,0:T(8,128)(2,1)}, bf16[8,3,56,384]{3,2,1,0:T(8,128)(2,1)S(1)}, u32[]{:S(2)}, u32[]{:S(2)}) collective-permute-start(bf16[8,3,56,384]{3,2,1,0:T(8,128)(2,1)} %get-tuple-element.45), channel_id=1, source_target_pairs={{0,4},{4,8},{8,12},{12,16},{16,20},{20,24},{24,28},{28,0},{1,5},{5... | collective-permute-start | bytes 3096584 | tf_op jit(solution)/shard_map/ppermute | solution.py:34
  215.5 2.0 copy-start.1
  217.6 82.2 %copy-start.3 = (f32[651,128]{1,0:T(8,128)S(1)}, f32[651,128]{1,0:T(8,128)}, u32[]{:S(2)}) copy-start(f32[651,128]{1,0:T(8,128)} %first_ref.1) | copy-start | bytes 999940
  217.6 82.2 %copy-start.4 = (f32[651,128]{1,0:T(8,128)S(1)}, f32[651,128]{1,0:T(8,128)}, u32[]{:S(2)}) copy-start(f32[651,128]{1,0:T(8,128)} %second_ref.1) | copy-start | bytes 999940

commit v4 on v3

--- a/solution.py
+++ b/solution.py
@@ -27,11 +27,6 @@
 BETA_TWO = 0.5
 ADAM_EPS = 1e-08
 DECAY = 0.05
-
-
-def from_behind(value, axis, by):
-    peers = lax.axis_size(axis)
-    return lax.ppermute(value, axis, [(i, (i + by) % peers) for i in range(peers)])
 
 
 def row_edges():
@@ -121,9 +116,9 @@
 
 
 def block_kernel(
-    cols_ref, keep_ref, x_ref, xh_ref, dy_ref, dyh_ref, bias_ref,
-    wire_ref,
-    out_ref, outh_ref, gx_ref, gxh_ref, gwire_ref, gs_ref,
+    strips, cols_ref, keep_ref, x_ref, dy_ref, x_any, dy_any, bias_ref, wire_ref,
+    out_ref, gx_ref, outh_ref, gxh_ref, gwire_ref, gs_ref,
+    fetched, halo_out, halo_in, back_out, back_in, fetch_sem, send_sems, recv_sems,
     wq_ref, wp_ref, wu_ref, wd_ref, bq_ref, bp_ref, bu_ref, bd_ref, g1_ref, b1_ref, g2_ref, b2_ref,
     gwq_ref, gwp_ref, gwu_ref, gwdt_ref,
     gbq_ref, gbp_ref, gbu_ref, gbd_ref, gg1_ref, gb1_ref, gg2_ref, gb2_ref,
@@ -142,8 +137,40 @@
     vectors = (bq_ref, bp_ref, bu_ref, bd_ref, g1_ref, b1_ref, g2_ref, b2_ref)
     vector_grads = (gbq_ref, gbp_ref, gbu_ref, gbd_ref, gg1_ref, gb1_ref, gg2_ref, gb2_ref)
 
+    strip, bucket = lax.axis_index("strip"), lax.axis_index("bucket")
+    above = (lax.rem(strip + strips - 1, strips), bucket)
+    below = (lax.rem(strip + 1, strips), bucket)
+
+    def halo_copy(kind, image):
+        source = halo_out.at[kind, image] if kind < 2 else back_out.at[kind - 2, image]
+        target = halo_in.at[kind, image] if kind < 2 else back_in.at[kind - 2, image]
+        return pltpu.make_async_remote_copy(
+            src_ref=source, dst_ref=target, send_sem=send_sems.at[kind, image], recv_sem=recv_sems.at[kind, image],
+            device_id=above if kind < 2 else below, device_id_type=pl.DeviceIdType.MESH,
+        )
+
     @pl.when(step == 0)
     def _():
+        barrier = pltpu.get_barrier_semaphore()
+        fetches = [
+            pltpu.make_async_copy(array.at[:, pl.ds(0, SHIFT)], fetched.at[kind], fetch_sem.at[kind])
+            for kind, array in enumerate((x_any, dy_any))
+        ]
+        for fetch in fetches:
+            fetch.start()
+        for neighbour in (above, below):
+            pl.semaphore_signal(barrier, inc=1, device_id=neighbour, device_id_type=pl.DeviceIdType.MESH)
+        pl.semaphore_wait(barrier, 2)
+        for fetch in fetches:
+            fetch.wait()
+
+        def send_rows(image, _):
+            for kind in range(2):
+                halo_out[kind, image] = fetched[kind, image].astype(BF16)
+                halo_copy(kind, image).start()
+            return 0
+
+        lax.fori_loop(0, fetched.shape[1], send_rows, 0)
         for ref, (first, slabs, rows) in zip(matrices, slab_plan()):
             for j in range(slabs):
                 ref[:, j * 128 : j * 128 + 128] = wire_ref[first + j * rows : first + (j + 1) * rows, :]
@@ -162,41 +189,44 @@
         for ref in (gwq_ref, gwp_ref, gwu_ref, gwdt_ref, gs_ref) + vector_grads:
             ref[...] = jnp.zeros_like(ref)
 
-    def to_windows(main, halo, target):
+    def to_windows(main, kind, target):
+        halo_copy(kind, step).wait_recv()
+        wrapped_row = lax.broadcasted_iota(jnp.int32, (8, 128), 0) >= WIN - SHIFT
         for a in range(WIN):
-            row = main[0, SHIFT + a] if a < own else halo[0, a - own].astype(F32)
+            row = main[0, SHIFT + a] if a < own else halo_in[kind, step, a - own].astype(F32)
             for s in range(slabs):
-                part = row[:, s * 128 : s * 128 + 128]
-                line[s, a, 0:columns, :] = part
-                line[s, a, pl.ds(width, 8), :] = part[0:8]
+                line[s, a, 8 : 8 + columns, :] = row[:, s * 128 : s * 128 + 128]
+        for a in range(WIN):
+            for s in range(slabs):
+                front = line[s, a, 8 - (WIN - SHIFT) : 16 - (WIN - SHIFT), :]
+                for w in range(wide):
+                    first = 8 + w * WIN + SHIFT
+                    tile = jnp.where(wrapped_row & (w == cols_ref[0] - 1), front, line[s, a, first : first + 8, :])
+                    target[w * CELLS + a * 8 : w * CELLS + a * 8 + 8, s * 128 : s * 128 + 128] = tile
+
+    def from_windows(source, main, kind):
         for w in range(wide):
             for a in range(WIN):
                 for s in range(slabs):
-                    target[w * CELLS + a * 8 : w * CELLS + a * 8 + 8, s * 128 : s * 128 + 128] = line[
-                        s, a, w * WIN + SHIFT : w * WIN + SHIFT + 8, :
-                    ]
-
-    def from_windows(source, main, halo):
-        for w in range(wide):
-            for a in range(WIN):
-                for s in range(slabs):
-                    line[s, a, w * WIN + SHIFT : w * WIN + SHIFT + 8, :] = source[
+                    first = 8 + w * WIN + SHIFT
+                    line[s, a, first : first + 8, :] = source[
                         w * CELLS + a * 8 : w * CELLS + a * 8 + 8, s * 128 : s * 128 + 128
                     ]
         kept = lax.broadcasted_iota(jnp.int32, (columns, 128), 0) < width
         front = lax.broadcasted_iota(jnp.int32, (8, 128), 0) < SHIFT
         for a in range(WIN):
             for s in range(slabs):
-                wrapped = line[s, a, pl.ds(width, 8), :]
-                line[s, a, 0:8, :] = jnp.where(front, wrapped, line[s, a, 0:8, :])
-                row = jnp.where(kept, line[s, a, 0:columns, :], 0.0)
+                wrapped = line[s, a, pl.ds(width + 8, 8), :]
+                line[s, a, 8:16, :] = jnp.where(front, wrapped, line[s, a, 8:16, :])
+                row = jnp.where(kept, line[s, a, 8 : 8 + columns, :], 0.0)
                 if a < own:
                     main[0, SHIFT + a, :, s * 128 : s * 128 + 128] = row
                 else:
-                    halo[0, a - own, :, s * 128 : s * 128 + 128] = row.astype(BF16)
-
-    to_windows(x_ref, xh_ref, xw)
-    to_windows(dy_ref, dyh_ref, dyw)
+                    back_out[kind - 2, step, a - own, :, s * 128 : s * 128 + 128] = row.astype(BF16)
+        halo_copy(kind, step).start()
+
+    to_windows(x_ref, 0, xw)
+    to_windows(dy_ref, 1, dyw)
 
     normal, scale_one = row_norm(xw[...])
     n1s[...] = normal
@@ -275,7 +305,7 @@
     lax.fori_loop(0, FF // chunk, feed, 0, unroll=True)
 
     resw[...] = (x1s[...] + keep_two * (ys[...] + bd_ref[...])) * valid
-    from_windows(resw, out_ref, outh_ref)
+    from_windows(resw, out_ref, 2)
 
     gh2 = gh2s[...]
     gg2_ref[...] += column_sum(gh2 * n2s[...])
@@ -322,7 +352,7 @@
     gg1_ref[...] += column_sum(gz * n1s[...])
     gb1_ref[...] += column_sum(gz)
     resw[...] = x1s[...] + norm_pull(gz * g1_ref[...], n1s[...], scale_one)
-    from_windows(resw, gx_ref, gxh_ref)
+    from_windows(resw, gx_ref, 3)
 
     @pl.when(step == pl.num_programs(0) - 1)
     def _():
@@ -337,8 +367,19 @@
         pieces.append(jnp.zeros((spare, 128), F32))
         gwire_ref[SMALL_START:, :] = jnp.concatenate(pieces, axis=0).astype(BF16)
 
-
-def run_block(cols, keep, x, xh, dy, dyh, bias, wire):
+        def finish(image, _):
+            for kind in range(2):
+                halo_copy(kind, image).wait_send()
+            for kind in range(2, 4):
+                halo_copy(kind, image).wait()
+            outh_ref[image] = back_in[0, image]
+            gxh_ref[image] = back_in[1, image]
+            return 0
+
+        lax.fori_loop(0, fetched.shape[1], finish, 0)
+
+
+def run_block(cols, keep, x, dy, bias, wire, strips):
     samples, rows, columns, _ = x.shape
     wide = columns // WIN
     tokens = wide * CELLS
@@ -350,23 +391,35 @@
         return pl.BlockSpec(shape, lambda i: (0,) * len(shape))
 
     smem = pl.BlockSpec(memory_space=pltpu.SMEM)
+    vmem = pl.BlockSpec(memory_space=pltpu.VMEM)
+    hbm = pl.BlockSpec(memory_space=pl.ANY)
     full = jax.ShapeDtypeStruct(x.shape, F32)
-    part = jax.ShapeDtypeStruct(xh.shape, BF16)
+    halo = (samples, SHIFT, columns, C)
+    part = jax.ShapeDtypeStruct(halo, BF16)
     sums = (GROUPS, CELLS, GROUP_HEADS * LANES)
     vectors = [3 * C, C, FF, C, C, C, C, C]
     return pl.pallas_call(
-        block_kernel,
+        lambda *refs: block_kernel(strips, *refs),
         grid=(samples,),
-        in_specs=[smem, smem, per_image(x), per_image(xh), per_image(dy), per_image(dyh), whole(bias.shape)]
-        + [whole(wire.shape)],
-        out_specs=[per_image(x), per_image(xh), per_image(x), per_image(xh), whole(wire.shape), whole(sums)],
-        out_shape=[full, part, full, part, jax.ShapeDtypeStruct(wire.shape, BF16), jax.ShapeDtypeStruct(sums, F32)],
-        scratch_shapes=[pltpu.VMEM(s, BF16) for s in ((C, 3 * C), (C, C), (C, FF), (FF, C))]
+        in_specs=[smem, smem, per_image(x), per_image(dy), hbm, hbm, whole(bias.shape), whole(wire.shape)],
+        out_specs=[per_image(x), per_image(x), vmem, vmem, whole(wire.shape), whole(sums)],
+        out_shape=[full, full, part, part, jax.ShapeDtypeStruct(wire.shape, BF16), jax.ShapeDtypeStruct(sums, F32)],
+        scratch_shapes=[
+            pltpu.VMEM((2,) + halo, F32),
+            pltpu.VMEM((2,) + halo, BF16),
+            pltpu.VMEM((2,) + halo, BF16),
+            pltpu.VMEM((2,) + halo, BF16),
+            pltpu.VMEM((2,) + halo, BF16),
+            pltpu.SemaphoreType.DMA((2,)),
+            pltpu.SemaphoreType.DMA((4, samples)),
+            pltpu.SemaphoreType.DMA((4, samples)),
+        ]
+        + [pltpu.VMEM(s, BF16) for s in ((C, 3 * C), (C, C), (C, FF), (FF, C))]
         + [pltpu.VMEM((1, size), F32) for size in vectors]
         + [pltpu.VMEM(s, F32) for s in ((C, 3 * C), (C, C), (C, FF), (C, FF))]
         + [pltpu.VMEM((1, size), F32) for size in vectors]
         + [
-            pltpu.VMEM((C // 128, WIN, columns + 8, 128), F32),
+            pltpu.VMEM((C // 128, WIN, columns + 16, 128), F32),
             pltpu.VMEM((tokens, C), F32),
             pltpu.VMEM((tokens, C), F32),
             pltpu.VMEM((tokens, C), F32),
@@ -386,9 +439,9 @@
             pltpu.VMEM((C, tokens), BF16),
             pltpu.VMEM((C, tokens), BF16),
         ],
-        compiler_params=pltpu.CompilerParams(vmem_limit_bytes=58 * 1024 * 1024),
+        compiler_params=pltpu.CompilerParams(vmem_limit_bytes=60 * 1024 * 1024, collective_id=1, has_side_effects=True),
         name="block",
-    )(cols, keep, x, xh, dy, dyh, bias, wire)
+    )(cols, keep, x, dy, x, dy, bias, wire)
 
 
 SMALL_START = 3 * C * C // 128 + C * C // 128 + 2 * C * FF // 128
@@ -666,8 +719,6 @@
     strips = lax.axis_size("strip")
     buckets = lax.axis_size("bucket")
     wire_total = wire_rows(strips * buckets)
-    x_halo = from_behind(block_input[:, :SHIFT].astype(BF16), "strip", -1)
-    dy_halo = from_behind(cotangent[:, :SHIFT].astype(BF16), "strip", -1)
     my_index = lax.axis_index(("strip", "bucket")).astype(jnp.int32).reshape(1)
     blocks = -(-(SMALL_START // 128 + 2) // 8) * 8
     owners = jnp.pad(owner_list, (0, blocks * 128 - owner_list.shape[0]), constant_values=-1).reshape(blocks, 128)
@@ -679,8 +730,8 @@
     table = table[: pairs * HEADS].reshape(pairs, HEADS)
     bias = attention_bias(table, lax.axis_index("strip") == strips - 1)
     keep = keep_mask.astype(F32) / KEEP_PROB
-    output, output_halo, grad_input, grad_halo, grad_wire, pair_sums = run_block(
-        window_cols, keep, block_input, x_halo, cotangent, dy_halo, bias, wire
+    output, grad_input, output_halo, grad_halo, grad_wire, pair_sums = run_block(
+        window_cols, keep, block_input, cotangent, bias, wire, strips
     )
     pair_sums = pair_sums.reshape(GROUPS, CELLS, GROUP_HEADS, LANES).transpose(0, 2, 1, 3)
     grad_table = lax.dot_general(
@@ -689,8 +740,8 @@
     ).reshape(-1)
     grad_table = jnp.pad(grad_table, (0, TABLE_ROWS * 128 - pairs * HEADS)).reshape(TABLE_ROWS, 128)
     grad_wire = lax.dynamic_update_slice(grad_wire, grad_table.astype(BF16), (SMALL_START + SMALL_ROWS, 0))
-    output = output.at[:, :SHIFT].set(from_behind(output_halo, "strip", 1).astype(F32))
-    grad_input = grad_input.at[:, :SHIFT].set(from_behind(grad_halo, "strip", 1).astype(F32))
+    output = output.at[:, :SHIFT].set(output_halo.astype(F32))
+    grad_input = grad_input.at[:, :SHIFT].set(grad_halo.astype(F32))
     grads = all_reduce(grad_wire, strips, buckets, ORDERS)
     first, second_new, new_weights = run_collect(starts, ranks, grads, master, first_moment, second_moment)
     return (output, grad_input, first, second_new, new_weights)

time: 322 us -> 270 us (0.84)
  Pallas kernels: 288 us -> 249 us
  starting transfers between devices: 8.94 us -> 0 us
    pallas_call x2, Pallas kernels: 158 us -> 101 us  [all_reduce(): pl.pallas_call(lambda *refs: all_reduce_kernel(strips, buckets, parts, *r...]
    pallas_call x1, Pallas kernels: 103 us -> 120 us  [run_block(): pl.pallas_call(lambda *refs: block_kernel(strips, *refs), grid=(samples,)...]
    ppermute x4 -> x0, starting transfers between devices: 8.94 us -> none  [from_behind(): lax.ppermute(value, axis, [(i, (i + by) % peers) for i in range(peers)])]
    slice x2 -> x0, local copies, waits for them, and re-layouts: 5.36 us -> none  [the longest x1 2.71 us: shards(): dy_halo = from_behind(cotangent[:, :SHIFT].astype(BF16), 'strip', -1)]
    unnamed x29 -> x35, local copies, waits for them, and re-layouts: 5.95 us -> 9.43 us
  transfers between devices with their start and end apart: 4 -> 0, of which waited for: 0 -> 0; matrix products, arithmetic and copies ran while one was open for 4% -> 0% of each run, Pallas kernels for 58% -> 0%
where the time goes in v4:
time: 270 us; the launch traced here: 269 us
  Pallas kernels  249 us (92%)
  local copies, waits for them, and re-layouts  13.8 us (5%)
  matrix products  3.78 us (1%)
    pallas_call x1, Pallas kernels, run_block(): pl.pallas_call(lambda *refs: block_kernel(strips, *refs), grid=(samples,)...  120 us
    pallas_call x2, Pallas kernels, all_reduce(): pl.pallas_call(lambda *refs: all_reduce_kernel(strips, buckets, parts, *r...  101 us
    pallas_call x1, Pallas kernels, run_collect(): pl.pallas_call(collect_kernel, in_specs=[pl.BlockSpec(memory_space=pltpu....  18.8 us
    unnamed x35, local copies, waits for them, and re-layouts  9.43 us
    pallas_call x1, Pallas kernels, run_dispatch(): pl.pallas_call(dispatch_kernel, in_specs=[pl.BlockSpec(memory_space=pltpu...  8.43 us

profile of v4, /device:TPU:0, one launch (start us, length us, event | category | flops | bytes accessed | tf_op | source)
XLA Modules:
  0.0 269.5 jit_solution(4785898892873266058)
XLA Ops:
  0.6 0.0 copy-start.14
  0.7 0.8 pad_bitcast_fusion.owner_ref
  1.5 1.0 copy-done.2
  2.5 8.4 %dispatch.1 = (bf16[14336,128]{1,0:T(8,128)(2,1)S(1)}, f32[112,128]{1,0:T(8,128)S(1)}, s32[112,128]{1,0:T(8,128)S(1)}) custom-call(s32[1]{0:T(128)} %bitcast.me_ref, s32[112,128]{1,0:T(8,128)S(1)} %pad_bitcast_fusion.owner_ref, f32[651,128]{1,0:T(8,128)S(1)} %copy-done.2), custom_call_target="tpu_custom_call" | custom-call | tf_op jit(solution)/shard_map/dispatch/pallas_call | solution.py:516
  10.9 0.0 copy-start.13
  10.9 0.0 copy-start.12
  10.9 52.4 %all_reduce.2.refs_7_ = bf16[14336,128]{1,0:T(8,128)(2,1)S(1)} custom-call(bf16[14336,128]{1,0:T(8,128)(2,1)S(1)} %get-tuple-element.41.refs_0_), custom_call_target="tpu_custom_call" | custom-call | tf_op jit(solution)/shard_map/all_reduce/pallas_call | solution.py:699
  63.3 1.8 copy-done
  65.2 0.1 reshape.162
  65.3 0.1 copy.24
  65.4 2.6 fusion.6
  68.0 0.2 add.45
  68.3 0.2 add.48
  68.5 0.8 multiply_select_fusion.refs_6_
  69.3 0.1 copy.23
  69.4 0.6 convert_multiply_fusion.refs_1_
  70.7 0.0 copy-start.15
  70.7 120.1 %block.1 = (f32[8,7,56,384]{3,2,1,0:T(8,128)}, f32[8,7,56,384]{3,2,1,0:T(8,128)}, bf16[8,3,56,384]{3,2,1,0:T(8,128)(2,1)}, bf16[8,3,56,384]{3,2,1,0:T(8,128)(2,1...) custom-call(s32[1]{0:T(128)S(6)} %copy.35.refs_0_, f32[8,2]{1,0:T(8,128)} %convert_multiply_fusion.refs_1_, ...), custom_call_target="tpu_custom_call" | custom-call | tf_op jit(solution)/shard_map/block/pallas_call | solution.py:401
  190.8 1.1 reshape.163
  191.9 0.0 copy-start.3
  191.9 0.0 copy-start.4
  192.0 0.1 reshape.164
  192.1 1.2 fusion.9
  193.4 0.1 copy.26
  193.5 0.1 reshape.165
  193.6 1.3 dynamic_update_slice.3.refs_0_
  195.0 2.0 copy-done.1
  197.0 48.8 %all_reduce.3.grad_ref = bf16[14336,128]{1,0:T(8,128)(2,1)S(1)} custom-call(bf16[14336,128]{1,0:T(8,128)(2,1)S(1)} %copy-done.1), custom_call_target="tpu_custom_call" | custom-call | tf_op jit(solution)/shard_map/all_reduce/pallas_call | solution.py:699
  245.9 18.8 %collect.1 = (f32[651,128]{1,0:T(8,128)}, f32[651,128]{1,0:T(8,128)}, f32[651,128]{1,0:T(8,128)}) custom-call(s32[112,128]{1,0:T(8,128)S(1)} %get-tuple-element.46.start_ref, f32[112,128]{1,0:T(8,128)S(1)} %get-tuple-element.47.rank_ref, bf16[14336,128]{1,0:T(8,128)(2,1)S(1)} %all_reduce.3.grad_ref, f32[651,128]{1,0:T(8,128)S(1)} %copy-done.3, ...), custom_call_target="tpu_custom_call" | custom-call | tf_op jit(solution)/shard_map/collect/pallas_call | solution.py:577
  264.8 0.3 convert_dynamic-update-slice_fusion
  265.0 2.2 copy.36
  267.3 2.2 copy.37
  (31 shorter events, 0.2 us)
Async XLA Ops:
  0.6 64.8 %copy-start.14 = (s32[56,64]{1,0:T(8,128)S(1)}, s32[56,64]{1,0:T(8,128)}, u32[]{:S(2)}) copy-start(s32[56,64]{1,0:T(8,128)} %constant.101) | copy-start | bytes 43012
  1.5 1.0 copy-start.2
  2.5 65.8 %copy-start.10 = (pred[56,64]{1,0:T(8,128)(4,1)S(1)}, pred[56,64]{1,0:T(8,128)(4,1)}, u32[]{:S(2)}) copy-start(pred[56,64]{1,0:T(8,128)(4,1)} %constant.88.clone) | copy-start | bytes 10756
  2.5 65.8 %copy-start.11 = (pred[56,64]{1,0:T(8,128)(4,1)S(1)}, pred[56,64]{1,0:T(8,128)(4,1)}, u32[]{:S(2)}) copy-start(pred[56,64]{1,0:T(8,128)(4,1)} %constant.89.clone) | copy-start | bytes 10756
  10.9 57.6 %copy-start.13 = (pred[56]{0:T(512)(128)(4,1)S(1)}, pred[56]{0:T(512)(128)(4,1)}, u32[]{:S(2)}) copy-start(pred[56]{0:T(512)(128)(4,1)} %constant.90.clone) | copy-start | bytes 172
  10.9 58.4 %copy-start.12 = (s32[8,2]{0,1:T(2,128)S(1)}, s32[8,2]{0,1:T(2,128)}, u32[]{:S(2)}) copy-start(s32[8,2]{0,1:T(2,128)} %param.20) | copy-start | bytes 196
  63.3 1.8 copy-start
  70.7 121.4 %copy-start.15 = (s32[3584]{0:T(1024)S(1)}, s32[3584]{0:T(1024)}, u32[]{:S(2)}) copy-start(s32[3584]{0:T(1024)} %constant.87.clone) | copy-start | bytes 43012
  191.9 54.0 %copy-start.3 = (f32[651,128]{1,0:T(8,128)S(1)}, f32[651,128]{1,0:T(8,128)}, u32[]{:S(2)}) copy-start(f32[651,128]{1,0:T(8,128)} %master_ref.3) | copy-start | bytes 999940
  191.9 54.0 %copy-start.4 = (f32[651,128]{1,0:T(8,128)S(1)}, f32[651,128]{1,0:T(8,128)}, u32[]{:S(2)}) copy-start(f32[651,128]{1,0:T(8,128)} %first_ref.1) | copy-start | bytes 999940
  191.9 54.0 %copy-start.5 = (f32[651,128]{1,0:T(8,128)S(1)}, f32[651,128]{1,0:T(8,128)}, u32[]{:S(2)}) copy-start(f32[651,128]{1,0:T(8,128)} %second_ref.1) | copy-start | bytes 999940
  195.0 2.0 copy-start.1
  197.0 67.7 %copy-start.6 = (f32[8,7,56,384]{3,2,1,0:T(8,128)S(1)}, f32[8,7,56,384]{3,2,1,0:T(8,128)}, u32[]{:S(2)}) copy-start(f32[8,7,56,384]{3,2,1,0:T(8,128)} %get-tuple-element.42) | copy-start | bytes 14450692
  197.0 67.7 %copy-start.7 = (f32[8,7,56,384]{3,2,1,0:T(8,128)S(1)}, f32[8,7,56,384]{3,2,1,0:T(8,128)}, u32[]{:S(2)}) copy-start(f32[8,7,56,384]{3,2,1,0:T(8,128)} %get-tuple-element.44) | copy-start | bytes 14450692
  197.0 67.7 %copy-start.8 = (bf16[8,3,56,384]{3,2,1,0:T(8,128)(2,1)S(1)}, bf16[8,3,56,384]{3,2,1,0:T(8,128)(2,1)}, u32[]{:S(2)}) copy-start(bf16[8,3,56,384]{3,2,1,0:T(8,128)(2,1)} %get-tuple-element.43) | copy-start | bytes 3096580
  197.0 67.7 %copy-start.9 = (bf16[8,3,56,384]{3,2,1,0:T(8,128)(2,1)S(1)}, bf16[8,3,56,384]{3,2,1,0:T(8,128)(2,1)}, u32[]{:S(2)}) copy-start(bf16[8,3,56,384]{3,2,1,0:T(8,128)(2,1)} %get-tuple-element.45) | copy-start | bytes 3096580

commit v5 on v1

v5 whole, which is shorter than its diff:
```python
import functools
import math

import jax
import jax.numpy as jnp
from jax import lax
from jax.experimental import pallas as pl
from jax.experimental.pallas import tpu as pltpu
from jax.sharding import PartitionSpec as P

C = 384
HEADS = 12
HD = 32
FF = 1536
WIN = 7
SHIFT = 3
STEP = 10
SMALL_ROWS = 39
TABLE_ROWS = 16


PRECISE = lax.Precision.HIGHEST
NORM_EPS = 1e-05
KEEP_PROB = 0.8
MASK_FILL = -100.0
BETA_ONE = 0.5
BETA_TWO = 0.5
ADAM_EPS = 1e-08
DECAY = 0.05


def row_edges():
    first = 3 * C * C // 128
    second = first + C * C // 128
    third = second + C * FF // 128
    fourth = third + FF * C // 128
    fifth = fourth + SMALL_ROWS
    return [first, second, third, fourth, fifth]


GROUPS = 3
GROUP_HEADS = HEADS // GROUPS
CELLS = WIN * 8
LANES = 64
LOG2E = math.log2(math.e)
F32 = jnp.float32
BF16 = jnp.bfloat16


def nn(left, right):
    return lax.dot_general(left, right, (((1,), (0,)), ((), ())), preferred_element_type=F32)


def nt(left, right):
    return lax.dot_general(left, right, (((1,), (1,)), ((), ())), preferred_element_type=F32)


def tn(left, right):
    return lax.dot_general(left, right, (((0,), (0,)), ((), ())), preferred_element_type=F32)


def gelu_pair(u):
    normal = 0.5 + 0.5 * lax.erf(u * math.sqrt(0.5))
    gauss = jnp.exp2(u * u * (-0.5 * LOG2E))
    return u * normal, normal + u * gauss * (1.0 / math.sqrt(2.0 * math.pi))


def row_norm(values):
    center = values - jnp.mean(values, axis=-1, keepdims=True)
    scale = lax.rsqrt(jnp.mean(center * center, axis=-1, keepdims=True) + NORM_EPS)
    return center * scale, scale


def norm_pull(grad, normal, scale):
    first = jnp.mean(grad, axis=-1, keepdims=True)
    second = jnp.mean(grad * normal, axis=-1, keepdims=True)
    return scale * (grad - first - normal * second)


def column_sum(values):
    return jnp.sum(values, axis=0, keepdims=True)


SMALL_START = 3 * C * C // 128 + C * C // 128 + 2 * C * FF // 128
SMALL_SPAN = 64


def slab_plan():
    return [
        (0, 3 * C // 128, C),
        (3 * C * C // 128, C // 128, C),
        (4 * C * C // 128, FF // 128, C),
        (4 * C * C // 128 + C * FF // 128, C // 128, FF),
    ]


ORDERS = (("x", "y", "z"), ("y", "x", "z")) * 2
LAG = 2
FIRST_ROWS = 3 * C * C // 128


def split_three(values):
    high = values.astype(BF16)
    rest = values - high.astype(F32)
    middle = rest.astype(BF16)
    return high, middle, (rest - middle.astype(F32)).astype(BF16)


def wire_rows(rows, strips, buckets):
    unit = 16 * strips * buckets
    return -(-rows // unit) * unit


def reduce_plan(strips, buckets, rows, orders):
    sizes = {"z": strips // 2, "y": 2, "x": buckets // 2}
    unit = 8 * strips * buckets
    units = rows // 2 // unit
    orders = orders[:units]
    parts, first = [], 0
    for p, order in enumerate(orders):
        length = (units // len(orders) + (p < units % len(orders))) * unit
        levels, share = [], length
        for axis in order:
            share = share // sizes[axis]
            levels.append((axis, sizes[axis], share))
        parts.append((first, length, levels))
        first += length
    return parts


def reduce_scratch(plan):
    shapes, copies = [], 0
    for _, length, levels in plan:
        shapes += [(length, 128), (length, 128)]
        for _, size, share in levels:
            shapes += [((size - 1) * share, 128), (share, 128)]
        copies += 2 + 2 * sum(size - 1 for _, size, _ in levels)
    return [pltpu.VMEM(shape, BF16) for shape in shapes] + [
        pltpu.SemaphoreType.DMA((copies,)), pltpu.SemaphoreType.DMA((copies,))
    ]


class Place:
    def __init__(self, strips, buckets):
        strip, bucket = lax.axis_index("strip"), lax.axis_index("bucket")
        self.sizes = {"z": strips // 2, "y": 2, "x": buckets // 2, "core": 2}
        self.mine = {"z": strip // 2, "y": strip % 2, "x": bucket // 2, "core": bucket % 2}
        self.above = (lax.rem(strip + strips - 1, strips), bucket)
        self.below = (lax.rem(strip + 1, strips), bucket)

    def peer(self, axis, offset):
        return lax.rem(self.mine[axis] + offset, self.sizes[axis])

    def device(self, axis, offset):
        place = dict(self.mine)
        place[axis] = self.peer(axis, offset)
        return (place["z"] * 2 + place["y"], place["x"] * 2 + place["core"])

    def greet(self, halos):
        barrier = pltpu.get_barrier_semaphore()
        partners = [self.device(axis, offset) for axis, size in self.sizes.items() for offset in range(1, size)]
        partners += [self.above, self.below] if halos else []
        for partner in partners:
            pl.semaphore_signal(barrier, inc=1, device_id=partner, device_id_type=pl.DeviceIdType.MESH)
        pl.semaphore_wait(barrier, len(partners))


def reduce_stages(place, plan, wire, scratch):
    buffers, send_sems, recv_sems = list(scratch[:-2]), scratch[-2], scratch[-1]
    half = wire.shape[0] // 2
    counter = [0]

    def span(start, length):
        return pl.ds(pl.multiple_of(start, 16), length)

    def copies_of(count):
        first = counter[0]
        counter[0] += count
        return first

    def copy(at, source, target, axis, offset):
        return pltpu.make_async_remote_copy(
            src_ref=source, dst_ref=target, send_sem=send_sems.at[at], recv_sem=recv_sems.at[at],
            device_id=place.device(axis, offset), device_id_type=pl.DeviceIdType.MESH,
        )

    def part_stages(first, length, levels):
        core_in, core_sum = buffers.pop(0), buffers.pop(0)
        boxes = [(buffers.pop(0), buffers.pop(0)) for _ in levels]
        held = [core_sum] + [total for _, total in boxes]

        def own():
            return place.mine["core"] * half + first

        def start_of(level):
            start = own()
            for axis, _, share in levels[:level]:
                start = start + place.mine[axis] * share
            return start

        core_at, back_at = copies_of(1), copies_of(1)
        down_at = [copies_of(size - 1) for _, size, _ in levels]
        up_at = [copies_of(size - 1) for _, size, _ in levels]

        def core_out():
            other = (1 - place.mine["core"]) * half + first
            return [copy(core_at, wire.at[span(other, length)], core_in, "core", 1)]

        def down(level):
            axis, size, share = levels[level]
            inbox = boxes[level][0]
            return [
                copy(down_at[level] + offset - 1, held[level].at[span(place.peer(axis, offset) * share, share)],
                     inbox.at[pl.ds((offset - 1) * share, share)], axis, offset)
                for offset in range(1, size)
            ]

        def up(level):
            axis, size, share = levels[level]
            region = wire.at[span(start_of(level + 1), share)]
            return [copy(up_at[level] + offset - 1, region, region, axis, offset) for offset in range(1, size)]

        def core_back():
            region = wire.at[span(own(), length)]
            return [copy(back_at, region, region, "core", 1)]

        def add_core():
            core_sum[...] = wire[span(own(), length), :] + core_in[...]

        def add(level):
            axis, size, share = levels[level]
            inbox, total = boxes[level]
            value = held[level][span(place.mine[axis] * share, share), :].astype(F32)
            for offset in range(1, size):
                value = value + inbox[(offset - 1) * share : offset * share, :].astype(F32)
            if level + 1 < len(levels):
                total[...] = value.astype(BF16)
            else:
                wire[span(start_of(len(levels)), share), :] = value.astype(BF16)

        count = len(levels)
        moves = [core_out] + [functools.partial(down, level) for level in range(count)]
        moves += [functools.partial(up, level) for level in reversed(range(count))] + [core_back]
        work = {1: add_core}
        for level in range(count):
            work[level + 2] = functools.partial(add, level)

        def stage(index):
            if index > 0:
                for one in moves[index - 1]():
                    one.wait()
            if index in work:
                work[index]()
            if index < len(moves):
                for one in moves[index]():
                    one.start()

        return [functools.partial(stage, index) for index in range(len(moves) + 1)]

    return [part_stages(*part) for part in plan]


def reduce_ticks(parts):
    ticks = []
    for p, stages in enumerate(parts):
        for index, stage in enumerate(stages):
            at = index + p // 2
            while len(ticks) <= at:
                ticks.append([])
            ticks[at].append(stage)

    def run(tick):
        for stage in tick:
            stage()

    return [functools.partial(run, tick) for tick in ticks]


def tick_slots(ticks, slots):
    return [[tick for i, tick in enumerate(ticks) if i * slots // len(ticks) == slot] for slot in range(slots)]


def head_bits():
    lane_head = lax.broadcasted_iota(jnp.int32, (1, 128), 1) // HD
    return [(lane_head == h).astype(F32).astype(BF16) for h in range(GROUP_HEADS)]


def stack_of(part, bits):
    return jnp.concatenate([part * bit for bit in bits], axis=0)


def unstack(part):
    lane_head = lax.broadcasted_iota(jnp.int32, (1, 128), 1) // HD
    total = None
    for h in range(GROUP_HEADS):
        piece = jnp.where(lane_head == h, part[h * LANES : h * LANES + CELLS], 0.0)
        total = piece if total is None else total + piece
    return total


def load_matrix(target, wire, first, rows):
    for j in range(target.shape[1] // 128):
        target[:, j * 128 : j * 128 + 128] = wire[first + j * rows : first + (j + 1) * rows, :]


def load_vectors(refs, wire, first):
    small = jnp.zeros((SMALL_SPAN, 128), F32)
    for i in range(3):
        small = small + wire[FIRST_ROWS + i * SMALL_SPAN : FIRST_ROWS + (i + 1) * SMALL_SPAN, :].astype(F32)
    for ref, row in zip(refs, first):
        for j in range(ref.shape[1] // 128):
            ref[:, j * 128 : j * 128 + 128] = small[row + j : row + j + 1]


def to_windows(line, last, main, halo, step, target):
    slabs, columns = C // 128, main.shape[2]
    wide, own = columns // WIN, WIN - SHIFT
    wrapped_row = lax.broadcasted_iota(jnp.int32, (8, 128), 0) >= own
    for a in range(WIN):
        row = main[0, SHIFT + a] if a < own else halo[step, a - own].astype(F32)
        for s in range(slabs):
            line[s, a, 8 : 8 + columns, :] = row[:, s * 128 : s * 128 + 128]
    for a in range(WIN):
        for s in range(slabs):
            front = line[s, a, 8 - own : 16 - own, :]
            for w in range(wide):
                first = 8 + w * WIN + SHIFT
                tile = jnp.where(wrapped_row & (w == last), front, line[s, a, first : first + 8, :])
                target[w * CELLS + a * 8 : w * CELLS + a * 8 + 8, s * 128 : s * 128 + 128] = tile


def from_windows(line, width, source, main, halo, step):
    slabs, columns = C // 128, main.shape[2]
    wide, own = columns // WIN, WIN - SHIFT
    for w in range(wide):
        for a in range(WIN):
            for s in range(slabs):
                first = 8 + w * WIN + SHIFT
                line[s, a, first : first + 8, :] = source[
                    w * CELLS + a * 8 : w * CELLS + a * 8 + 8, s * 128 : s * 128 + 128
                ]
    kept = lax.broadcasted_iota(jnp.int32, (columns, 128), 0) < width
    front = lax.broadcasted_iota(jnp.int32, (8, 128), 0) < SHIFT
    for a in range(WIN):
        for s in range(slabs):
            wrapped = line[s, a, pl.ds(width + 8, 8), :]
            line[s, a, 8:16, :] = jnp.where(front, wrapped, line[s, a, 8:16, :])
            row = jnp.where(kept, line[s, a, 8 : 8 + columns, :], 0.0)
            if a < own:
                main[0, a, :, s * 128 : s * 128 + 128] = row
            else:
                halo[step, a - own, :, s * 128 : s * 128 + 128] = row.astype(BF16)


def place_onehot(row):
    shape = (128, HEADS * LANES)
    source = lax.broadcasted_iota(jnp.int32, shape, 0)
    lane = lax.broadcasted_iota(jnp.int32, shape, 1)
    return (lane == source // 8 * LANES + row * 8 + source % 8).astype(F32).astype(BF16)


def offset_onehot(column):
    shape = (256, 128)
    source = lax.broadcasted_iota(jnp.int32, shape, 0)
    lane = lax.broadcasted_iota(jnp.int32, shape, 1)
    wanted = (lane % 8 - column + WIN - 1) * HEADS + lane // 8
    return ((source == wanted) & (lane < HEADS * 8)).astype(F32).astype(BF16)


SPAN = 2 * WIN - 1


def build_bias(raw, last_strip, offsets, spread, bias):
    flat = jnp.concatenate([raw[r : r + 1] for r in range(TABLE_ROWS)], axis=1)
    offsets[...] = jnp.zeros_like(offsets)
    spread[...] = jnp.zeros_like(spread)
    for d in range(SPAN):
        offsets[SPAN - 1 - d : SPAN - d, 0 : SPAN * HEADS] = flat[:, d * SPAN * HEADS : (d + 1) * SPAN * HEADS]
    terms = split_three(offsets[...])
    for column in range(WIN):
        pick = offset_onehot(column)
        part = nn(terms[0], pick) + nn(terms[1], pick) + nn(terms[2], pick)
        spread[pl.ds(column, SPAN, stride=8), :] = part[0:SPAN]
    terms = split_three(spread[...])
    total = jnp.zeros((CELLS, HEADS * LANES), F32)
    for row in range(WIN):
        pick = place_onehot(row)
        for term in terms:
            total = total + nn(term[8 * (WIN - 1 - row) : 8 * (WIN - 1 - row) + CELLS], pick)
    shape = (CELLS, HEADS * LANES)
    key = lax.broadcasted_iota(jnp.int32, shape, 0)
    query = lax.broadcasted_iota(jnp.int32, shape, 1) % LANES
    edge = WIN - SHIFT
    by_row = ((key // 8 >= edge) != (query // 8 >= edge)) & last_strip
    by_col = (key % 8 >= edge) != (query % 8 >= edge)
    for variant, masked in enumerate((by_row, by_row | by_col)):
        value = (total + jnp.where(masked, MASK_FILL, 0.0)) * LOG2E
        value = jnp.where(key % 8 < WIN, value, -1e30)
        for g in range(GROUPS):
            bias[variant, g] = value[:, g * GROUP_HEADS * LANES : (g + 1) * GROUP_HEADS * LANES]


def pull_bias(sums, spread):
    grads = jnp.concatenate([sums[g] for g in range(GROUPS)], axis=1)
    high, middle, _ = split_three(grads)
    spread[...] = jnp.zeros_like(spread)
    for row in range(WIN):
        pick = place_onehot(row)
        first = 8 * (WIN - 1 - row)
        spread[first : first + CELLS, :] += nt(high, pick) + nt(middle, pick)
    total = jnp.zeros((SPAN, 256), F32)
    for column in range(WIN):
        pick = offset_onehot(column)
        high, middle, _ = split_three(spread[pl.ds(column, SPAN, stride=8), :])
        total = total + nt(high, pick) + nt(middle, pick)
    flat = [total[SPAN - 1 - d : SPAN - d, 0 : SPAN * HEADS] for d in range(SPAN)]
    flat.append(jnp.zeros((1, TABLE_ROWS * 128 - SPAN * SPAN * HEADS), F32))
    flat = jnp.concatenate(flat, axis=1)
    return jnp.concatenate([flat[:, r * 128 : r * 128 + 128] for r in range(TABLE_ROWS)], axis=0)


def block_kernel(
    strips, buckets, images, plan_one, plan_two,
    cols_ref, keep_ref, x_ref, dy_ref, x_any, dy_any, one_any, two_any,
    out_ref, gx_ref, outh_any, gxh_any, gone_any, gtwo_any,
    wq_ref, wp_ref, wu_ref, wd_ref, bq_ref, bp_ref, bu_ref, bd_ref, g1_ref, b1_ref, g2_ref, b2_ref,
    gwq_ref, gwp_ref, gwu_ref, gwdt_ref, gbq_ref, gbp_ref, gbu_ref, gbd_ref, gg1_ref, gb1_ref, gg2_ref, gb2_ref,
    bias, gs_ref, offsets, spread,
    xw, zs, qkv, prob, ctx, gctx, gx1s,
    line, dyw, x1s, n2s, h2s, gfs, ys, gh2s, resw, htr, gtr, gscores, gqkv,
    fetched, halo_out, halo_in, back_in, wire_one, wire_two,
    local_sems, send_sems, recv_sems, *scratch,
):
    step = pl.program_id(0)
    tokens = dyw.shape[0]
    wide = tokens // CELLS
    place = Place(strips, buckets)
    last = cols_ref[0] - 1
    width = cols_ref[0] * WIN
    count_one = len(reduce_scratch(plan_one))
    parts_one = reduce_stages(place, plan_one, wire_one, scratch[:count_one])
    parts_two = reduce_stages(place, plan_two, wire_two, scratch[count_one:])
    gather_ticks = reduce_ticks(parts_one + parts_two)
    early = len(parts_one[0])
    one_ticks, two_ticks = reduce_ticks(parts_one), reduce_ticks(parts_two)

    def halo(kind, image):
        return pltpu.make_async_remote_copy(
            src_ref=halo_out.at[kind % 2, image], dst_ref=(halo_in if kind < 2 else back_in).at[kind % 2, image],
            send_sem=send_sems.at[kind, image], recv_sem=recv_sems.at[kind, image],
            device_id=place.above if kind < 2 else place.below, device_id_type=pl.DeviceIdType.MESH,
        )

    def fetch(array, image, kind):
        return pltpu.make_async_copy(array.at[image, pl.ds(0, SHIFT)], fetched.at[kind], local_sems.at[kind])

    def send_rows(kind, image, held):
        halo_out[kind, image] = fetched[held].astype(BF16)
        halo(kind, image).start()

    @pl.when(step == 0)
    def _():
        loads = [
            pltpu.make_async_copy(source, target, local_sems.at[2 + i])
            for i, (source, target) in enumerate(((one_any, wire_one), (two_any, wire_two)))
        ]
        first = [fetch(x_any, image, image) for image in range(2)]
        for copy in loads + first:
            copy.start()
        place.greet(True)
        for copy in loads:
            copy.wait()
        gather_ticks[0]()
        for image in range(2):
            first[image].wait()
            send_rows(0, image, image)
        fetch(x_any, 2, 0).start()
        fetch(dy_any, 0, 1).start()
        line[...] = jnp.zeros_like(line)
        for ref in (gwq_ref, gwp_ref, gwu_ref, gwdt_ref, gbq_ref, gbp_ref, gbu_ref, gbd_ref,
                    gg1_ref, gb1_ref, gg2_ref, gb2_ref, gs_ref, qkv, gctx):
            ref[...] = jnp.zeros_like(ref)
        for tick in gather_ticks[1:early]:
            tick()
        load_matrix(wq_ref, wire_one, 0, C)
        load_vectors((bq_ref, bp_ref, bu_ref, bd_ref, g1_ref, b1_ref, g2_ref, b2_ref), wire_one,
                     (0, 9, 12, 24, 27, 30, 33, 36))
        raw = jnp.zeros((SMALL_SPAN, 128), F32)
        for i in range(3):
            raw = raw + wire_one[FIRST_ROWS + i * SMALL_SPAN : FIRST_ROWS + (i + 1) * SMALL_SPAN, :].astype(F32)
        build_bias(raw[SMALL_ROWS : SMALL_ROWS + TABLE_ROWS], lax.axis_index("strip") == strips - 1, offsets, spread, bias)

    @pl.when((step > 0) & (step + 1 < images))
    def _():
        fetch(x_any, step + 1, 0).wait()
        send_rows(0, step + 1, 0)

    @pl.when((step > 0) & (step + 2 < images))
    def _():
        fetch(x_any, step + 2, 0).start()

    @pl.when((step > 0) & (step - 1 < images))
    def _():
        fetch(dy_any, step - 1, 1).wait()
        send_rows(1, step - 1, 1)

    @pl.when((step > 0) & (step < images))
    def _():
        fetch(dy_any, step, 1).start()

    bits = head_bits()

    def attend(image):
        at = lax.rem(image, LAG)
        halo(0, image).wait_recv()
        to_windows(line, last, x_ref, halo_in.at[0], image, xw.at[at])
        normal, _ = row_norm(xw[at])
        zs[at] = (normal * g1_ref[...] + b1_ref[...]).astype(BF16)
        triple = nn(zs[at], wq_ref[...]) + bq_ref[...]
        for w in range(wide):
            qkv[at, w, 0:CELLS, :] = triple[w * CELLS : w * CELLS + CELLS].astype(BF16)
        for w in range(wide):
            variant = (w == last).astype(jnp.int32)
            for g in range(GROUPS):
                q = qkv[at, w, :, g * 128 : g * 128 + 128]
                k = qkv[at, w, 0:CELLS, C + g * 128 : C + g * 128 + 128]
                v = qkv[at, w, 0:CELLS, 2 * C + g * 128 : 2 * C + g * 128 + 128]
                s = nt(k, stack_of(q, bits)) * (HD ** (-0.5) * LOG2E) + bias[variant, g]
                e = jnp.exp2(s - jnp.max(s, axis=0, keepdims=True))
                a = (e * (1.0 / jnp.sum(e, axis=0, keepdims=True))).astype(BF16)
                prob[at, w, g] = a
                resw[w * CELLS : w * CELLS + CELLS, g * 128 : g * 128 + 128] = unstack(tn(a, v))
        ctx[at] = resw[...].astype(BF16)

    def feed(image):
        at = lax.rem(image, LAG)
        keep_one = keep_ref[image, 0]
        keep_two = keep_ref[image, 1]
        x1 = xw[at] + keep_one * (nn(ctx[at], wp_ref[...]) + bp_ref[...])
        x1s[...] = x1
        normal, scale_two = row_norm(x1)
        n2s[...] = normal
        h2 = (normal * g2_ref[...] + b2_ref[...]).astype(BF16)
        h2s[...] = h2
        htr[...] = h2.astype(F32).T.astype(BF16)

        halo(1, image).wait_recv()
        to_windows(line, last, dy_ref, halo_in.at[1], image, dyw)
        token = lax.broadcasted_iota(jnp.int32, (tokens, 1), 0)
        valid = ((token % 8 < WIN) & (token < cols_ref[0] * CELLS)).astype(F32)
        gy = dyw[...] * valid
        gf = (gy * keep_two).astype(BF16)
        gfs[...] = gf
        gbd_ref[...] += column_sum(gf.astype(F32))
        gtr[...] = gf.astype(F32).T.astype(BF16)
        ys[...] = jnp.zeros_like(ys)
        gh2s[...] = jnp.zeros_like(gh2s)
        chunk = 512
        for j in range(FF // chunk):
            part = slice(j * chunk, (j + 1) * chunk)
            u = nn(h2s[...], wu_ref[:, part]) + bu_ref[:, part]
            gm = nt(gfs[...], wd_ref[part, :])
            m, slope = gelu_pair(u)
            m = m.astype(BF16)
            gu = (gm * slope).astype(BF16)
            ys[...] += nn(m, wd_ref[part, :])
            gwdt_ref[:, part] += nn(gtr[...], m)
            gwu_ref[:, part] += nn(htr[...], gu)
            gbu_ref[:, part] += column_sum(gu.astype(F32))
            gh2s[...] += nt(gu, wu_ref[:, part])

        resw[...] = (x1s[...] + keep_two * (ys[...] + bd_ref[...])) * valid
        halo(1, image).wait_send()
        from_windows(line, width, resw, out_ref, halo_out.at[1], image)
        halo(3, image).start()

        gh2 = gh2s[...]
        gg2_ref[...] += column_sum(gh2 * n2s[...])
        gb2_ref[...] += column_sum(gh2)
        gx1 = dyw[...] * valid + norm_pull(gh2 * g2_ref[...], n2s[...], scale_two)
        gx1s[at] = gx1
        ga = (keep_one * gx1).astype(BF16)
        gbp_ref[...] += column_sum(ga.astype(F32))
        gwp_ref[...] += nn(ctx[at].astype(F32).T.astype(BF16), ga)
        gc = nt(ga, wp_ref[...])
        for w in range(wide):
            gctx[at, w, 0:CELLS, :] = gc[w * CELLS : w * CELLS + CELLS].astype(BF16)

    def pull(image, middle):
        at = lax.rem(image, LAG)
        scale = HD ** (-0.5)
        for w in range(wide):
            rows = slice(w * CELLS, w * CELLS + CELLS)
            for g in range(GROUPS):
                v = qkv[at, w, 0:CELLS, 2 * C + g * 128 : 2 * C + g * 128 + 128]
                gstack = stack_of(gctx[at, w, :, g * 128 : g * 128 + 128], bits)
                low = prob[at, w, g]
                a = low.astype(F32)
                grad = nt(v, gstack)
                inner = jnp.sum(grad * a, axis=0, keepdims=True)
                gscores[w, g] = a * (grad - inner)
                gqkv[rows, 2 * C + g * 128 : 2 * C + g * 128 + 128] = nn(low, gstack)
        middle()
        for w in range(wide):
            rows = slice(w * CELLS, w * CELLS + CELLS)
            for g in range(GROUPS):
                q = qkv[at, w, :, g * 128 : g * 128 + 128]
                k = qkv[at, w, 0:CELLS, C + g * 128 : C + g * 128 + 128]
                gs = gscores[w, g].astype(BF16)
                gqkv[rows, g * 128 : g * 128 + 128] = unstack(tn(gs, k)) * scale
                gqkv[rows, C + g * 128 : C + g * 128 + 128] = nn(gs, stack_of(q, bits)) * scale
        gs_ref[...] += jnp.sum(gscores[...], axis=0)

        gtriple = gqkv[...].astype(BF16)
        gbq_ref[...] += column_sum(gtriple.astype(F32))
        gwq_ref[...] += nn(zs[at].astype(F32).T.astype(BF16), gtriple)
        gz = nt(gtriple, wq_ref[...]).astype(BF16).astype(F32)
        normal, scale_one = row_norm(xw[at])
        gg1_ref[...] += column_sum(gz * normal)
        gb1_ref[...] += column_sum(gz)
        resw[...] = gx1s[at] + norm_pull(gz * g1_ref[...], normal, scale_one)
        halo(0, image).wait_send()
        from_windows(line, width, resw, gx_ref, halo_out.at[0], image)
        halo(2, image).start()

    def pack_two():
        first = 0
        for grad in (gwp_ref, gwu_ref):
            for j in range(grad.shape[1] // 128):
                wire_two[first : first + C, :] = grad[:, j * 128 : j * 128 + 128].astype(BF16)
                first += C
        for j in range(C // 128):
            wire_two[first : first + FF, :] = gwdt_ref[j * 128 : j * 128 + 128, :].T.astype(BF16)
            first += FF
        wire_two[first:, :] = jnp.zeros((wire_two.shape[0] - first, 128), BF16)

    def pack_one():
        for j in range(3 * C // 128):
            wire_one[j * C : (j + 1) * C, :] = gwq_ref[:, j * 128 : j * 128 + 128].astype(BF16)
        vectors = (gbq_ref, gbp_ref, gbu_ref, gbd_ref, gg1_ref, gb1_ref, gg2_ref, gb2_ref)
        pieces = [ref[:, j * 128 : j * 128 + 128] for ref in vectors for j in range(ref.shape[1] // 128)]
        pieces.append(pull_bias(gs_ref, spread))
        pieces.append(jnp.zeros((wire_one.shape[0] - FIRST_ROWS - SMALL_ROWS - TABLE_ROWS, 128), F32))
        wire_one[FIRST_ROWS:, :] = jnp.concatenate(pieces, axis=0).astype(BF16)

    @pl.when(step == LAG)
    def _():
        first = 0
        for ref, rows in ((wp_ref, C), (wu_ref, C), (wd_ref, FF)):
            load_matrix(ref, wire_two, first, rows)
            first += ref.shape[1] // 128 * rows

    @pl.when((step >= LAG) & (step < images + LAG))
    def _():
        feed(step - LAG)

    @pl.when((step >= LAG) & (step < images))
    def _():
        pull(step - LAG, lambda: None)

    @pl.when(step < images)
    def _():
        attend(step)

    late = gather_ticks[early:]
    for k in range(LAG):
        mine = late[k * len(late) // LAG : (k + 1) * len(late) // LAG]

        @pl.when(step == k)
        def _(mine=mine):
            for tick in mine:
                tick()

    @pl.when(step == images + LAG - 1)
    def _():
        pack_two()
        two_ticks[0]()

    for k in range(LAG):

        @pl.when(step == images + LAG + k)
        def _(k=k):
            two_ticks[2 * k + 1]()
            pull(images - LAG + k, two_ticks[2 * k + 2])

    @pl.when(step == images + 2 * LAG - 1)
    def _():
        pack_one()
        rest = two_ticks[2 * LAG + 1 :]
        for i in range(max(len(rest), len(one_ticks))):
            for ticks in (one_ticks, rest):
                if i < len(ticks):
                    ticks[i]()
        for image in range(images):
            for kind in range(2, 4):
                halo(kind, image).wait()
        stores = [
            pltpu.make_async_copy(source, target, local_sems.at[i])
            for i, (source, target) in enumerate(
                ((wire_one, gone_any), (wire_two, gtwo_any), (back_in.at[0], gxh_any), (back_in.at[1], outh_any))
            )
        ]
        for copy in stores:
            copy.start()
        for copy in stores:
            copy.wait()


SMEM_SPEC = pl.BlockSpec(memory_space=pltpu.SMEM)
HBM_SPEC = pl.BlockSpec(memory_space=pl.ANY)


def run_block(cols, keep, x, dy, one, two, strips, buckets):
    samples, rows, columns, _ = x.shape
    wide = columns // WIN
    tokens = wide * CELLS
    own = rows - SHIFT
    halo = (samples, SHIFT, columns, C)
    plan_one = reduce_plan(strips, buckets, one.shape[0], ORDERS[:2])
    plan_two = reduce_plan(strips, buckets, two.shape[0], ORDERS)
    top = samples - 1

    def attended(i):
        return (jnp.minimum(i, top), 0, 0, 0)

    def fed(i):
        return (jnp.minimum(jnp.maximum(i - LAG, 0), top), 0, 0, 0)

    def pulled(i):
        early = jnp.minimum(jnp.maximum(i - LAG, 0), top - LAG)
        return (early + jnp.maximum(i - (samples + LAG) + 1, 0), 0, 0, 0)

    vectors = [3 * C, C, FF, C, C, C, C, C]
    sums = (GROUPS, CELLS, GROUP_HEADS * LANES)

    def struct(shape, dtype=F32):
        return jax.ShapeDtypeStruct(shape, dtype)

    token = pltpu.VMEM((tokens, C), F32)
    low = pltpu.VMEM((tokens, C), BF16)
    turned = pltpu.VMEM((C, tokens), BF16)
    scratch = [pltpu.VMEM(s, BF16) for s in ((C, 3 * C), (C, C), (C, FF), (FF, C))]
    scratch += [pltpu.VMEM((1, size), F32) for size in vectors]
    scratch += [pltpu.VMEM(s, F32) for s in ((C, 3 * C), (C, C), (C, FF), (C, FF))]
    scratch += [pltpu.VMEM((1, size), F32) for size in vectors]
    scratch += [
        pltpu.VMEM((2,) + sums, F32), pltpu.VMEM(sums, F32),
        pltpu.VMEM((16, 256), F32), pltpu.VMEM((SPAN * 8, 128), F32),
        pltpu.VMEM((LAG, tokens, C), F32), pltpu.VMEM((LAG, tokens, C), BF16),
        pltpu.VMEM((LAG, wide, LANES, 3 * C), BF16), pltpu.VMEM((LAG, wide) + sums, BF16),
        pltpu.VMEM((LAG, tokens, C), BF16), pltpu.VMEM((LAG, wide, LANES, C), BF16),
        pltpu.VMEM((LAG, tokens, C), F32),
        pltpu.VMEM((C // 128, WIN, columns + 16, 128), F32),
        token, token, token, low, low, token, token, token, turned, turned,
        pltpu.VMEM((wide,) + sums, F32), pltpu.VMEM((tokens, 3 * C), F32),
        pltpu.VMEM((2,) + halo[1:], F32),
        pltpu.VMEM((2,) + halo, BF16), pltpu.VMEM((2,) + halo, BF16), pltpu.VMEM((2,) + halo, BF16),
        pltpu.VMEM(one.shape, BF16), pltpu.VMEM(two.shape, BF16),
        pltpu.SemaphoreType.DMA((4,)), pltpu.SemaphoreType.DMA((4, samples)), pltpu.SemaphoreType.DMA((4, samples)),
    ]
    block = (1, rows, columns, C)
    part = (1, own, columns, C)
    return pl.pallas_call(
        lambda *refs: block_kernel(strips, buckets, samples, plan_one, plan_two, *refs),
        grid=(samples + 2 * LAG,),
        in_specs=[SMEM_SPEC, SMEM_SPEC, pl.BlockSpec(block, attended), pl.BlockSpec(block, fed)] + [HBM_SPEC] * 4,
        out_specs=[pl.BlockSpec(part, fed), pl.BlockSpec(part, pulled)] + [HBM_SPEC] * 4,
        out_shape=[struct((samples, own, columns, C)), struct((samples, own, columns, C)), struct(halo, BF16),
                   struct(halo, BF16), struct(one.shape, BF16), struct(two.shape, BF16)],
        scratch_shapes=scratch + reduce_scratch(plan_one) + reduce_scratch(plan_two),
        compiler_params=pltpu.CompilerParams(
            vmem_limit_bytes=62 * 1024 * 1024, collective_id=1, has_side_effects=True
        ),
        name="block",
    )(cols, keep, x, dy, x, dy, one, two)


def dispatch_kernel(me_ref, owner_ref, master_ref, one_ref, two_ref, rank_ref, start_ref, padded, packed, start_s, sem):
    blocks = owner_ref.shape[0]
    capacity = master_ref.shape[0]
    mine = (owner_ref[...] == me_ref[0]).astype(F32)
    low = mine.astype(BF16)
    row = lax.broadcasted_iota(jnp.int32, (128, 128), 0)
    col = lax.broadcasted_iota(jnp.int32, (128, 128), 1)
    within = nn(low, (row <= col).astype(F32).astype(BF16))
    sums = nn(low, jnp.ones((128, 128), BF16))
    below = lax.broadcasted_iota(jnp.int32, (blocks, blocks), 1) < lax.broadcasted_iota(jnp.int32, (blocks, blocks), 0)
    start = nn(below.astype(F32).astype(BF16), sums.astype(BF16))
    rank_ref[...] = jnp.where(mine > 0, within - 1.0, -1.0)
    start_ref[...] = start.astype(jnp.int32)
    copy = pltpu.make_async_copy(start_ref, start_s, sem)
    copy.start()
    padded[...] = jnp.zeros_like(padded)
    padded[0:capacity, :] = master_ref[...]
    one_ref[FIRST_ROWS:, :] = jnp.zeros((one_ref.shape[0] - FIRST_ROWS, 128), BF16)
    used = SMALL_START - FIRST_ROWS
    two_ref[used:, :] = jnp.zeros((two_ref.shape[0] - used, 128), BF16)
    copy.wait()
    slot = row.astype(F32)

    def block(b, _):
        hot = (slot == rank_ref[pl.ds(b, 1), :]).astype(F32).astype(BF16)
        rows = padded[pl.ds(start_s[b, 0], 128), :].astype(BF16)
        packed[pl.ds(pl.multiple_of(b * 128, 128), 128), :] = tn(hot, rows)
        return 0

    small = SMALL_START // 128
    lax.fori_loop(0, small, block, 0, unroll=4)
    hot = (slot == rank_ref[small : small + 1, :]).astype(F32).astype(BF16)
    for i, piece in enumerate(split_three(padded[pl.ds(start_s[small, 0], 128), :])):
        first = FIRST_ROWS + i * SMALL_SPAN
        one_ref[first : first + SMALL_SPAN, :] = tn(hot, piece)[0:SMALL_SPAN].astype(BF16)
    for first, slabs, rows in slab_plan():
        for j in range(slabs):
            target, offset = (one_ref, 0) if first < FIRST_ROWS else (two_ref, FIRST_ROWS)
            target[first - offset + j * rows : first - offset + (j + 1) * rows, :] = packed[
                pl.ds(first + j, rows, stride=slabs), :
            ].astype(BF16)


def run_dispatch(me, owners, master, one_rows, two_rows):
    blocks = owners.shape[0]
    vmem = pl.BlockSpec(memory_space=pltpu.VMEM)
    return pl.pallas_call(
        dispatch_kernel,
        in_specs=[pl.BlockSpec(memory_space=pltpu.SMEM), vmem, vmem],
        out_specs=[vmem] * 4,
        out_shape=[
            jax.ShapeDtypeStruct((one_rows, 128), BF16),
            jax.ShapeDtypeStruct((two_rows, 128), BF16),
            jax.ShapeDtypeStruct((blocks, 128), F32),
            jax.ShapeDtypeStruct((blocks, 128), jnp.int32),
        ],
        scratch_shapes=[
            pltpu.VMEM((-(-(master.shape[0] + 128) // 8) * 8, 128), F32),
            pltpu.VMEM((SMALL_START, 128), F32),
            pltpu.SMEM((blocks, 128), jnp.int32),
            pltpu.SemaphoreType.DMA,
        ],
        compiler_params=pltpu.CompilerParams(vmem_limit_bytes=62 * 1024 * 1024),
        name="dispatch",
    )(me, owners, master)


def collect_kernel(
    start_ref, rank_ref, one_ref, two_ref, master_ref, first_ref, second_ref, outh_ref, gxh_ref, out_any, gx_any,
    first_out, second_out, master_out, out_final, gx_final, packed, total, wide, sems,
):
    own = out_any.shape[1]
    moves = [
        pltpu.make_async_copy(main, final.at[:, pl.ds(SHIFT, own)], sems.at[i])
        for i, (main, final) in enumerate(((out_any, out_final), (gx_any, gx_final)))
    ]
    for i, (halo, final) in enumerate(((outh_ref, out_final), (gxh_ref, gx_final))):
        wide[i] = halo[...].astype(F32)
        moves.append(pltpu.make_async_copy(wide.at[i], final.at[:, pl.ds(0, SHIFT)], sems.at[2 + i]))
    for move in moves:
        move.start()
    capacity = master_ref.shape[0]
    total[...] = jnp.zeros_like(total)
    for first, slabs, rows in slab_plan():
        for j in range(slabs):
            source, offset = (one_ref, 0) if first < FIRST_ROWS else (two_ref, FIRST_ROWS)
            packed[pl.ds(first + j, rows, stride=slabs), :] = source[
                first - offset + j * rows : first - offset + (j + 1) * rows, :
            ].astype(F32)
    packed[SMALL_START : SMALL_START + SMALL_SPAN, :] = one_ref[FIRST_ROWS : FIRST_ROWS + SMALL_SPAN, :].astype(F32)
    packed[SMALL_START + SMALL_SPAN : SMALL_START + 128, :] = jnp.zeros((128 - SMALL_SPAN, 128), F32)
    slot = lax.broadcasted_iota(jnp.int32, (128, 128), 0).astype(F32)

    def block(b, _):
        hot = (slot == rank_ref[pl.ds(b, 1), :]).astype(F32).astype(BF16)
        part = nn(hot, packed[pl.ds(pl.multiple_of(b * 128, 128), 128), :].astype(BF16))
        where = pl.ds(start_ref[b, 0], 128)
        total[where, :] = total[where, :] + part
        return 0

    lax.fori_loop(0, SMALL_START // 128 + 1, block, 0, unroll=4)
    slots = lax.broadcasted_iota(jnp.int32, (capacity, 1), 0)
    edges = [edge // 128 for edge in row_edges()[:4]] + [SMALL_START // 128 + 1]
    rates = [2.0 / math.sqrt(C), 2.0 / math.sqrt(C // 8), 2.0 / math.sqrt(C), 2.0 / math.sqrt(FF), 1.0, 0.0]
    rate = jnp.full((capacity, 1), rates[0], F32)
    for edge, amount in zip(edges, rates[1:]):
        rate = jnp.where(slots >= start_ref[edge, 0], amount, rate)
    decay = jnp.where(slots < start_ref[edges[3], 0], DECAY, 0.0)
    grads = total[0:capacity, :]
    weights = master_ref[...]
    first = BETA_ONE * first_ref[...] + (1.0 - BETA_ONE) * grads
    second = BETA_TWO * second_ref[...] + (1.0 - BETA_TWO) * grads * grads
    first_out[...] = first
    second_out[...] = second
    first_hat = first / (1.0 - BETA_ONE**STEP)
    second_hat = second / (1.0 - BETA_TWO**STEP)
    master_out[...] = weights - rate * (first_hat / (jnp.sqrt(second_hat) + ADAM_EPS) + decay * weights)
    for move in moves:
        move.wait()


def run_collect(starts, ranks, one, two, master, first, second, outh, gxh, out, gx):
    vmem = pl.BlockSpec(memory_space=pltpu.VMEM)
    samples, own, columns, channels = out.shape
    final = jax.ShapeDtypeStruct((samples, own + SHIFT, columns, channels), F32)
    return pl.pallas_call(
        collect_kernel,
        in_specs=[SMEM_SPEC] + [vmem] * 8 + [HBM_SPEC] * 2,
        out_specs=[vmem] * 3 + [HBM_SPEC] * 2,
        out_shape=[jax.ShapeDtypeStruct(master.shape, F32)] * 3 + [final, final],
        scratch_shapes=[
            pltpu.VMEM((SMALL_START + 128, 128), F32),
            pltpu.VMEM((-(-(master.shape[0] + 128) // 8) * 8, 128), F32),
            pltpu.VMEM((2,) + outh.shape, F32),
            pltpu.SemaphoreType.DMA((4,)),
        ],
        compiler_params=pltpu.CompilerParams(vmem_limit_bytes=62 * 1024 * 1024),
        name="collect",
    )(starts, ranks, one, two, master, first, second, outh, gxh, out, gx)


def shards(
    block_input, cotangent, window_cols, keep_mask, owner_list, master, first_moment, second_moment
):
    strips = lax.axis_size("strip")
    buckets = lax.axis_size("bucket")
    my_index = lax.axis_index(("strip", "bucket")).astype(jnp.int32).reshape(1)
    blocks = -(-(SMALL_START // 128 + 2) // 8) * 8
    owners = jnp.pad(owner_list, (0, blocks * 128 - owner_list.shape[0]), constant_values=-1).reshape(blocks, 128)
    one_rows = wire_rows(FIRST_ROWS + 3 * SMALL_SPAN, strips, buckets)
    two_rows = wire_rows(SMALL_START - FIRST_ROWS, strips, buckets)
    one, two, ranks, starts = run_dispatch(my_index, owners, master, one_rows, two_rows)
    keep = keep_mask.astype(F32) / KEEP_PROB
    output, grad_input, output_halo, grad_halo, gone, gtwo = run_block(
        window_cols, keep, block_input, cotangent, one, two, strips, buckets
    )
    first, second_new, new_weights, output, grad_input = run_collect(
        starts, ranks, gone, gtwo, master, first_moment, second_moment, output_halo, grad_halo, output, grad_input
    )
    return (output, grad_input, first, second_new, new_weights)


def solution(mesh):
    in_specs = (
        P("bucket", "strip", None, None),
        P("bucket", "strip", None, None),
        P("bucket"),
        P("bucket", None),
        P(),
        P(("strip", "bucket"), None),
        P(("strip", "bucket"), None),
        P(("strip", "bucket"), None),
    )
    out_specs = (
        P("bucket", "strip", None, None),
        P("bucket", "strip", None, None),
        P(("strip", "bucket"), None),
        P(("strip", "bucket"), None),
        P(("strip", "bucket"), None),
    )
    return jax.shard_map(shards, mesh=mesh, in_specs=in_specs, out_specs=out_specs, check_vma=False)
```

time: 675 us -> 407 us (0.60); the launches traced: 667 us -> 407 us
  local copies, waits for them, and re-layouts: 247 us -> 2.2 us
  Pallas kernels: 193 us -> 403 us
  blocking collectives: 121 us -> 0 us
  other arithmetic: 51.6 us -> 0.6 us
  waiting for transfers between devices: 23.7 us -> 0 us
  between operations: 15 us -> 1.3 us
  starting transfers between devices: 11.4 us -> 0 us
    pallas_call x1 -> x3, Pallas kernels: 193 us -> 403 us  [the longest x1 220 us: run_block(): pl.pallas_call(lambda *refs: block_kernel(strips, buckets, samples, plan_...]
    unnamed x1 -> x0, blocking collectives: 121 us -> none
    gather x2 -> x0, local copies, waits for them, and re-layouts: 72.8 us -> none  [the longest x1 42.2 us: shards(): packed_grad[jnp.maximum(sources, 0)]]
    scatter x1 -> x0, local copies, waits for them, and re-layouts: 65.2 us -> none  [slot_owner_rows(): return jnp.full((slot_total,), -1, jnp.int32).at[slots].set(jnp.arange(sl...]
    concatenate x1 -> x0, local copies, waits for them, and re-layouts: 60.7 us -> none  [pack(): return jnp.concatenate(parts).reshape(-1, 128)]
    all_gather x1 -> x0, waiting for transfers between devices: 22.9 us -> none  [shards(): gathered = lax.all_gather(master, ('strip', 'bucket'), axis=0, tiled=True)]
    another operation x6 -> x0, other arithmetic: 22.7 us -> none
    select_n x4 -> x0, other arithmetic: 13.6 us -> none  [the longest x1 12.8 us: shards(): jnp.where((sources >= 0)[:, None], packed_grad[jnp.maximum(sources, 0)],...]
  transfers between devices with their start and end apart: 6 -> 0, of which waited for: 2 -> 0; matrix products, arithmetic and copies ran while one was open for 62% -> 0% of each run, Pallas kernels for 0% -> 0%
where the time goes in v5:
time: 407 us
  Pallas kernels  403 us (99%)
    pallas_call x1, Pallas kernels, run_block(): pl.pallas_call(lambda *refs: block_kernel(strips, buckets, samples, plan_...  220 us
    pallas_call x1, Pallas kernels, run_collect(): pl.pallas_call(collect_kernel, in_specs=[SMEM_SPEC] + [vmem] * 8 + [HBM_S...  172 us
    pallas_call x1, Pallas kernels, run_dispatch(): pl.pallas_call(dispatch_kernel, in_specs=[pl.BlockSpec(memory_space=pltpu...  11 us

profile of v5, /device:TPU:0, one launch (start us, length us, event | category | flops | bytes accessed | tf_op | source)
XLA Modules:
  0.0 407.2 jit_solution(11849453078876312093)
XLA Ops:
  1.3 0.8 copy.13
  2.0 0.6 convert_multiply_fusion.refs_1_
  2.6 1.4 pad_bitcast_fusion.owner_ref
  4.1 11.0 %dispatch.1 = (bf16[4096,128]{1,0:T(8,128)(2,1)}, bf16[10752,128]{1,0:T(8,128)(2,1)}, f32[112,128]{1,0:T(8,128)}, s32[112,128]{1,0:T(8,128)}) custom-call(s32[1]{0:T(128)} %bitcast.me_ref, s32[112,128]{1,0:T(8,128)} %pad_bitcast_fusion.owner_ref, f32[651,128]{1,0:T(8,128)} %master_ref.3), custom_call_target="tpu_custom_call" | custom-call | tf_op jit(solution)/shard_map/dispatch/pallas_call | solution.py:824
  15.1 219.9 %block.1 = (f32[8,4,56,384]{3,2,1,0:T(8,128)}, f32[8,4,56,384]{3,2,1,0:T(8,128)}, bf16[8,3,56,384]{3,2,1,0:T(8,128)(2,1)}, bf16[8,3,56,384]{3,2,1,0:T(8,128)(2,1...) custom-call(s32[1]{0:T(128)S(6)} %copy.14.refs_0_, f32[8,2]{1,0:T(8,128)} %convert_multiply_fusion.refs_1_, ...), custom_call_target="tpu_custom_call" | custom-call | tf_op jit(solution)/shard_map/block/pallas_call | solution.py:763
  235.1 172.1 %collect.1 = (f32[651,128]{1,0:T(8,128)}, f32[651,128]{1,0:T(8,128)}, f32[651,128]{1,0:T(8,128)}, f32[8,7,56,384]{3,2,1,0:T(8,128)}, f32[8,7,56,384]{3,2,1,0:T(8,128)}) custom-call(s32[112,128]{1,0:T(8,128)} %get-tuple-element.20.start_ref, f32[112,128]{1,0:T(8,128)} %get-tuple-element.21.rank_ref, bf16[4096,128]{1,0:T(8,128)(2,1)} %get-tuple-element.24.one_ref, ...), custom_call_target="tpu_custom_call" | custom-call | tf_op jit(solution)/shard_map/collect/pallas_call | solution.py:903

commit v6 on v5

--- a/solution.py
+++ b/solution.py
@@ -847,15 +847,18 @@
     first_out, second_out, master_out, out_final, gx_final, packed, total, wide, sems,
 ):
     own = out_any.shape[1]
-    moves = [
-        pltpu.make_async_copy(main, final.at[:, pl.ds(SHIFT, own)], sems.at[i])
-        for i, (main, final) in enumerate(((out_any, out_final), (gx_any, gx_final)))
+    loads = [
+        pltpu.make_async_copy(main, wide.at[i, :, pl.ds(SHIFT, own)], sems.at[i])
+        for i, main in enumerate((out_any, gx_any))
     ]
-    for i, (halo, final) in enumerate(((outh_ref, out_final), (gxh_ref, gx_final))):
-        wide[i] = halo[...].astype(F32)
-        moves.append(pltpu.make_async_copy(wide.at[i], final.at[:, pl.ds(0, SHIFT)], sems.at[2 + i]))
-    for move in moves:
-        move.start()
+    stores = [pltpu.make_async_copy(wide.at[i], final, sems.at[2 + i]) for i, final in enumerate((out_final, gx_final))]
+    for load in loads:
+        load.start()
+    for i, halo in enumerate((outh_ref, gxh_ref)):
+        wide[i, :, 0:SHIFT] = halo[...].astype(F32)
+    for load, store in zip(loads, stores):
+        load.wait()
+        store.start()
     capacity = master_ref.shape[0]
     total[...] = jnp.zeros_like(total)
     for first, slabs, rows in slab_plan():
@@ -892,8 +895,8 @@
     first_hat = first / (1.0 - BETA_ONE**STEP)
     second_hat = second / (1.0 - BETA_TWO**STEP)
     master_out[...] = weights - rate * (first_hat / (jnp.sqrt(second_hat) + ADAM_EPS) + decay * weights)
-    for move in moves:
-        move.wait()
+    for store in stores:
+        store.wait()
 
 
 def run_collect(starts, ranks, one, two, master, first, second, outh, gxh, out, gx):
@@ -908,7 +911,7 @@
         scratch_shapes=[
             pltpu.VMEM((SMALL_START + 128, 128), F32),
             pltpu.VMEM((-(-(master.shape[0] + 128) // 8) * 8, 128), F32),
-            pltpu.VMEM((2,) + outh.shape, F32),
+            pltpu.VMEM((2,) + final.shape, F32),
             pltpu.SemaphoreType.DMA((4,)),
         ],
         compiler_params=pltpu.CompilerParams(vmem_limit_bytes=62 * 1024 * 1024),

time: 407 us -> 248 us (0.61)
  Pallas kernels: 403 us -> 244 us
    pallas_call x1, Pallas kernels: 172 us -> 13.3 us  [run_collect(): pl.pallas_call(collect_kernel, in_specs=[SMEM_SPEC] + [vmem] * 8 + [HBM_S...]
where the time goes in v6:
time: 248 us
  Pallas kernels  244 us (98%)
    pallas_call x1, Pallas kernels, run_block(): pl.pallas_call(lambda *refs: block_kernel(strips, buckets, samples, plan_...  220 us
    pallas_call x1, Pallas kernels, run_collect(): pl.pallas_call(collect_kernel, in_specs=[SMEM_SPEC] + [vmem] * 8 + [HBM_S...  13.3 us
    pallas_call x1, Pallas kernels, run_dispatch(): pl.pallas_call(dispatch_kernel, in_specs=[pl.BlockSpec(memory_space=pltpu...  11 us

profile of v6, /device:TPU:0, one launch (start us, length us, event | category | flops | bytes accessed | tf_op | source)
XLA Modules:
  0.0 248.1 jit_solution(14440321492883720265)
XLA Ops:
  1.3 0.8 copy.13
  2.0 0.6 convert_multiply_fusion.refs_1_
  2.6 1.4 pad_bitcast_fusion.owner_ref
  4.1 11.0 %dispatch.1 = (bf16[4096,128]{1,0:T(8,128)(2,1)}, bf16[10752,128]{1,0:T(8,128)(2,1)}, f32[112,128]{1,0:T(8,128)}, s32[112,128]{1,0:T(8,128)}) custom-call(s32[1]{0:T(128)} %bitcast.me_ref, s32[112,128]{1,0:T(8,128)} %pad_bitcast_fusion.owner_ref, f32[651,128]{1,0:T(8,128)} %master_ref.3), custom_call_target="tpu_custom_call" | custom-call | tf_op jit(solution)/shard_map/dispatch/pallas_call | solution.py:824
  15.1 219.7 %block.1 = (f32[8,4,56,384]{3,2,1,0:T(8,128)}, f32[8,4,56,384]{3,2,1,0:T(8,128)}, bf16[8,3,56,384]{3,2,1,0:T(8,128)(2,1)}, bf16[8,3,56,384]{3,2,1,0:T(8,128)(2,1...) custom-call(s32[1]{0:T(128)S(6)} %copy.14.refs_0_, f32[8,2]{1,0:T(8,128)} %convert_multiply_fusion.refs_1_, ...), custom_call_target="tpu_custom_call" | custom-call | tf_op jit(solution)/shard_map/block/pallas_call | solution.py:763
  234.8 13.3 %collect.1 = (f32[651,128]{1,0:T(8,128)}, f32[651,128]{1,0:T(8,128)}, f32[651,128]{1,0:T(8,128)}, f32[8,7,56,384]{3,2,1,0:T(8,128)}, f32[8,7,56,384]{3,2,1,0:T(8,128)}) custom-call(s32[112,128]{1,0:T(8,128)} %get-tuple-element.20.start_ref, f32[112,128]{1,0:T(8,128)} %get-tuple-element.21.rank_ref, bf16[4096,128]{1,0:T(8,128)(2,1)} %get-tuple-element.24.one_ref, ...), custom_call_target="tpu_custom_call" | custom-call | tf_op jit(solution)/shard_map/collect/pallas_call | solution.py:906

commit v7 on v6

--- a/solution.py
+++ b/solution.py
@@ -419,16 +419,59 @@
     return jnp.concatenate([flat[:, r * 128 : r * 128 + 128] for r in range(TABLE_ROWS)], axis=0)
 
 
+def rank_rows(me, owner_ref, rank_ref, start_ref):
+    blocks = owner_ref.shape[0]
+    mine = (owner_ref[...] == me).astype(F32)
+    low = mine.astype(BF16)
+    row = lax.broadcasted_iota(jnp.int32, (128, 128), 0)
+    col = lax.broadcasted_iota(jnp.int32, (128, 128), 1)
+    within = nn(low, (row <= col).astype(F32).astype(BF16))
+    sums = nn(low, jnp.ones((128, 128), BF16))
+    below = lax.broadcasted_iota(jnp.int32, (blocks, blocks), 1) < lax.broadcasted_iota(jnp.int32, (blocks, blocks), 0)
+    start = nn(below.astype(F32).astype(BF16), sums.astype(BF16))
+    rank_ref[...] = jnp.where(mine > 0, within - 1.0, -1.0)
+    start_ref[...] = start.astype(jnp.int32)
+
+
+def spread_rows(first, slabs, rows, target, offset, rank_ref, start_s, padded, packed):
+    slot = lax.broadcasted_iota(jnp.int32, (128, 128), 0).astype(F32)
+
+    def block(b, _):
+        at = first // 128 + b
+        hot = (slot == rank_ref[pl.ds(at, 1), :]).astype(F32).astype(BF16)
+        begin = jnp.clip(start_s[at, 0], 0, padded.shape[0] - 128)
+        held = padded[pl.ds(begin, 128), :].astype(BF16)
+        packed[pl.ds(pl.multiple_of(b * 128, 128), 128), :] = tn(hot, held)
+        return 0
+
+    count = slabs * rows // 128
+    lax.fori_loop(0, count, block, 0, unroll=3 if count % 3 == 0 else 1)
+    for j in range(slabs):
+        target[offset + j * rows : offset + (j + 1) * rows, :] = packed[pl.ds(j, rows, stride=slabs), :].astype(BF16)
+
+
+def spread_small(target, rank_ref, start_s, padded):
+    slot = lax.broadcasted_iota(jnp.int32, (128, 128), 0).astype(F32)
+    small = SMALL_START // 128
+    hot = (slot == rank_ref[small : small + 1, :]).astype(F32).astype(BF16)
+    begin = jnp.clip(start_s[small, 0], 0, padded.shape[0] - 128)
+    for i, piece in enumerate(split_three(padded[pl.ds(begin, 128), :])):
+        first = FIRST_ROWS + i * SMALL_SPAN
+        target[first : first + SMALL_SPAN, :] = tn(hot, piece)[0:SMALL_SPAN].astype(BF16)
+    used = FIRST_ROWS + 3 * SMALL_SPAN
+    target[used:, :] = jnp.zeros((target.shape[0] - used, 128), BF16)
+
+
 def block_kernel(
     strips, buckets, images, plan_one, plan_two,
-    cols_ref, keep_ref, x_ref, dy_ref, x_any, dy_any, one_any, two_any,
-    out_ref, gx_ref, outh_any, gxh_any, gone_any, gtwo_any,
+    cols_ref, keep_ref, x_ref, dy_ref, x_any, dy_any, owner_ref, master_ref,
+    out_ref, gx_ref, rank_ref, start_ref, outh_any, gxh_any, gone_any, gtwo_any,
     wq_ref, wp_ref, wu_ref, wd_ref, bq_ref, bp_ref, bu_ref, bd_ref, g1_ref, b1_ref, g2_ref, b2_ref,
     gwq_ref, gwp_ref, gwu_ref, gwdt_ref, gbq_ref, gbp_ref, gbu_ref, gbd_ref, gg1_ref, gb1_ref, gg2_ref, gb2_ref,
     bias, gs_ref, offsets, spread,
     xw, zs, qkv, prob, ctx, gctx, gx1s,
     line, dyw, x1s, n2s, h2s, gfs, ys, gh2s, resw, htr, gtr, gscores, gqkv,
-    fetched, halo_out, halo_in, back_in, wire_one, wire_two,
+    fetched, halo_out, halo_in, back_in, wire_one, wire_two, padded, packed, start_s,
     local_sems, send_sems, recv_sems, *scratch,
 ):
     step = pl.program_id(0)
@@ -440,7 +483,7 @@
     count_one = len(reduce_scratch(plan_one))
     parts_one = reduce_stages(place, plan_one, wire_one, scratch[:count_one])
     parts_two = reduce_stages(place, plan_two, wire_two, scratch[count_one:])
-    gather_ticks = reduce_ticks(parts_one + parts_two)
+    gather_ticks = reduce_ticks(parts_one + [[]] * (4 - len(parts_one)) + parts_two)
     early = len(parts_one[0])
     one_ticks, two_ticks = reduce_ticks(parts_one), reduce_ticks(parts_two)
 
@@ -460,27 +503,39 @@
 
     @pl.when(step == 0)
     def _():
-        loads = [
-            pltpu.make_async_copy(source, target, local_sems.at[2 + i])
-            for i, (source, target) in enumerate(((one_any, wire_one), (two_any, wire_two)))
-        ]
         first = [fetch(x_any, image, image) for image in range(2)]
-        for copy in loads + first:
+        for copy in first:
             copy.start()
+        me = lax.axis_index("strip") * buckets + lax.axis_index("bucket")
+        rank_rows(me, owner_ref, rank_ref, start_ref)
+        starts = pltpu.make_async_copy(start_ref, start_s, local_sems.at[2])
+        starts.start()
+        capacity = master_ref.shape[0]
+        padded[0:capacity, :] = master_ref[...]
+        padded[capacity:, :] = jnp.zeros((padded.shape[0] - capacity, 128), F32)
+        starts.wait()
+        plans = slab_plan()
+        spread_rows(*plans[0], wire_one, 0, rank_ref, start_s, padded, packed)
+        spread_small(wire_one, rank_ref, start_s, padded)
         place.greet(True)
-        for copy in loads:
-            copy.wait()
         gather_ticks[0]()
         for image in range(2):
             first[image].wait()
             send_rows(0, image, image)
         fetch(x_any, 2, 0).start()
         fetch(dy_any, 0, 1).start()
+        for plan in plans[1:3]:
+            spread_rows(*plan, wire_two, plan[0] - FIRST_ROWS, rank_ref, start_s, padded, packed)
+        gather_ticks[1]()
+        spread_rows(*plans[3], wire_two, plans[3][0] - FIRST_ROWS, rank_ref, start_s, padded, packed)
+        used = SMALL_START - FIRST_ROWS
+        wire_two[used:, :] = jnp.zeros((wire_two.shape[0] - used, 128), BF16)
+        gather_ticks[2]()
         line[...] = jnp.zeros_like(line)
         for ref in (gwq_ref, gwp_ref, gwu_ref, gwdt_ref, gbq_ref, gbp_ref, gbu_ref, gbd_ref,
                     gg1_ref, gb1_ref, gg2_ref, gb2_ref, gs_ref, qkv, gctx):
             ref[...] = jnp.zeros_like(ref)
-        for tick in gather_ticks[1:early]:
+        for tick in gather_ticks[3:early]:
             tick()
         load_matrix(wq_ref, wire_one, 0, C)
         load_vectors((bq_ref, bp_ref, bu_ref, bd_ref, g1_ref, b1_ref, g2_ref, b2_ref), wire_one,
@@ -534,8 +589,8 @@
 
     def feed(image):
         at = lax.rem(image, LAG)
-        keep_one = keep_ref[image, 0]
-        keep_two = keep_ref[image, 1]
+        keep_one = keep_ref[image, 0].astype(F32) * (1.0 / KEEP_PROB)
+        keep_two = keep_ref[image, 1].astype(F32) * (1.0 / KEEP_PROB)
         x1 = xw[at] + keep_one * (nn(ctx[at], wp_ref[...]) + bp_ref[...])
         x1s[...] = x1
         normal, scale_two = row_norm(x1)
@@ -710,14 +765,18 @@
 HBM_SPEC = pl.BlockSpec(memory_space=pl.ANY)
 
 
-def run_block(cols, keep, x, dy, one, two, strips, buckets):
+def whole(shape):
+    return pl.BlockSpec(shape, lambda i: (0,) * len(shape))
+
+
+def run_block(cols, keep, x, dy, owners, master, one_rows, two_rows, strips, buckets):
     samples, rows, columns, _ = x.shape
     wide = columns // WIN
     tokens = wide * CELLS
     own = rows - SHIFT
     halo = (samples, SHIFT, columns, C)
-    plan_one = reduce_plan(strips, buckets, one.shape[0], ORDERS[:2])
-    plan_two = reduce_plan(strips, buckets, two.shape[0], ORDERS)
+    plan_one = reduce_plan(strips, buckets, one_rows, ORDERS[:2])
+    plan_two = reduce_plan(strips, buckets, two_rows, ORDERS)
     top = samples - 1
 
     def attended(i):
@@ -755,7 +814,9 @@
         pltpu.VMEM((wide,) + sums, F32), pltpu.VMEM((tokens, 3 * C), F32),
         pltpu.VMEM((2,) + halo[1:], F32),
         pltpu.VMEM((2,) + halo, BF16), pltpu.VMEM((2,) + halo, BF16), pltpu.VMEM((2,) + halo, BF16),
-        pltpu.VMEM(one.shape, BF16), pltpu.VMEM(two.shape, BF16),
+        pltpu.VMEM((one_rows, 128), BF16), pltpu.VMEM((two_rows, 128), BF16),
+        pltpu.VMEM((-(-(master.shape[0] + 128) // 8) * 8, 128), F32), pltpu.VMEM((C * FF // 128, 128), F32),
+        pltpu.SMEM(owners.shape, jnp.int32),
         pltpu.SemaphoreType.DMA((4,)), pltpu.SemaphoreType.DMA((4, samples)), pltpu.SemaphoreType.DMA((4, samples)),
     ]
     block = (1, rows, columns, C)
@@ -763,112 +824,33 @@
     return pl.pallas_call(
         lambda *refs: block_kernel(strips, buckets, samples, plan_one, plan_two, *refs),
         grid=(samples + 2 * LAG,),
-        in_specs=[SMEM_SPEC, SMEM_SPEC, pl.BlockSpec(block, attended), pl.BlockSpec(block, fed)] + [HBM_SPEC] * 4,
-        out_specs=[pl.BlockSpec(part, fed), pl.BlockSpec(part, pulled)] + [HBM_SPEC] * 4,
-        out_shape=[struct((samples, own, columns, C)), struct((samples, own, columns, C)), struct(halo, BF16),
-                   struct(halo, BF16), struct(one.shape, BF16), struct(two.shape, BF16)],
+        in_specs=[SMEM_SPEC, SMEM_SPEC, pl.BlockSpec(block, attended), pl.BlockSpec(block, fed)] + [HBM_SPEC] * 2
+        + [whole(owners.shape), whole(master.shape)],
+        out_specs=[pl.BlockSpec(part, fed), pl.BlockSpec(part, pulled)] + [whole(owners.shape)] * 2 + [HBM_SPEC] * 4,
+        out_shape=[struct((samples, own, columns, C)), struct((samples, own, columns, C)), struct(owners.shape),
+                   struct(owners.shape, jnp.int32), struct(halo, BF16), struct(halo, BF16), struct((one_rows, 128), BF16),
+                   struct((two_rows, 128), BF16)],
         scratch_shapes=scratch + reduce_scratch(plan_one) + reduce_scratch(plan_two),
         compiler_params=pltpu.CompilerParams(
             vmem_limit_bytes=62 * 1024 * 1024, collective_id=1, has_side_effects=True
         ),
         name="block",
-    )(cols, keep, x, dy, x, dy, one, two)
-
-
-def dispatch_kernel(me_ref, owner_ref, master_ref, one_ref, two_ref, rank_ref, start_ref, padded, packed, start_s, sem):
-    blocks = owner_ref.shape[0]
-    capacity = master_ref.shape[0]
-    mine = (owner_ref[...] == me_ref[0]).astype(F32)
-    low = mine.astype(BF16)
-    row = lax.broadcasted_iota(jnp.int32, (128, 128), 0)
-    col = lax.broadcasted_iota(jnp.int32, (128, 128), 1)
-    within = nn(low, (row <= col).astype(F32).astype(BF16))
-    sums = nn(low, jnp.ones((128, 128), BF16))
-    below = lax.broadcasted_iota(jnp.int32, (blocks, blocks), 1) < lax.broadcasted_iota(jnp.int32, (blocks, blocks), 0)
-    start = nn(below.astype(F32).astype(BF16), sums.astype(BF16))
-    rank_ref[...] = jnp.where(mine > 0, within - 1.0, -1.0)
-    start_ref[...] = start.astype(jnp.int32)
-    copy = pltpu.make_async_copy(start_ref, start_s, sem)
-    copy.start()
-    padded[...] = jnp.zeros_like(padded)
-    padded[0:capacity, :] = master_ref[...]
-    one_ref[FIRST_ROWS:, :] = jnp.zeros((one_ref.shape[0] - FIRST_ROWS, 128), BF16)
-    used = SMALL_START - FIRST_ROWS
-    two_ref[used:, :] = jnp.zeros((two_ref.shape[0] - used, 128), BF16)
-    copy.wait()
-    slot = row.astype(F32)
-
-    def block(b, _):
-        hot = (slot == rank_ref[pl.ds(b, 1), :]).astype(F32).astype(BF16)
-        rows = padded[pl.ds(start_s[b, 0], 128), :].astype(BF16)
-        packed[pl.ds(pl.multiple_of(b * 128, 128), 128), :] = tn(hot, rows)
-        return 0
-
-    small = SMALL_START // 128
-    lax.fori_loop(0, small, block, 0, unroll=4)
-    hot = (slot == rank_ref[small : small + 1, :]).astype(F32).astype(BF16)
-    for i, piece in enumerate(split_three(padded[pl.ds(start_s[small, 0], 128), :])):
-        first = FIRST_ROWS + i * SMALL_SPAN
-        one_ref[first : first + SMALL_SPAN, :] = tn(hot, piece)[0:SMALL_SPAN].astype(BF16)
-    for first, slabs, rows in slab_plan():
-        for j in range(slabs):
-            target, offset = (one_ref, 0) if first < FIRST_ROWS else (two_ref, FIRST_ROWS)
-            target[first - offset + j * rows : first - offset + (j + 1) * rows, :] = packed[
-                pl.ds(first + j, rows, stride=slabs), :
-            ].astype(BF16)
-
-
-def run_dispatch(me, owners, master, one_rows, two_rows):
-    blocks = owners.shape[0]
-    vmem = pl.BlockSpec(memory_space=pltpu.VMEM)
-    return pl.pallas_call(
-        dispatch_kernel,
-        in_specs=[pl.BlockSpec(memory_space=pltpu.SMEM), vmem, vmem],
-        out_specs=[vmem] * 4,
-        out_shape=[
-            jax.ShapeDtypeStruct((one_rows, 128), BF16),
-            jax.ShapeDtypeStruct((two_rows, 128), BF16),
-            jax.ShapeDtypeStruct((blocks, 128), F32),
-            jax.ShapeDtypeStruct((blocks, 128), jnp.int32),
-        ],
-        scratch_shapes=[
-            pltpu.VMEM((-(-(master.shape[0] + 128) // 8) * 8, 128), F32),
-            pltpu.VMEM((SMALL_START, 128), F32),
-            pltpu.SMEM((blocks, 128), jnp.int32),
-            pltpu.SemaphoreType.DMA,
-        ],
-        compiler_params=pltpu.CompilerParams(vmem_limit_bytes=62 * 1024 * 1024),
-        name="dispatch",
-    )(me, owners, master)
+    )(cols, keep, x, dy, x, dy, owners, master)
 
 
 def collect_kernel(
-    start_ref, rank_ref, one_ref, two_ref, master_ref, first_ref, second_ref, outh_ref, gxh_ref, out_any, gx_any,
-    first_out, second_out, master_out, out_final, gx_final, packed, total, wide, sems,
+    start_ref, rank_ref, one_any, two_any, master_ref, first_ref, second_ref, outh_any, gxh_any, out_any, gx_any,
+    first_out, second_out, master_out, out_final, gx_final, packed, total, wide, one, two, halos, sems,
 ):
     own = out_any.shape[1]
-    loads = [
-        pltpu.make_async_copy(main, wide.at[i, :, pl.ds(SHIFT, own)], sems.at[i])
-        for i, main in enumerate((out_any, gx_any))
-    ]
-    stores = [pltpu.make_async_copy(wide.at[i], final, sems.at[2 + i]) for i, final in enumerate((out_final, gx_final))]
+    pairs = [(one_any, one), (two_any, two), (outh_any, halos.at[0]), (gxh_any, halos.at[1])]
+    pairs += [(main, wide.at[i, :, pl.ds(SHIFT, own)]) for i, main in enumerate((out_any, gx_any))]
+    loads = [pltpu.make_async_copy(source, target, sems.at[i]) for i, (source, target) in enumerate(pairs)]
+    stores = [pltpu.make_async_copy(wide.at[i], final, sems.at[6 + i]) for i, final in enumerate((out_final, gx_final))]
     for load in loads:
         load.start()
-    for i, halo in enumerate((outh_ref, gxh_ref)):
-        wide[i, :, 0:SHIFT] = halo[...].astype(F32)
-    for load, store in zip(loads, stores):
-        load.wait()
-        store.start()
     capacity = master_ref.shape[0]
     total[...] = jnp.zeros_like(total)
-    for first, slabs, rows in slab_plan():
-        for j in range(slabs):
-            source, offset = (one_ref, 0) if first < FIRST_ROWS else (two_ref, FIRST_ROWS)
-            packed[pl.ds(first + j, rows, stride=slabs), :] = source[
-                first - offset + j * rows : first - offset + (j + 1) * rows, :
-            ].astype(F32)
-    packed[SMALL_START : SMALL_START + SMALL_SPAN, :] = one_ref[FIRST_ROWS : FIRST_ROWS + SMALL_SPAN, :].astype(F32)
-    packed[SMALL_START + SMALL_SPAN : SMALL_START + 128, :] = jnp.zeros((128 - SMALL_SPAN, 128), F32)
     slot = lax.broadcasted_iota(jnp.int32, (128, 128), 0).astype(F32)
 
     def block(b, _):
@@ -878,7 +860,30 @@
         total[where, :] = total[where, :] + part
         return 0
 
-    lax.fori_loop(0, SMALL_START // 128 + 1, block, 0, unroll=4)
+    def unpack(plan, source, offset):
+        first, slabs, rows = plan
+        for j in range(slabs):
+            packed[pl.ds(first + j, rows, stride=slabs), :] = source[
+                first - offset + j * rows : first - offset + (j + 1) * rows, :
+            ].astype(F32)
+
+    plans = slab_plan()
+    small = SMALL_START // 128
+    loads[0].wait()
+    unpack(plans[0], one, 0)
+    packed[SMALL_START : SMALL_START + SMALL_SPAN, :] = one[FIRST_ROWS : FIRST_ROWS + SMALL_SPAN, :].astype(F32)
+    packed[SMALL_START + SMALL_SPAN : SMALL_START + 128, :] = jnp.zeros((128 - SMALL_SPAN, 128), F32)
+    lax.fori_loop(0, FIRST_ROWS // 128, block, 0, unroll=9)
+    for i in range(2):
+        loads[2 + i].wait()
+        wide[i, :, 0:SHIFT] = halos[i].astype(F32)
+        loads[4 + i].wait()
+        stores[i].start()
+    loads[1].wait()
+    for plan in plans[1:]:
+        unpack(plan, two, FIRST_ROWS)
+    lax.fori_loop(FIRST_ROWS // 128, small, block, 0, unroll=9)
+    block(small, 0)
     slots = lax.broadcasted_iota(jnp.int32, (capacity, 1), 0)
     edges = [edge // 128 for edge in row_edges()[:4]] + [SMALL_START // 128 + 1]
     rates = [2.0 / math.sqrt(C), 2.0 / math.sqrt(C // 8), 2.0 / math.sqrt(C), 2.0 / math.sqrt(FF), 1.0, 0.0]
@@ -905,14 +910,17 @@
     final = jax.ShapeDtypeStruct((samples, own + SHIFT, columns, channels), F32)
     return pl.pallas_call(
         collect_kernel,
-        in_specs=[SMEM_SPEC] + [vmem] * 8 + [HBM_SPEC] * 2,
+        in_specs=[SMEM_SPEC, vmem, HBM_SPEC, HBM_SPEC] + [vmem] * 3 + [HBM_SPEC] * 4,
         out_specs=[vmem] * 3 + [HBM_SPEC] * 2,
         out_shape=[jax.ShapeDtypeStruct(master.shape, F32)] * 3 + [final, final],
         scratch_shapes=[
             pltpu.VMEM((SMALL_START + 128, 128), F32),
             pltpu.VMEM((-(-(master.shape[0] + 128) // 8) * 8, 128), F32),
             pltpu.VMEM((2,) + final.shape, F32),
-            pltpu.SemaphoreType.DMA((4,)),
+            pltpu.VMEM(one.shape, BF16),
+            pltpu.VMEM(two.shape, BF16),
+            pltpu.VMEM((2,) + outh.shape, BF16),
+            pltpu.SemaphoreType.DMA((8,)),
         ],
         compiler_params=pltpu.CompilerParams(vmem_limit_bytes=62 * 1024 * 1024),
         name="collect",
@@ -924,15 +932,12 @@
 ):
     strips = lax.axis_size("strip")
     buckets = lax.axis_size("bucket")
-    my_index = lax.axis_index(("strip", "bucket")).astype(jnp.int32).reshape(1)
     blocks = -(-(SMALL_START // 128 + 2) // 8) * 8
     owners = jnp.pad(owner_list, (0, blocks * 128 - owner_list.shape[0]), constant_values=-1).reshape(blocks, 128)
     one_rows = wire_rows(FIRST_ROWS + 3 * SMALL_SPAN, strips, buckets)
     two_rows = wire_rows(SMALL_START - FIRST_ROWS, strips, buckets)
-    one, two, ranks, starts = run_dispatch(my_index, owners, master, one_rows, two_rows)
-    keep = keep_mask.astype(F32) / KEEP_PROB
-    output, grad_input, output_halo, grad_halo, gone, gtwo = run_block(
-        window_cols, keep, block_input, cotangent, one, two, strips, buckets
+    output, grad_input, ranks, starts, output_halo, grad_halo, gone, gtwo = run_block(
+        window_cols, keep_mask, block_input, cotangent, owners, master, one_rows, two_rows, strips, buckets
     )
     first, second_new, new_weights, output, grad_input = run_collect(
         starts, ranks, gone, gtwo, master, first_moment, second_moment, output_halo, grad_halo, output, grad_input

time: 248 us -> 241 us (0.972)
  Pallas kernels: 244 us -> 236 us
    pallas_call x2 -> x1, Pallas kernels: 24.3 us -> 10.8 us  [run_collect(): pl.pallas_call(collect_kernel, in_specs=[SMEM_SPEC, vmem, HBM_SPEC, HBM_S...]
    pallas_call x1, Pallas kernels: 220 us -> 225 us  [run_block(): pl.pallas_call(lambda *refs: block_kernel(strips, buckets, samples, plan_...]
where the time goes in v7:
time: 241 us; the launch traced here: 240 us
  Pallas kernels  236 us (98%)
  local copies, waits for them, and re-layouts  2.79 us (1%)
    pallas_call x1, Pallas kernels, run_block(): pl.pallas_call(lambda *refs: block_kernel(strips, buckets, samples, plan_...  225 us
    pallas_call x1, Pallas kernels, run_collect(): pl.pallas_call(collect_kernel, in_specs=[SMEM_SPEC, vmem, HBM_SPEC, HBM_S...  10.8 us

profile of v7, /device:TPU:0, one launch (start us, length us, event | category | flops | bytes accessed | tf_op | source)
XLA Modules:
  0.0 240.3 jit_solution(10966313690954269610)
XLA Ops:
  1.3 1.3 copy.13.refs_1_
  2.6 1.4 pad_bitcast_fusion.refs_6_
  4.1 225.3 %block.1 = (f32[8,4,56,384]{3,2,1,0:T(8,128)}, f32[8,4,56,384]{3,2,1,0:T(8,128)}, f32[112,128]{1,0:T(8,128)}, s32[112,128]{1,0:T(8,128)}, bf16[8,3,56,384]{3,2,1...) custom-call(s32[1]{0:T(128)S(6)} %copy.14.refs_0_, ...), custom_call_target="tpu_custom_call" | custom-call | tf_op jit(solution)/shard_map/block/pallas_call | solution.py:824
  229.4 10.8 %collect.1 = (f32[651,128]{1,0:T(8,128)}, f32[651,128]{1,0:T(8,128)}, f32[651,128]{1,0:T(8,128)}, f32[8,7,56,384]{3,2,1,0:T(8,128)}, f32[8,7,56,384]{3,2,1,0:T(8,128)}) custom-call(s32[112,128]{1,0:T(8,128)} %get-tuple-element.18.start_ref, f32[112,128]{1,0:T(8,128)} %get-tuple-element.19.rank_ref, bf16[4096,128]{1,0:T(8,128)(2,1)} %get-tuple-element.20.one_any, ...), custom_call_target="tpu_custom_call" | custom-call | tf_op jit(solution)/shard_map/collect/pallas_call | solution.py:911

commit v8 on v7

--- a/solution.py
+++ b/solution.py
@@ -94,7 +94,7 @@
     ]
 
 
-ORDERS = (("x", "y", "z"), ("y", "x", "z")) * 2
+ORDERS = (("x", "y", "z"), ("y", "x", "z"), ("x", "y", "z"), ("z", "x", "y"))
 LAG = 2
 FIRST_ROWS = 3 * C * C // 128
 
@@ -641,7 +641,7 @@
         for w in range(wide):
             gctx[at, w, 0:CELLS, :] = gc[w * CELLS : w * CELLS + CELLS].astype(BF16)
 
-    def pull(image, middle):
+    def pull(image):
         at = lax.rem(image, LAG)
         scale = HD ** (-0.5)
         for w in range(wide):
@@ -655,7 +655,6 @@
                 inner = jnp.sum(grad * a, axis=0, keepdims=True)
                 gscores[w, g] = a * (grad - inner)
                 gqkv[rows, 2 * C + g * 128 : 2 * C + g * 128 + 128] = nn(low, gstack)
-        middle()
         for w in range(wide):
             rows = slice(w * CELLS, w * CELLS + CELLS)
             for g in range(GROUPS):
@@ -711,7 +710,7 @@
 
     @pl.when((step >= LAG) & (step < images))
     def _():
-        pull(step - LAG, lambda: None)
+        pull(step - LAG)
 
     @pl.when(step < images)
     def _():
@@ -735,13 +734,13 @@
 
         @pl.when(step == images + LAG + k)
         def _(k=k):
-            two_ticks[2 * k + 1]()
-            pull(images - LAG + k, two_ticks[2 * k + 2])
+            two_ticks[k + 1]()
+            pull(images - LAG + k)
 
     @pl.when(step == images + 2 * LAG - 1)
     def _():
         pack_one()
-        rest = two_ticks[2 * LAG + 1 :]
+        rest = two_ticks[LAG + 1 :]
         for i in range(max(len(rest), len(one_ticks))):
             for ticks in (one_ticks, rest):
                 if i < len(ticks):

time: 241 us -> 232 us (0.963)
  Pallas kernels: 236 us -> 227 us
    pallas_call x1, Pallas kernels: 225 us -> 217 us  [run_block(): pl.pallas_call(lambda *refs: block_kernel(strips, buckets, samples, plan_...]
where the time goes in v8:
time: 232 us
  Pallas kernels  227 us (98%)
  local copies, waits for them, and re-layouts  2.79 us (1%)
    pallas_call x1, Pallas kernels, run_block(): pl.pallas_call(lambda *refs: block_kernel(strips, buckets, samples, plan_...  217 us
    pallas_call x1, Pallas kernels, run_collect(): pl.pallas_call(collect_kernel, in_specs=[SMEM_SPEC, vmem, HBM_SPEC, HBM_S...  10.8 us

profile of v8, /device:TPU:0, one launch (start us, length us, event | category | flops | bytes accessed | tf_op | source)
XLA Modules:
  0.0 231.6 jit_solution(9756239033897359017)
XLA Ops:
  1.3 1.3 copy.13.refs_1_
  2.6 1.4 pad_bitcast_fusion.refs_6_
  4.1 216.5 %block.1 = (f32[8,4,56,384]{3,2,1,0:T(8,128)}, f32[8,4,56,384]{3,2,1,0:T(8,128)}, f32[112,128]{1,0:T(8,128)}, s32[112,128]{1,0:T(8,128)}, bf16[8,3,56,384]{3,2,1...) custom-call(s32[1]{0:T(128)S(6)} %copy.14.refs_0_, ...), custom_call_target="tpu_custom_call" | custom-call | tf_op jit(solution)/shard_map/block/pallas_call | solution.py:823
  220.6 10.8 %collect.1 = (f32[651,128]{1,0:T(8,128)}, f32[651,128]{1,0:T(8,128)}, f32[651,128]{1,0:T(8,128)}, f32[8,7,56,384]{3,2,1,0:T(8,128)}, f32[8,7,56,384]{3,2,1,0:T(8,128)}) custom-call(s32[112,128]{1,0:T(8,128)} %get-tuple-element.18.start_ref, f32[112,128]{1,0:T(8,128)} %get-tuple-element.19.rank_ref, bf16[4096,128]{1,0:T(8,128)(2,1)} %get-tuple-element.20.one_any, ...), custom_call_target="tpu_custom_call" | custom-call | tf_op jit(solution)/shard_map/collect/pallas_call | solution.py:910

commit v9 on v8

--- a/solution.py
+++ b/solution.py
@@ -589,8 +589,9 @@
 
     def feed(image):
         at = lax.rem(image, LAG)
-        keep_one = keep_ref[image, 0].astype(F32) * (1.0 / KEEP_PROB)
-        keep_two = keep_ref[image, 1].astype(F32) * (1.0 / KEEP_PROB)
+        keep = keep_ref[pl.ds(image, 1), :].astype(F32) * (1.0 / KEEP_PROB)
+        keep_one = keep[:, 0:1]
+        keep_two = keep[:, 1:2]
         x1 = xw[at] + keep_one * (nn(ctx[at], wp_ref[...]) + bp_ref[...])
         x1s[...] = x1
         normal, scale_two = row_norm(x1)
@@ -823,7 +824,7 @@
     return pl.pallas_call(
         lambda *refs: block_kernel(strips, buckets, samples, plan_one, plan_two, *refs),
         grid=(samples + 2 * LAG,),
-        in_specs=[SMEM_SPEC, SMEM_SPEC, pl.BlockSpec(block, attended), pl.BlockSpec(block, fed)] + [HBM_SPEC] * 2
+        in_specs=[SMEM_SPEC, whole(keep.shape), pl.BlockSpec(block, attended), pl.BlockSpec(block, fed)] + [HBM_SPEC] * 2
         + [whole(owners.shape), whole(master.shape)],
         out_specs=[pl.BlockSpec(part, fed), pl.BlockSpec(part, pulled)] + [whole(owners.shape)] * 2 + [HBM_SPEC] * 4,
         out_shape=[struct((samples, own, columns, C)), struct((samples, own, columns, C)), struct(owners.shape),

time: 232 us -> 231 us (level)
  no operation moved by 1% of the time
where the time goes in v9:
time: 231 us
  Pallas kernels  227 us (98%)
  local copies, waits for them, and re-layouts  2.79 us (1%)
    pallas_call x1, Pallas kernels, run_block(): pl.pallas_call(lambda *refs: block_kernel(strips, buckets, samples, plan_...  216 us
    pallas_call x1, Pallas kernels, run_collect(): pl.pallas_call(collect_kernel, in_specs=[SMEM_SPEC, vmem, HBM_SPEC, HBM_S...  10.8 us

profile of v9, /device:TPU:0, one launch (start us, length us, event | category | flops | bytes accessed | tf_op | source)
XLA Modules:
  0.0 231.4 jit_solution(7179076963416263557)
XLA Ops:
  1.3 1.3 copy.13.refs_1_
  2.6 1.4 pad_bitcast_fusion.refs_6_
  4.1 216.4 %block.1 = (f32[8,4,56,384]{3,2,1,0:T(8,128)}, f32[8,4,56,384]{3,2,1,0:T(8,128)}, f32[112,128]{1,0:T(8,128)}, s32[112,128]{1,0:T(8,128)}, bf16[8,3,56,384]{3,2,1...) custom-call(s32[1]{0:T(128)S(6)} %copy.14.refs_0_, ...), custom_call_target="tpu_custom_call" | custom-call | tf_op jit(solution)/shard_map/block/pallas_call | solution.py:824
  220.5 10.8 %collect.1 = (f32[651,128]{1,0:T(8,128)}, f32[651,128]{1,0:T(8,128)}, f32[651,128]{1,0:T(8,128)}, f32[8,7,56,384]{3,2,1,0:T(8,128)}, f32[8,7,56,384]{3,2,1,0:T(8,128)}) custom-call(s32[112,128]{1,0:T(8,128)} %get-tuple-element.18.start_ref, f32[112,128]{1,0:T(8,128)} %get-tuple-element.19.rank_ref, bf16[4096,128]{1,0:T(8,128)(2,1)} %get-tuple-element.20.one_any, ...), custom_call_target="tpu_custom_call" | custom-call | tf_op jit(solution)/shard_map/collect/pallas_call | solution.py:911
